TPU v7x, 128 devices: a whole 4x4x4 slice. The times are simulated.
128 devices in a mesh: ctx: 32 (over x_hi, y, z), rep: 4 (over x_lo, core).
Axes of the slice: x: 4 (x_hi: 2, x_lo: 2; x = x_hi * 2 + x_lo), y: 4, z: 4, core: 2. Of those that a mesh axis runs over, the one named last changes fastest.
Arguments:
- stream: bfloat16 [4, 16384, 1536], P('rep', 'ctx'), may hold values from -6 to 6
- norm_gain_vector: float32 [1536], replicated, may hold values from 0.1 to 1.9
- conv_kernel: bfloat16 [3, 1536, 768], replicated, may hold values from -0.09375 to 0.09375
- point_kernel: bfloat16 [768, 1536], replicated, may hold values from -0.21875 to 0.21875
- out_grad: bfloat16 [4, 16384, 1536], P('rep', 'ctx'), may hold values from -6 to 6
Outputs:
- stream_out: bfloat16 [4, 16384, 1536], P('rep', 'ctx')
- stream_grad: bfloat16 [4, 16384, 1536], P('rep', 'ctx')
- kernel_grad: float32 [3, 1536, 768], P(None, 'ctx')
- point_grad: float32 [768, 1536], P(None, 'ctx')
- gain_grad: float32 [1536], P('ctx')
All inputs are finite; a program needn't handle non-finite values.
Results may differ from a plain program's by a relative error of at most 0.0054.
Values may be sent and summed in bfloat16 or wider, within the bound.
No kernel may reach another device: no remote copies, remote signals or barrier semaphores. Data moves between devices by JAX's collectives and lax.ppermute only.
A program may use at most 128 MiB of HBM per device.

v0:
```python
import jax
import jax.numpy as jnp
from jax import lax
from jax.sharding import PartitionSpec as P


def shifted(array, axis, by):
    peers = lax.axis_size(axis)
    return lax.ppermute(array, axis, [(i, (i + by) % peers) for i in range(peers)])


def gelu_slope(value):
    return jax.jvp(jax.nn.gelu, (value,), (jnp.ones_like(value),))[1]


def contract_rows(left, right):
    return lax.dot_general(
        left, right, (((0,), (0,)), ((), ())), preferred_element_type=jnp.float32
    )


def contract_cols(left, right):
    return lax.dot_general(
        left, right, (((1,), (1,)), ((), ())), preferred_element_type=jnp.float32
    )


def act_pair(value, offsets):
    return [shifted(value, "ctx", offset) for offset in offsets]


def grad_pair(value, offsets):
    return [shifted(value, "ctx", offset) for offset in offsets]


def shards(stream, norm_gain_vector, conv_kernel, point_kernel, out_grad):
    cycle = lax.axis_size("ctx")
    quarter = cycle // 4
    offsets = (cycle - quarter, quarter)
    complete_input = stream[0].astype(jnp.float32)
    cotan = out_grad[0]
    root_mean_square = jnp.sqrt(
        jnp.mean(complete_input * complete_input, axis=-1, keepdims=True) + 1e-06
    )
    unit_norm_input = complete_input / root_mean_square
    normalized_input = unit_norm_input * norm_gain_vector
    activation_value = jax.nn.gelu(normalized_input).astype(jnp.bfloat16)
    forward_neighbor, backward_neighbor = act_pair(activation_value, offsets)
    pre = jnp.dot(activation_value, conv_kernel[1], preferred_element_type=jnp.float32)
    pre = pre + jnp.dot(forward_neighbor, conv_kernel[2], preferred_element_type=jnp.float32)
    pre = pre + jnp.dot(backward_neighbor, conv_kernel[0], preferred_element_type=jnp.float32)
    mid = jax.nn.gelu(pre).astype(jnp.bfloat16)
    stream_out = (
        complete_input + jnp.dot(mid, point_kernel, preferred_element_type=jnp.float32)
    ).astype(jnp.bfloat16)
    point_part = contract_rows(mid, cotan)
    before_norm_gradient = (contract_cols(cotan, point_kernel) * gelu_slope(pre)).astype(
        jnp.bfloat16
    )
    following_gradient, preceding_gradient = grad_pair(before_norm_gradient, offsets)
    kernel_part = jnp.stack(
        [
            contract_rows(backward_neighbor, before_norm_gradient),
            contract_rows(activation_value, before_norm_gradient),
            contract_rows(forward_neighbor, before_norm_gradient),
        ]
    )
    act_grad = contract_cols(before_norm_gradient, conv_kernel[1])
    act_grad = act_grad + contract_cols(preceding_gradient, conv_kernel[2])
    act_grad = act_grad + contract_cols(following_gradient, conv_kernel[0])
    normalized_gradient = act_grad * gelu_slope(normalized_input)
    gain_portion = jnp.sum(normalized_gradient * unit_norm_input, axis=0)
    unit_norm_gradient = normalized_gradient * norm_gain_vector
    backward_shifted = (
        unit_norm_gradient
        - unit_norm_input * jnp.mean(unit_norm_gradient * unit_norm_input, axis=-1, keepdims=True)
    ) / root_mean_square
    stream_grad = (cotan.astype(jnp.float32) + backward_shifted).astype(jnp.bfloat16)
    shares = (
        lax.psum_scatter(kernel_part, "ctx", scatter_dimension=1, tiled=True),
        lax.psum_scatter(point_part, "ctx", scatter_dimension=1, tiled=True),
        lax.psum_scatter(gain_portion, "ctx", scatter_dimension=0, tiled=True),
    )
    kernel_grad, point_grad, gain_grad = lax.psum((shares[0], shares[1], shares[2]), "rep")
    return (stream_out[None], stream_grad[None], kernel_grad, point_grad, gain_grad)


def solution(mesh):
    placed = (P("rep", "ctx", None), P(), P(), P(), P("rep", "ctx", None))
    return jax.shard_map(
        shards,
        mesh=mesh,
        in_specs=placed,
        out_specs=(
            P("rep", "ctx", None),
            P("rep", "ctx", None),
            P(None, "ctx", None),
            P(None, "ctx"),
            P("ctx"),
        ),
        check_vma=False,
    )
```

profile of v0, /device:TPU:1, one launch (start us, length us, event | category | flops | bytes accessed | tf_op | source)
XLA Modules:
  0.0 653.8 jit_solution(2633888571100908463)
XLA Ops:
  7.3 1.9 fusion.4
  9.3 2.2 multiply_convert_fusion
  11.5 6.3 collective-permute-start
  17.8 4.0 fusion.34
  21.8 61.1 %collective-permute-done = bf16[512,1536]{1,0:T(8,128)(2,1)S(1)} collective-permute-done((bf16[512,1536]{1,0:T(8,128)(2,1)S(1)}, bf16[512,1536]{1,0:T(8,128)(2,1)S(1)}, u32[]{:S(2)}, u32[]{:S(2)}) %collective-permute-start) | collective-permute-done | bytes 1572896 | tf_op jit(solution)/shard_map/ppermute | solution.py:9
  82.9 1.1 copy-done.7
  84.0 1.4 fusion.30
  85.6 1.4 add_add_fusion
  87.0 1.1 copy-done.12
  88.1 3.7 fusion.56
  92.1 3.9 fusion.53
  96.0 3.7 convolution_bitcast_fusion.1
  99.7 3.6 convolution_bitcast_fusion
  103.3 3.6 convolution_bitcast_fusion.2
  106.9 11.1 %pad_maximum_fusion = f32[3,1536,768]{2,1,0:T(8,128)} fusion(f32[1,1536,768]{2,1,0:T(8,128)} %convolution_bitcast_fusion, f32[1,1536,768]{2,1,0:T(8,128)} %convolution_bitcast_fusion.1, f32[1,1536,768]{2,1,0:T(8,128)} %convolution_bitcast_fusion.2), kind=kLoop, calls=%fused_computation | loop fusion | flops 7077888 | bytes 28311552 | tf_op jit(solution)/shard_map/stack | solution.py:61
  118.0 0.6 copy-done.11
  118.6 0.6 dynamic-slice
  119.9 3.8 collective-permute-start.2
  123.7 1.7 collective-permute-start.3
  125.3 4.6 fusion.25
  129.9 3.1 fusion.32
  133.0 26.5 %collective-permute-done.2 = bf16[512,768]{1,0:T(8,128)(2,1)S(1)} collective-permute-done((bf16[512,768]{1,0:T(8,128)(2,1)S(1)}, bf16[512,768]{1,0:T(8,128)(2,1)S(1)}, u32[]{:S(2)}, u32[]{:S(2)}) %collective-permute-start.2) | collective-permute-done | bytes 786464 | tf_op jit(solution)/shard_map/ppermute | solution.py:9
  159.5 3.1 convolution_add_fusion.1
  162.8 6.8 %multiply_reduce_fusion = (f32[1536]{0:T(1024)S(1)}, f32[512]{0:T(512)S(1)}, f32[512,1536]{1,0:T(8,128)}) fusion(f32[512]{0:T(512)S(1)} %add_sqrt_fusion, bf16[1,512,1536]{2,1,0:T(8,128)(2,1)S(1)} %copy-done.2, f32[1536]{0:T(1024)S(1)} %copy-done.6, f32[512,1536]{1,0:T(8,128)S(1)} %convolution_add_fusion.1, ...), kind=kOutput, calls=%fused_computation.35 | convolution fusion | flops 1228404736 | bytes 11026432 | tf_op jit(solution)/shard_map/dot_general | solution.py:23
  169.6 81.2 %all-reduce = f32[1536]{0:T(1024)S(1)} all-reduce(f32[1536]{0:T(1024)S(1)} %get-tuple-element.5), channel_id=4, replica_groups=mesh['ctx'=32,'rep'=4] {'ctx'}, use_global_device_ids=true, to_apply=%region_7.0.clone | all-reduce | flops 1536 | bytes 12288
  250.9 22.7 %psum.23 = f32[48]{0:T(128)} all-reduce(f32[48]{0:T(128)S(1)} %dynamic-slice.1), channel_id=1, replica_groups=mesh['ctx'=32,'rep'=4] {'rep'}, use_global_device_ids=true, to_apply=%region_8.0 | all-reduce | flops 48 | bytes 384 | tf_op jit(solution)/shard_map/psum | solution.py:84
  273.6 69.4 %reduce-scatter.5.cloned.1.call-done = f32[768,48]{0,1:T(8,128)} async-done(((f32[768,1536]{0,1:T(8,128)}), f32[768,48]{0,1:T(8,128)}) %reduce-scatter.5.cloned.1.call-update) | async-done | bytes 147472 | tf_op jit(solution)/shard_map/reduce_scatter | solution.py:81
  343.1 261.3 %reduce-scatter.3.cloned.1.call-done = f32[3,48,768]{2,1,0:T(8,128)} async-done(((f32[3,1536,768]{2,1,0:T(8,128)}), f32[3,48,768]{2,1,0:T(8,128)}) %reduce-scatter.3.cloned.1.call-update) | async-done | bytes 442384 | tf_op jit(solution)/shard_map/reduce_scatter | solution.py:80
  604.4 4.9 fusion.66
  609.4 34.5 %all-reduce.4.cloned.1.call-done = (f32[3,48,768]{2,1,0:T(8,128)}, f32[768,48]{0,1:T(8,128)}) async-done(((f32[3,48,768]{2,1,0:T(8,128)}, f32[768,48]{0,1:T(8,128)}), (f32[3,48,768]{2,1,0:T(8,128)}, f32[768,48]{0,1:T(8,128)})) %all-reduce.4.cloned.1.call-update) | async-done | bytes 589840 | tf_op jit(solution)/shard_map/psum | solution.py:84
  643.9 1.8 copy.12
  645.7 1.6 copy.13
  (40 shorter events, 0.9 us)
Async XLA Ops:
  7.2 84.9 %copy-start = (bf16[768,1536]{1,0:T(8,128)(2,1)S(1)}, bf16[768,1536]{1,0:T(8,128)(2,1)}, u32[]{:S(2)}) copy-start(bf16[768,1536]{1,0:T(8,128)(2,1)} %param.8) | copy-start | bytes 7077892
  7.2 335.9 %reduce-scatter.5.cloned.1.call-start = ((), (), s32[]{:S(2)}) async-start(), calls=%async_computation.3 | async-start | bytes 4866048 | tf_op jit(solution)/shard_map/reduce_scatter | solution.py:81
  7.2 2.0 copy-start.1
  7.2 10.6 %copy-start.6 = (f32[1536]{0:T(1024)S(1)}, f32[1536]{0:T(1024)}, u32[]{:S(2)}) copy-start(f32[1536]{0:T(1024)} %param.6) | copy-start | bytes 18436
  9.3 74.8 %slice-start = ((s8[7077888]{0:T(1024)(128)(4,1)}), s8[4194304]{0:T(1024)(128)(4,1)S(1)}, s32[]{:S(2)}) async-start(s8[7077888]{0:T(1024)(128)(4,1)} %bitcast.80), calls=%async_computation.5 | async-start | bytes 8388608
  11.5 10.3 %copy-start.4 = (bf16[512,1536]{1,0:T(8,128)(2,1)}, bf16[512,1536]{1,0:T(8,128)(2,1)S(1)}, u32[]{:S(2)}) copy-start(bf16[512,1536]{1,0:T(8,128)(2,1)S(1)} %multiply_convert_fusion) | copy-start | bytes 4718596
  11.5 72.5 %slice-start.1 = ((s8[7077888]{0:T(1024)(128)(4,1)}), s8[2883584]{0:T(1024)(128)(4,1)S(1)}, s32[]{:S(2)}) async-start(s8[7077888]{0:T(1024)(128)(4,1)} %bitcast.80), calls=%async_computation.6 | async-start | bytes 5767168
  11.5 71.4 %collective-permute-start = (bf16[512,1536]{1,0:T(8,128)(2,1)S(1)}, bf16[512,1536]{1,0:T(8,128)(2,1)S(1)}, u32[]{:S(2)}, u32[]{:S(2)}) collective-permute-start(bf16[512,1536]{1,0:T(8,128)(2,1)S(1)} %multiply_convert_fusion), channel_id=1, source_target_pairs={{0,96},{4,100},{8,104},{12,108},{16,112},{20,116},{24,120},{28,124... | collective-permute-start | bytes 4718600 | tf_op jit(solution)/shard_map/ppermute | solution.py:9
  17.8 67.8 %collective-permute-start.1 = (bf16[512,1536]{1,0:T(8,128)(2,1)S(1)}, bf16[512,1536]{1,0:T(8,128)(2,1)S(1)}, u32[]{:S(2)}, u32[]{:S(2)}) collective-permute-start(bf16[512,1536]{1,0:T(8,128)(2,1)S(1)} %multiply_convert_fusion), channel_id=1, source_target_pairs={{0,32},{4,36},{8,40},{12,44},{16,48},{20,52},{24,56},{28,60},{32,6... | collective-permute-start | bytes 4718600 | tf_op jit(solution)/shard_map/ppermute | solution.py:9
  82.9 1.1 copy-start.7
  85.4 2.7 copy-start.3
  85.6 1.4 copy-start.9
  87.0 1.1 copy-start.12
  91.8 512.6 %reduce-scatter.3.cloned.1.call-start = ((), (), s32[]{:S(2)}) async-start(), calls=%async_computation.2 | async-start | bytes 14598144 | tf_op jit(solution)/shard_map/reduce_scatter | solution.py:80
  92.0 3.9 copy-start.5
  96.0 3.7 copy-start.8
  99.7 3.6 copy-start.10
  118.0 0.7 copy-start.11
  118.0 525.9 %all-reduce.4.cloned.1.call-start = ((), (), s32[]{:S(2)}) async-start(), calls=%async_computation.4 | async-start | bytes 1179648 | tf_op jit(solution)/shard_map/psum | solution.py:84
  119.9 39.6 %collective-permute-start.2 = (bf16[512,768]{1,0:T(8,128)(2,1)S(1)}, bf16[512,768]{1,0:T(8,128)(2,1)S(1)}, u32[]{:S(2)}, u32[]{:S(2)}) collective-permute-start(bf16[512,768]{1,0:T(8,128)(2,1)S(1)} %fusion.53), channel_id=1, source_target_pairs={{0,32},{4,36},{8,40},{12,44},{16,48},{20,52},{24,56},{28,60},{32,6... | collective-permute-start | bytes 2359304 | tf_op jit(solution)/shard_map/ppermute | solution.py:9
  123.7 39.2 %collective-permute-start.3 = (bf16[512,768]{1,0:T(8,128)(2,1)S(1)}, bf16[512,768]{1,0:T(8,128)(2,1)S(1)}, u32[]{:S(2)}, u32[]{:S(2)}) collective-permute-start(bf16[512,768]{1,0:T(8,128)(2,1)S(1)} %fusion.53), channel_id=1, source_target_pairs={{0,96},{4,100},{8,104},{12,108},{16,112},{20,116},{24,120},{28,124... | collective-permute-start | bytes 2359304 | tf_op jit(solution)/shard_map/ppermute | solution.py:9
  133.0 29.9 %copy-start.2 = (bf16[1,512,1536]{2,1,0:T(8,128)(2,1)S(1)}, bf16[1,512,1536]{2,1,0:T(8,128)(2,1)}, u32[]{:S(2)}) copy-start(bf16[1,512,1536]{2,1,0:T(8,128)(2,1)} %param.5) | copy-start | bytes 4718596
Sparse Core Ops, SparseCore 0:
  91.9 251.1 reduce-scatter.4
  348.4 255.9 reduce-scatter.2
  607.2 36.6 all-reduce.3
where the time goes:
time: 654 us
  waiting for transfers between devices  453 us (69%)
  blocking collectives  104 us (16%)
  matrix products  42.7 us (7%)
  other arithmetic  20.2 us (3%)
  between operations  14.6 us (2%)
  starting transfers between devices  12 us (2%)
  local copies, waits for them, and re-layouts  7.03 us (1%)
    reduce_scatter x1, waiting for transfers between devices, shards(): lax.psum_scatter(kernel_part, 'ctx', scatter_dimension=1, tiled=True)  261 us
    ppermute x4, waiting for transfers between devices, shifted(): lax.ppermute(array, axis, [(i, (i + by) % peers) for i in range(peers)])  88 us
    unnamed x1, blocking collectives  81.2 us
    reduce_scatter x1, waiting for transfers between devices, shards(): lax.psum_scatter(point_part, 'ctx', scatter_dimension=1, tiled=True)  69.4 us
    psum x1, waiting for transfers between devices, shards(): lax.psum((shares[0], shares[1], shares[2]), 'rep')  34.5 us
    psum x1, blocking collectives, shards(): lax.psum((shares[0], shares[1], shares[2]), 'rep')  22.7 us
    dot_general x4, matrix products, contract_cols(): lax.dot_general(left, right, (((1,), (1,)), ((), ())), preferred_element_...  16.9 us
    dot_general x4, matrix products, contract_rows(): lax.dot_general(left, right, (((0,), (0,)), ((), ())), preferred_element_...  14.5 us
  transfers between devices with their start and end apart: 7, of which 7 were waited for; matrix products, arithmetic and copies ran while one was open for 8% of the time, Pallas kernels for 0%

commit v1 on v0

v1 whole, which is shorter than its diff:
```python
import jax
import jax.numpy as jnp
from jax import lax
from jax.sharding import Mesh, PartitionSpec as P

F32 = jnp.float32
BF16 = jnp.bfloat16
CHIP = ("xh", "y", "z", "xl")


def gelu_slope(value):
    return jax.jvp(jax.nn.gelu, (value,), (jnp.ones_like(value),))[1]


def dot(left, right):
    return jnp.dot(left, right, preferred_element_type=F32)


def contract_rows(left, right):
    return lax.dot_general(
        left, right, (((0,), (0,)), ((), ())), preferred_element_type=F32
    )


def contract_cols(left, right):
    return lax.dot_general(
        left, right, (((1,), (1,)), ((), ())), preferred_element_type=F32
    )


def shifted(value, by):
    axes = ("xh", "y", "z")
    return lax.ppermute(value, axes, [(i, (i + by) % 32) for i in range(32)])


def core_sum(share, core):
    half = share.shape[1] // 2
    low, high = share[:, :half], share[:, half:]
    away = jnp.where(core == 0, high, low).astype(BF16)
    kept = jnp.where(core == 0, low, high)
    return kept + lax.ppermute(away, "core", [(0, 1), (1, 0)]).astype(F32)


def shards(stream, norm_gain_vector, conv_kernel, point_kernel, out_grad):
    core = lax.axis_index("core")
    rows = stream[0].astype(F32)
    cotan = out_grad[0]
    rms = jnp.sqrt(jnp.mean(rows * rows, axis=-1, keepdims=True) + 1e-06)
    xhat = rows / rms
    normed = xhat * norm_gain_vector
    act = jax.nn.gelu(normed).astype(BF16)
    from_before = shifted(dot(act, conv_kernel[0]).astype(BF16), 8)
    from_after = shifted(dot(act, conv_kernel[2]).astype(BF16), -8)
    pre = dot(act, conv_kernel[1]) + from_before.astype(F32) + from_after.astype(F32)
    mid = jax.nn.gelu(pre).astype(BF16)
    stream_out = (rows + dot(mid, point_kernel)).astype(BF16)
    pre_grad = (contract_cols(cotan, point_kernel) * gelu_slope(pre)).astype(BF16)
    grad_before = shifted(pre_grad, 8)
    grad_after = shifted(pre_grad, -8)
    shares = [
        contract_rows(act, grad_after),
        contract_rows(act, pre_grad),
        contract_rows(act, grad_before),
        contract_rows(cotan, mid),
    ]
    act_grad = contract_cols(pre_grad, conv_kernel[1])
    act_grad = act_grad + contract_cols(grad_before, conv_kernel[2])
    act_grad = act_grad + contract_cols(grad_after, conv_kernel[0])
    norm_grad = act_grad * gelu_slope(normed)
    gain_share = jnp.sum(norm_grad * xhat, axis=0)
    hat_grad = norm_grad * norm_gain_vector
    back = (hat_grad - xhat * jnp.mean(hat_grad * xhat, axis=-1, keepdims=True)) / rms
    stream_grad = (cotan.astype(F32) + back).astype(BF16)

    parts = [core_sum(share, core).astype(BF16).reshape(32, 1, 48, 384) for share in shares]
    packed = jnp.concatenate(
        [jnp.stack([parts[0], parts[1]], 2), jnp.stack([parts[2], parts[3]], 2)], 1
    ).reshape(64, 2, 48, 384)
    got = lax.all_to_all(packed, CHIP, 0, 0, tiled=True)
    total = jnp.sum(got.astype(F32), axis=0)
    gain_got = lax.all_to_all(gain_share.reshape(128, 12), CHIP + ("core",), 0, 0, tiled=True)
    gain_total = jnp.sum(gain_got, axis=0)
    whole = lax.all_gather(total, ("xl", "core"))
    gain_grad = lax.all_gather(gain_total, ("xl", "core"), tiled=True)
    whole = whole.reshape(2, 2, 2, 48, 384).transpose(0, 2, 3, 1, 4).reshape(4, 48, 768)
    kernel_grad = whole[:3]
    point_grad = whole[3].T
    return (stream_out[None], stream_grad[None], kernel_grad, point_grad, gain_grad)


def solution(mesh):
    fine = Mesh(mesh.devices.reshape(2, 4, 4, 2, 2), ("xh", "y", "z", "xl", "core"))
    ctx, rep = ("xh", "y", "z"), ("xl", "core")
    placed = (P(rep, ctx, None), P(), P(), P(), P(rep, ctx, None))
    return jax.shard_map(
        shards,
        mesh=fine,
        in_specs=placed,
        out_specs=(
            P(rep, ctx, None),
            P(rep, ctx, None),
            P(None, ctx, None),
            P(None, ctx),
            P(ctx),
        ),
        check_vma=False,
    )
```

time: 654 us -> 209 us (0.32)
  waiting for transfers between devices: 453 us -> 63.6 us
  blocking collectives: 104 us -> 53.9 us
  starting transfers between devices: 12 us -> 33.8 us
  between operations: 14.6 us -> 1.67 us
  matrix products: 42.7 us -> 35.3 us
    reduce_scatter x2 -> x0, waiting for transfers between devices: 331 us -> none  [the longest x1 261 us: shards(): lax.psum_scatter(kernel_part, 'ctx', scatter_dimension=1, tiled=True)]
    unnamed x1, blocking collectives: 81.2 us -> 45.9 us
    psum x1 -> x0, waiting for transfers between devices: 34.5 us -> none  [shards(): lax.psum((shares[0], shares[1], shares[2]), 'rep')]
    ppermute x4 -> x8, waiting for transfers between devices: 88 us -> 56.4 us  [the longest x4 55.6 us: shifted(): return lax.ppermute(value, axes, [(i, (i + by) % 32) for i in range(32)])]
    psum x1 -> x0, blocking collectives: 22.7 us -> none  [shards(): lax.psum((shares[0], shares[1], shares[2]), 'rep')]
    all_to_all x0 -> x2, starting transfers between devices: none -> 21.4 us  [the longest x1 11.2 us: shards(): lax.all_to_all(gain_share.reshape(128, 12), CHIP + ('core',), 0, 0, tiled...]
    another operation x1 -> x0, other arithmetic: 11.1 us -> none  [shards(): jnp.stack([contract_rows(backward_neighbor, before_norm_gradient), contra...]
    all_gather x0 -> x1, blocking collectives: none -> 8 us  [shards(): whole = lax.all_gather(total, ('xl', 'core'))]
  transfers between devices with their start and end apart: 7 -> 10, of which waited for: 7 -> 5; matrix products, arithmetic and copies ran while one was open for 8% -> 18% of each run, Pallas kernels for 0% -> 0%
where the time goes in v1:
time: 209 us
  waiting for transfers between devices  63.6 us (30%)
  blocking collectives  53.9 us (26%)
  matrix products  35.3 us (17%)
  starting transfers between devices  33.8 us (16%)
  other arithmetic  16.5 us (8%)
  local copies, waits for them, and re-layouts  4.12 us (2%)
    ppermute x4, waiting for transfers between devices, shifted(): return lax.ppermute(value, axes, [(i, (i + by) % 32) for i in range(32)])  55.6 us
    unnamed x1, blocking collectives  45.9 us
    dot_general x4, matrix products, dot(): return jnp.dot(left, right, preferred_element_type=F32)  16.2 us
    dot_general x4, matrix products, contract_cols(): lax.dot_general(left, right, (((1,), (1,)), ((), ())), preferred_element_...  11.6 us
    all_to_all x1, starting transfers between devices, shards(): lax.all_to_all(gain_share.reshape(128, 12), CHIP + ('core',), 0, 0, tiled...  11.2 us
    all_to_all x1, starting transfers between devices, shards(): got = lax.all_to_all(packed, CHIP, 0, 0, tiled=True)  10.2 us
    ppermute x4, starting transfers between devices, shifted(): return lax.ppermute(value, axes, [(i, (i + by) % 32) for i in range(32)])  9.25 us
    all_gather x1, blocking collectives, shards(): whole = lax.all_gather(total, ('xl', 'core'))  8 us
  transfers between devices with their start and end apart: 10, of which 5 were waited for; matrix products, arithmetic and copies ran while one was open for 18% of the time, Pallas kernels for 0%

profile of v1, /device:TPU:1, one launch (start us, length us, event | category | flops | bytes accessed | tf_op | source)
XLA Modules:
  0.0 209.0 jit_solution(18109958029247630412)
XLA Ops:
  0.7 1.9 fusion.4
  2.7 2.1 fusion.54
  4.8 4.5 %fusion.59 = bf16[512,768]{1,0:T(8,128)(2,1)} fusion(bf16[512,1536]{1,0:T(8,128)(2,1)S(1)} %fusion.54, bf16[3,1536,768]{2,1,0:T(8,128)(2,1)} %param.7), kind=kOutput, calls=%fused_computation.85 | convolution fusion | flops 1208352768 | bytes 4718592 | tf_op jit(solution)/shard_map/dot_general | solution.py:16
  9.3 3.7 %collective-permute-start = (bf16[512,768]{1,0:T(8,128)(2,1)}, bf16[512,768]{1,0:T(8,128)(2,1)S(1)}, u32[]{:S(2)}, u32[]{:S(2)}) collective-permute-start(bf16[512,768]{1,0:T(8,128)(2,1)} %fusion.59), channel_id=1, source_target_pairs={{0,32},{4,36},{8,40},{12,44},{16,48},{20,52},{24,56},{28,60},{32,6... | collective-permute-start | bytes 2359304 | tf_op jit(solution)/shard_map/ppermute | solution.py:33
  13.1 3.9 %fusion.62 = bf16[512,768]{1,0:T(8,128)(2,1)} fusion(bf16[512,1536]{1,0:T(8,128)(2,1)S(1)} %fusion.54, bf16[3,1536,768]{2,1,0:T(8,128)(2,1)} %param.7), kind=kOutput, calls=%fused_computation.86 | convolution fusion | flops 1208352768 | bytes 4718592 | tf_op jit(solution)/shard_map/dot_general | solution.py:16
  17.0 2.5 %collective-permute-start.1 = (bf16[512,768]{1,0:T(8,128)(2,1)}, bf16[512,768]{1,0:T(8,128)(2,1)}, u32[]{:S(2)}, u32[]{:S(2)}) collective-permute-start(bf16[512,768]{1,0:T(8,128)(2,1)} %fusion.62), channel_id=1, source_target_pairs={{0,96},{4,100},{8,104},{12,108},{16,112},{20,116},{24,120},{28,124... | collective-permute-start | bytes 2359304 | tf_op jit(solution)/shard_map/ppermute | solution.py:33
  19.4 3.7 %fusion.34 = f32[512,768]{1,0:T(8,128)S(1)} fusion(bf16[512,1536]{1,0:T(8,128)(2,1)} %copy-done.9, bf16[3,1536,768]{2,1,0:T(8,128)(2,1)} %param.7), kind=kOutput, calls=%fused_computation.48 | convolution fusion | flops 1207959552 | bytes 5505024 | tf_op jit(solution)/shard_map/dot_general | solution.py:16
  23.1 23.3 %collective-permute-done = bf16[512,768]{1,0:T(8,128)(2,1)S(1)} collective-permute-done((bf16[512,768]{1,0:T(8,128)(2,1)}, bf16[512,768]{1,0:T(8,128)(2,1)S(1)}, u32[]{:S(2)}, u32[]{:S(2)}) %collective-permute-start) | collective-permute-done | bytes 786464 | tf_op jit(solution)/shard_map/ppermute | solution.py:33
  46.4 4.2 %collective-permute-done.1 = bf16[512,768]{1,0:T(8,128)(2,1)} collective-permute-done((bf16[512,768]{1,0:T(8,128)(2,1)}, bf16[512,768]{1,0:T(8,128)(2,1)}, u32[]{:S(2)}, u32[]{:S(2)}) %collective-permute-start.1) | collective-permute-done | bytes 786464 | tf_op jit(solution)/shard_map/ppermute | solution.py:33
  50.7 3.4 %fusion.53 = (bf16[512,768]{1,0:T(8,128)(2,1)S(1)}, bf16[512,768]{1,0:T(8,128)(2,1)S(1)}) fusion(bf16[512,768]{1,0:T(8,128)(2,1)} %collective-permute-done.1, f32[512,768]{1,0:T(8,128)S(1)} %fusion.34, bf16[512,768]{1,0:T(8,128)(2,1)S(1)} %collective-permute-done, bf16[768,1536]{1,0:T(8,128)(2,1)S(1)} %copy-done, bf16[1,512,1536]{2,1,0:T(8,128)(2,1)S(1)} %copy-done.6), kind=kOutput, calls=%fused_computation.77 | convolution fusion | flops 1217396736 | bytes 8650752 | tf_op jit(solution)/shard_map/dot_general | solution.py:26
  54.1 1.9 collective-permute-start.3
  56.0 1.2 collective-permute-start.2
  57.1 1.6 convolution_bitcast_fusion
  58.7 1.4 select_convert_fusion
  61.2 1.4 fusion.32
  62.6 28.1 %collective-permute-done.2 = bf16[512,768]{1,0:T(8,128)(2,1)S(1)} collective-permute-done((bf16[512,768]{1,0:T(8,128)(2,1)S(1)}, bf16[512,768]{1,0:T(8,128)(2,1)S(1)}, u32[]{:S(2)}, u32[]{:S(2)}) %collective-permute-start.2) | collective-permute-done | bytes 786464 | tf_op jit(solution)/shard_map/ppermute | solution.py:33
  90.7 1.4 convolution_add_fusion.1
  92.2 5.4 %multiply_reduce_fusion = (f32[1536]{0:T(1024)S(1)}, f32[512]{0:T(512)S(1)}, bf16[512,1536]{1,0:T(8,128)(2,1)}, f32[512,1536]{1,0:T(8,128)}) fusion(f32[512]{0:T(512)S(1)} %add_sqrt_fusion, bf16[1,512,1536]{2,1,0:T(8,128)(2,1)S(1)} %copy-done.4, f32[1536]{0:T(1024)S(1)} %copy-done.15, f32[512,1536]{1,0:T(8,128)S(1)} %convolution_add_fusion.1, ...), kind=kOutput, calls=%fused_computation.34 | convolution fusion | flops 1229977600 | bytes 12601344 | tf_op jit(solution)/shard_map/dot_general | solution.py:26
  98.3 11.2 %all-to-all-start.1 = ((f32[128,1,12]{2,1,0:T(1,128)}), f32[128,1,12]{2,1,0:T(1,128)S(1)}, u32[]{:S(2)}, u32[]{:S(2)}) async-start(f32[128,1,12]{2,1,0:T(1,128)} %bitcast.22), calls=%async_computation.1 | async-start | bytes 131072 | tf_op jit(solution)/shard_map/all_to_all | solution.py:81
  109.5 3.1 %fusion.66 = f32[1536,768]{1,0:T(8,128)S(1)} fusion(bf16[512,1536]{1,0:T(8,128)(2,1)} %get-tuple-element.9, bf16[512,768]{1,0:T(8,128)(2,1)} %copy-done.14), kind=kOutput, calls=%fused_computation.91 | convolution fusion | flops 1207959552 | bytes 7077888 | tf_op jit(solution)/shard_map/dot_general | solution.py:20
  112.7 1.4 fusion.67
  114.3 1.1 collective-permute-start.6
  115.8 1.4 fusion.65
  118.3 1.6 add_convert_fusion.1
  121.7 2.5 %maximum_maximum_fusion = bf16[32,2,2,48,384]{4,3,2,1,0:T(8,128)(2,1)} fusion(bf16[32,1,1,48,384]{4,3,2,1,0:T(8,128)(2,1)S(1)} %bitcast.104, bf16[32,1,1,48,384]{4,3,2,1,0:T(8,128)(2,1)S(1)} %bitcast.105, bf16[32,1,1,48,384]{4,3,2,1,0:T(8,128)(2,1)S(1)} %bitcast.106, bf16[32,1,1,48,384]{4,3,2,1,0:T(8,128)(2,1)S(1)} %bitcast.107), kind=kLoop, calls=%fused_computation.2 | loop fusion | flops 7077888 | bytes 9437184 | tf_op jit(solution)/shard_map/concatenate | solution.py:76
  124.2 10.2 %all-to-all-start = ((bf16[64,2,48,384]{3,2,1,0:T(8,128)(2,1)}), bf16[64,2,48,384]{3,2,1,0:T(8,128)(2,1)}, u32[]{:S(2)}, u32[]{:S(2)}) async-start(bf16[64,2,48,384]{3,2,1,0:T(8,128)(2,1)} %bitcast.103), calls=%async_computation | async-start | bytes 9437184 | tf_op jit(solution)/shard_map/all_to_all | solution.py:79
  135.7 4.1 %fusion.25 = bf16[1,512,1536]{2,1,0:T(8,128)(2,1)} fusion(bf16[512,768]{1,0:T(8,128)(2,1)S(1)} %copy-done.11, bf16[768,1536]{1,0:T(8,128)(2,1)S(1)} %copy-done, bf16[1,512,1536]{2,1,0:T(8,128)(2,1)} %param.5), kind=kOutput, calls=%fused_computation.39 | convolution fusion | flops 1210318848 | bytes 6291456 | tf_op jit(solution)/shard_map/dot_general | solution.py:16
  139.8 2.2 %fusion.58 = bf16[1,512,1536]{2,1,0:T(8,128)(2,1)} fusion(f32[512]{0:T(512)S(1)} %add_sqrt_fusion, f32[512]{0:T(512)S(1)} %broadcast_multiply_fusion, f32[512,1536]{1,0:T(8,128)S(1)} %copy-done.8, f32[1536]{0:T(1024)S(1)} %copy-done.15, bf16[1,512,1536]{2,1,0:T(8,128)(2,1)S(1)} %copy-done.7, bf16[1,512,1536]{2,1,0:T(8,128)(2,1)S(1)} %copy-done.5), kind=kLoop, calls=%fused_computation.84 | loop fusion | flops 7077888 | bytes 7874560 | tf_op jit(solution)/shard_map/broadcast_in_dim | solution.py:88
  142.4 45.9 %all-reduce = f32[48]{0:T(128)} all-reduce(f32[48]{0:T(128)S(1)} %dynamic-update-slice), channel_id=1, replica_groups=mesh['xh'=2,'y'=4,'z'=4,'xl'=2,'core'=2] {'xl','core'}, use_global_device_ids=true, to_apply=%add | all-reduce | flops 48 | bytes 384
  188.3 7.2 %all-to-all-done = bf16[64,2,48,384]{3,2,1,0:T(8,128)(2,1)} async-done(((bf16[64,2,48,384]{3,2,1,0:T(8,128)(2,1)}), bf16[64,2,48,384]{3,2,1,0:T(8,128)(2,1)}, u32[]{:S(2)}, u32[]{:S(2)}) %all-to-all-start) | async-done | bytes 4718624 | tf_op jit(solution)/shard_map/all_to_all | solution.py:79
  195.5 3.0 %convert_reduce_fusion = f32[2,48,384]{2,1,0:T(8,128)S(1)} fusion(bf16[64,2,48,384]{3,2,1,0:T(8,128)(2,1)} %all-to-all-done), kind=kLoop, calls=%fused_computation | loop fusion | flops 4681728 | bytes 4866048 | tf_op jit(solution)/shard_map/reduce_sum | solution.py:80
  198.5 8.0 %all-gather = f32[8,48,384]{2,1,0:T(8,128)S(1)} all-gather(f32[2,48,384]{2,1,0:T(8,128)S(1)} %convert_reduce_fusion), channel_id=2, replica_groups=mesh['xh'=2,'y'=4,'z'=4,'xl'=2,'core'=2] {'xl','core'}, dimensions={0}, use_global_device_ids=true | all-gather | bytes 737280 | tf_op jit(solution)/shard_map/all_gather | solution.py:83
  (70 shorter events, 8.6 us)
Async XLA Ops:
  0.6 50.1 %copy-start = (bf16[768,1536]{1,0:T(8,128)(2,1)S(1)}, bf16[768,1536]{1,0:T(8,128)(2,1)}, u32[]{:S(2)}) copy-start(bf16[768,1536]{1,0:T(8,128)(2,1)} %param.8) | copy-start | bytes 7077892
  0.6 2.0 copy-start.3
  4.8 8.3 %copy-start.9 = (bf16[512,1536]{1,0:T(8,128)(2,1)}, bf16[512,1536]{1,0:T(8,128)(2,1)S(1)}, u32[]{:S(2)}) copy-start(bf16[512,1536]{1,0:T(8,128)(2,1)S(1)} %fusion.54) | copy-start | bytes 4718596
  9.3 37.1 %collective-permute-start = (bf16[512,768]{1,0:T(8,128)(2,1)}, bf16[512,768]{1,0:T(8,128)(2,1)S(1)}, u32[]{:S(2)}, u32[]{:S(2)}) collective-permute-start(bf16[512,768]{1,0:T(8,128)(2,1)} %fusion.59), channel_id=1, source_target_pairs={{0,32},{4,36},{8,40},{12,44},{16,48},{20,52},{24,56},{28,60},{32,6... | collective-permute-start | bytes 2359304 | tf_op jit(solution)/shard_map/ppermute | solution.py:33
  17.0 33.7 %collective-permute-start.1 = (bf16[512,768]{1,0:T(8,128)(2,1)}, bf16[512,768]{1,0:T(8,128)(2,1)}, u32[]{:S(2)}, u32[]{:S(2)}) collective-permute-start(bf16[512,768]{1,0:T(8,128)(2,1)} %fusion.62), channel_id=1, source_target_pairs={{0,96},{4,100},{8,104},{12,108},{16,112},{20,116},{24,120},{28,124... | collective-permute-start | bytes 2359304 | tf_op jit(solution)/shard_map/ppermute | solution.py:33
  19.4 31.2 %copy-start.6 = (bf16[1,512,1536]{2,1,0:T(8,128)(2,1)S(1)}, bf16[1,512,1536]{2,1,0:T(8,128)(2,1)}, u32[]{:S(2)}) copy-start(bf16[1,512,1536]{2,1,0:T(8,128)(2,1)} %param.9) | copy-start | bytes 4718596
  19.4 41.7 %slice-start.2 = ((s8[7077888]{0:T(1024)(128)(4,1)}), s8[4194304]{0:T(1024)(128)(4,1)S(1)}, s32[]{:S(2)}) async-start(s8[7077888]{0:T(1024)(128)(4,1)} %bitcast.109), calls=%async_computation.4 | async-start | bytes 8388608
  23.1 38.0 %slice-start.3 = ((s8[7077888]{0:T(1024)(128)(4,1)}), s8[2883584]{0:T(1024)(128)(4,1)S(1)}, s32[]{:S(2)}) async-start(s8[7077888]{0:T(1024)(128)(4,1)} %bitcast.109), calls=%async_computation.5 | async-start | bytes 5767168
  54.1 4.6 %copy-start.10 = (bf16[512,768]{1,0:T(8,128)(2,1)}, bf16[512,768]{1,0:T(8,128)(2,1)S(1)}, u32[]{:S(2)}) copy-start(bf16[512,768]{1,0:T(8,128)(2,1)S(1)} %get-tuple-element.8) | copy-start | bytes 2359300
  54.1 7.1 %copy-start.14 = (bf16[512,768]{1,0:T(8,128)(2,1)}, bf16[512,768]{1,0:T(8,128)(2,1)S(1)}, u32[]{:S(2)}) copy-start(bf16[512,768]{1,0:T(8,128)(2,1)S(1)} %get-tuple-element.7) | copy-start | bytes 2359300
  54.1 38.1 %collective-permute-start.3 = (bf16[512,768]{1,0:T(8,128)(2,1)S(1)}, bf16[512,768]{1,0:T(8,128)(2,1)S(1)}, u32[]{:S(2)}, u32[]{:S(2)}) collective-permute-start(bf16[512,768]{1,0:T(8,128)(2,1)S(1)} %get-tuple-element.7), channel_id=1, source_target_pairs={{0,96},{4,100},{8,104},{12,108},{16,112},{20,116},{24,120},{28,124... | collective-permute-start | bytes 2359304 | tf_op jit(solution)/shard_map/ppermute | solution.py:33
  56.0 34.8 %collective-permute-start.2 = (bf16[512,768]{1,0:T(8,128)(2,1)S(1)}, bf16[512,768]{1,0:T(8,128)(2,1)S(1)}, u32[]{:S(2)}, u32[]{:S(2)}) collective-permute-start(bf16[512,768]{1,0:T(8,128)(2,1)S(1)} %get-tuple-element.7), channel_id=1, source_target_pairs={{0,32},{4,36},{8,40},{12,44},{16,48},{20,52},{24,56},{28,60},{32,6... | collective-permute-start | bytes 2359304 | tf_op jit(solution)/shard_map/ppermute | solution.py:33
  58.7 3.9 %copy-start.1 = (f32[1536,768]{1,0:T(8,128)}, f32[1536,768]{1,0:T(8,128)S(1)}, u32[]{:S(2)}) copy-start(f32[1536,768]{1,0:T(8,128)S(1)} %convolution_bitcast_fusion) | copy-start | bytes 14155780
  60.1 58.2 %collective-permute-start.7 = (bf16[1536,384]{1,0:T(8,128)(2,1)}, bf16[1536,384]{1,0:T(8,128)(2,1)}, u32[]{:S(2)}, u32[]{:S(2)}) collective-permute-start(bf16[1536,384]{1,0:T(8,128)(2,1)} %select_convert_fusion), channel_id=1, source_target_pairs={{0,1},{1,0},{2,3},{3,2},{4,5},{5,4},{6,7},{7,6},{8,9},{9,8},{10,11... | collective-permute-start | bytes 3538952 | tf_op jit(solution)/shard_map/ppermute | solution.py:41
  62.6 29.6 %copy-start.4 = (bf16[1,512,1536]{2,1,0:T(8,128)(2,1)S(1)}, bf16[1,512,1536]{2,1,0:T(8,128)(2,1)}, u32[]{:S(2)}) copy-start(bf16[1,512,1536]{2,1,0:T(8,128)(2,1)} %param.5) | copy-start | bytes 4718596
  62.6 29.6 %copy-start.15 = (f32[1536]{0:T(1024)S(1)}, f32[1536]{0:T(1024)}, u32[]{:S(2)}) copy-start(f32[1536]{0:T(1024)} %param.6) | copy-start | bytes 18436
  92.2 5.4 %copy-start.12 = (bf16[512,768]{1,0:T(8,128)(2,1)}, bf16[512,768]{1,0:T(8,128)(2,1)S(1)}, u32[]{:S(2)}) copy-start(bf16[512,768]{1,0:T(8,128)(2,1)S(1)} %collective-permute-done.3) | copy-start | bytes 2359300
  98.3 25.9 %all-to-all-start.1 = ((f32[128,1,12]{2,1,0:T(1,128)}), f32[128,1,12]{2,1,0:T(1,128)S(1)}, u32[]{:S(2)}, u32[]{:S(2)}) async-start(f32[128,1,12]{2,1,0:T(1,128)} %bitcast.22), calls=%async_computation.1 | async-start | bytes 131072 | tf_op jit(solution)/shard_map/all_to_all | solution.py:81
  109.5 3.2 %copy-start.2 = (bf16[512,1536]{1,0:T(8,128)(2,1)S(1)}, bf16[512,1536]{1,0:T(8,128)(2,1)}, u32[]{:S(2)}) copy-start(bf16[512,1536]{1,0:T(8,128)(2,1)} %get-tuple-element.9) | copy-start | bytes 4718596
  114.3 1.5 copy-start.13
  114.3 5.5 %collective-permute-start.6 = (bf16[1536,384]{1,0:T(8,128)(2,1)S(1)}, bf16[1536,384]{1,0:T(8,128)(2,1)S(1)}, u32[]{:S(2)}, u32[]{:S(2)}) collective-permute-start(bf16[1536,384]{1,0:T(8,128)(2,1)S(1)} %select_convert_fusion.1), channel_id=1, source_target_pairs={{0,1},{1,0},{2,3},{3,2},{4,5},{5,4},{6,7},{7,6},{8,9},{9,8},{10,11... | collective-permute-start | bytes 3538952 | tf_op jit(solution)/shard_map/ppermute | solution.py:41
  115.5 2.8 %slice-start = ((s8[4718592]{0:T(1024)(128)(4,1)}), s8[4194304]{0:T(1024)(128)(4,1)S(1)}, s32[]{:S(2)}) async-start(s8[4718592]{0:T(1024)(128)(4,1)} %bitcast.101), calls=%async_computation.2 | async-start | bytes 8388608
  115.7 2.6 %slice-start.1 = ((s8[4718592]{0:T(1024)(128)(4,1)}), s8[524288]{0:T(1024)(128)(4,1)S(1)}, s32[]{:S(2)}) async-start(s8[4718592]{0:T(1024)(128)(4,1)} %bitcast.101), calls=%async_computation.3 | async-start | bytes 1048576
  115.7 4.5 %collective-permute-start.5 = (bf16[1536,384]{1,0:T(8,128)(2,1)S(1)}, bf16[1536,384]{1,0:T(8,128)(2,1)S(1)}, u32[]{:S(2)}, u32[]{:S(2)}) collective-permute-start(bf16[1536,384]{1,0:T(8,128)(2,1)S(1)} %select_convert_fusion.2), channel_id=1, source_target_pairs={{0,1},{1,0},{2,3},{3,2},{4,5},{5,4},{6,7},{7,6},{8,9},{9,8},{10,11... | collective-permute-start | bytes 3538952 | tf_op jit(solution)/shard_map/ppermute | solution.py:41
  117.5 3.9 %collective-permute-start.4 = (bf16[1536,384]{1,0:T(8,128)(2,1)S(1)}, bf16[1536,384]{1,0:T(8,128)(2,1)S(1)}, u32[]{:S(2)}, u32[]{:S(2)}) collective-permute-start(bf16[1536,384]{1,0:T(8,128)(2,1)S(1)} %select_convert_fusion.3), channel_id=1, source_target_pairs={{0,1},{1,0},{2,3},{3,2},{4,5},{5,4},{6,7},{7,6},{8,9},{9,8},{10,11... | collective-permute-start | bytes 3538952 | tf_op jit(solution)/shard_map/ppermute | solution.py:41
  124.2 10.2 %copy-start.16 = (u32[128]{0:T(128)S(1)}, u32[128]{0:T(128)}, u32[]{:S(2)}) copy-start(u32[128]{0:T(128)} %constant.35) | copy-start | bytes 1540
  124.2 11.5 %copy-start.11 = (bf16[512,768]{1,0:T(8,128)(2,1)S(1)}, bf16[512,768]{1,0:T(8,128)(2,1)}, u32[]{:S(2)}) copy-start(bf16[512,768]{1,0:T(8,128)(2,1)} %copy-done.10) | copy-start | bytes 2359300
  124.2 71.3 %all-to-all-start = ((bf16[64,2,48,384]{3,2,1,0:T(8,128)(2,1)}), bf16[64,2,48,384]{3,2,1,0:T(8,128)(2,1)}, u32[]{:S(2)}, u32[]{:S(2)}) async-start(bf16[64,2,48,384]{3,2,1,0:T(8,128)(2,1)} %bitcast.103), calls=%async_computation | async-start | bytes 9437184 | tf_op jit(solution)/shard_map/all_to_all | solution.py:79
  135.7 4.1 %copy-start.5 = (bf16[1,512,1536]{2,1,0:T(8,128)(2,1)S(1)}, bf16[1,512,1536]{2,1,0:T(8,128)(2,1)}, u32[]{:S(2)}) copy-start(bf16[1,512,1536]{2,1,0:T(8,128)(2,1)} %param.5) | copy-start | bytes 4718596
  135.7 4.1 %copy-start.7 = (bf16[1,512,1536]{2,1,0:T(8,128)(2,1)S(1)}, bf16[1,512,1536]{2,1,0:T(8,128)(2,1)}, u32[]{:S(2)}) copy-start(bf16[1,512,1536]{2,1,0:T(8,128)(2,1)} %param.9) | copy-start | bytes 4718596
  135.7 4.1 %copy-start.8 = (f32[512,1536]{1,0:T(8,128)S(1)}, f32[512,1536]{1,0:T(8,128)}, u32[]{:S(2)}) copy-start(f32[512,1536]{1,0:T(8,128)} %get-tuple-element.10) | copy-start | bytes 9437188

commit v2 on v1

v2 whole, which is shorter than its diff:
```python
import jax
import jax.numpy as jnp
from jax import lax
from jax.sharding import Mesh, PartitionSpec as P

F32 = jnp.float32
BF16 = jnp.bfloat16
CHIP = ("xh", "y", "z", "xl")
PLANE = ("xh", "y", "xl")
CHUNKS = 2
WIDE = 768 // CHUNKS


def gelu_slope(value):
    return jax.jvp(jax.nn.gelu, (value,), (jnp.ones_like(value),))[1]


def dot(left, right):
    return jnp.dot(left, right, preferred_element_type=F32)


def contract_rows(left, right):
    return lax.dot_general(
        left, right, (((0,), (0,)), ((), ())), preferred_element_type=F32
    )


def contract_cols(left, right):
    return lax.dot_general(
        left, right, (((1,), (1,)), ((), ())), preferred_element_type=F32
    )


def swap_x(value):
    return lax.ppermute(value, "xh", [(0, 1), (1, 0)])


def swap_y(value):
    return lax.ppermute(value, "y", [(0, 2), (1, 3), (2, 0), (3, 1)])


def swap_core(value):
    return lax.ppermute(value, "core", [(0, 1), (1, 0)])


def core_sum(first, second, takes_first):
    kept = jnp.where(takes_first, first, second)
    away = jnp.where(takes_first, second, first).astype(BF16)
    return kept + swap_core(away).astype(F32)


def shards(stream, norm_gain_vector, conv_kernel, point_kernel, out_grad):
    core = lax.axis_index("core")
    odd = lax.axis_index("y") // 2
    rows = stream[0].astype(F32)
    cotan = out_grad[0]
    rms = jnp.sqrt(jnp.mean(rows * rows, axis=-1, keepdims=True) + 1e-06)
    xhat = rows / rms
    normed = xhat * norm_gain_vector
    act = jax.nn.gelu(normed).astype(BF16)
    near = lax.dynamic_index_in_dim(conv_kernel, 2 * odd, 0, False)
    far = lax.dynamic_index_in_dim(conv_kernel, 2 - 2 * odd, 0, False)
    cut = [slice(c * WIDE, (c + 1) * WIDE) for c in range(CHUNKS)]

    crossed = [swap_x(dot(act, far[:, at]).astype(BF16)) for at in cut]
    summed = [
        swap_y((dot(act, near[:, at]) + got.astype(F32)).astype(BF16))
        for at, got in zip(cut, crossed)
    ]
    pre = [dot(act, conv_kernel[1][:, at]) + got.astype(F32) for at, got in zip(cut, summed)]
    mid = [jax.nn.gelu(value).astype(BF16) for value in pre]
    pre_grad = [
        (contract_cols(cotan, point_kernel[at]) * gelu_slope(value)).astype(BF16)
        for at, value in zip(cut, pre)
    ]
    grad_near = [swap_y(value) for value in pre_grad]
    grad_far = [swap_x(value) for value in grad_near]

    early = []
    for c in range(CHUNKS):
        share = core_sum(
            contract_rows(act, pre_grad[c]), contract_rows(cotan, mid[c]), core == 0
        ).astype(BF16)
        share = share.reshape(8, 4, 48, WIDE).transpose(1, 0, 2, 3)
        got = lax.all_to_all(share, ("z",), 0, 0, tiled=True)
        early.append(jnp.sum(got.astype(F32), axis=0).astype(BF16))
    early = jnp.stack(early, 1).reshape(16, 48, WIDE)
    early = lax.all_to_all(early, PLANE, 0, 0, tiled=True)
    early = jnp.sum(early.astype(F32), axis=0)

    stream_out = rows
    act_grad = None
    for c, at in enumerate(cut):
        stream_out = stream_out + dot(mid[c], point_kernel[at])
    stream_out = stream_out.astype(BF16)
    act_grad = contract_cols(jnp.concatenate(pre_grad, 1), conv_kernel[1])
    act_grad = act_grad + contract_cols(jnp.concatenate(grad_near, 1), near)
    act_grad = act_grad + contract_cols(jnp.concatenate(grad_far, 1), far)
    norm_grad = act_grad * gelu_slope(normed)
    gain_share = jnp.sum(norm_grad * xhat, axis=0)
    hat_grad = norm_grad * norm_gain_vector
    back = (hat_grad - xhat * jnp.mean(hat_grad * xhat, axis=-1, keepdims=True)) / rms
    stream_grad = (cotan.astype(F32) + back).astype(BF16)

    late = [
        core_sum(
            contract_rows(act, grad_near[c]), contract_rows(act, grad_far[c]), core == odd
        ).astype(BF16).reshape(32, 48, WIDE // 128, 128).transpose(0, 2, 1, 3).reshape(32, -1, 128)
        for c in range(CHUNKS)
    ]
    late = jnp.stack(late, 1).reshape(64, -1, 128)
    depth = late.shape[1]
    gain = gain_share + swap_core(gain_share)
    gain = jnp.pad(gain.astype(BF16).reshape(64, 1, 24), ((0, 0), (0, 15), (0, 104)))
    late = lax.all_to_all(jnp.concatenate([late, gain], 1), CHIP, 0, 0, tiled=True)
    late = jnp.sum(late.astype(F32), axis=0)
    gain = jnp.pad(late[depth:depth + 1, :24].reshape(24), (0, 104)).reshape(1, 128)
    late = late[:depth]
    early = early.reshape(48, WIDE // 128, 128).transpose(1, 0, 2).reshape(depth, 128)
    mine = jnp.concatenate([early, late, jnp.pad(gain, ((0, 7), (0, 0)))], 0)
    whole = lax.all_gather(mine, ("xl", "core"))

    def matrix(part):
        part = part.reshape(2, 2, WIDE // 128, 48, 128).transpose(1, 3, 0, 2, 4)
        return part.reshape(2, 48, 768)

    middle, point = matrix(whole[:, :depth])
    before, after = matrix(whole[:, depth:2 * depth])
    gain_grad = whole.reshape(2, 2, -1, 128)[:, 0, 2 * depth, :24].reshape(48)
    kernel_grad = jnp.stack([before, middle, after])
    return (stream_out[None], stream_grad[None], kernel_grad, point.T, gain_grad)


def solution(mesh):
    fine = Mesh(mesh.devices.reshape(2, 4, 4, 2, 2), ("xh", "y", "z", "xl", "core"))
    ctx, rep = ("xh", "y", "z"), ("xl", "core")
    placed = (P(rep, ctx, None), P(), P(), P(), P(rep, ctx, None))
    return jax.shard_map(
        shards,
        mesh=fine,
        in_specs=placed,
        out_specs=(
            P(rep, ctx, None),
            P(rep, ctx, None),
            P(None, ctx, None),
            P(None, ctx),
            P(ctx),
        ),
        check_vma=False,
    )
```

time: 209 us -> 207 us (level)
  blocking collectives: 53.9 us -> 11.3 us
  starting transfers between devices: 33.8 us -> 45.1 us
  matrix products: 35.3 us -> 46.1 us
  other arithmetic: 16.5 us -> 27.1 us
  local copies, waits for them, and re-layouts: 4.12 us -> 13.8 us
    unnamed x1 -> x0, blocking collectives: 45.9 us -> none
    ppermute x8 -> x13, waiting for transfers between devices: 56.4 us -> 22.8 us  [the longest x4 19.3 us: swap_x(): return lax.ppermute(value, 'xh', [(0, 1), (1, 0)])]
    all_to_all x2 -> x4, waiting for transfers between devices: 7.21 us -> 38.7 us  [the longest x1 21.6 us: shards(): lax.all_to_all(jnp.concatenate([late, gain], 1), CHIP, 0, 0, tiled=True)]
    ppermute x8 -> x13, starting transfers between devices: 12.3 us -> 23.3 us  [the longest x4 10.3 us: swap_y(): return lax.ppermute(value, 'y', [(0, 2), (1, 3), (2, 0), (3, 1)])]
    dot_general x4 -> x8, matrix products: 7.56 us -> 17 us  [contract_rows(): lax.dot_general(left, right, (((0,), (0,)), ((), ())), preferred_element_...]
    reduce_sum x2 -> x4, other arithmetic: 3.17 us -> 7.89 us  [the longest x2 4.62 us: shards(): early.append(jnp.sum(got.astype(F32), axis=0).astype(BF16))]
    convert_element_type x8 -> x5, other arithmetic: 4.6 us -> 8.36 us  [the longest x2 5.71 us: shards(): late = [core_sum(contract_rows(act, grad_near[c]), contract_rows(act, gra...]
    squeeze x0 -> x1, local copies, waits for them, and re-layouts: none -> 3.56 us  [shards(): far = lax.dynamic_index_in_dim(conv_kernel, 2 - 2 * odd, 0, False)]
  transfers between devices with their start and end apart: 10 -> 17, of which waited for: 5 -> 8; matrix products, arithmetic and copies ran while one was open for 18% -> 34% of each run, Pallas kernels for 0% -> 0%
where the time goes in v2:
time: 207 us; the launch traced here: 206 us
  waiting for transfers between devices  61.6 us (30%)
  matrix products  46.1 us (22%)
  starting transfers between devices  45.1 us (22%)
  other arithmetic  27.1 us (13%)
  local copies, waits for them, and re-layouts  13.8 us (7%)
  blocking collectives  11.3 us (5%)
    all_to_all x1, waiting for transfers between devices, shards(): lax.all_to_all(jnp.concatenate([late, gain], 1), CHIP, 0, 0, tiled=True)  21.6 us
    ppermute x4, waiting for transfers between devices, swap_x(): return lax.ppermute(value, 'xh', [(0, 1), (1, 0)])  19.3 us
    all_to_all x2, waiting for transfers between devices, shards(): got = lax.all_to_all(share, ('z',), 0, 0, tiled=True)  17.1 us
    dot_general x8, matrix products, contract_rows(): lax.dot_general(left, right, (((0,), (0,)), ((), ())), preferred_element_...  17 us
    dot_general x8, matrix products, dot(): return jnp.dot(left, right, preferred_element_type=F32)  14.5 us
    dot_general x5, matrix products, contract_cols(): lax.dot_general(left, right, (((1,), (1,)), ((), ())), preferred_element_...  14.5 us
    all_gather x1, blocking collectives, shards(): whole = lax.all_gather(mine, ('xl', 'core'))  11.3 us
    ppermute x4, starting transfers between devices, swap_y(): return lax.ppermute(value, 'y', [(0, 2), (1, 3), (2, 0), (3, 1)])  10.3 us
  transfers between devices with their start and end apart: 17, of which 8 were waited for; matrix products, arithmetic and copies ran while one was open for 34% of the time, Pallas kernels for 0%

profile of v2, /device:TPU:1, one launch (start us, length us, event | category | flops | bytes accessed | tf_op | source)
XLA Modules:
  0.0 206.1 jit_solution(17595909991740936270)
XLA Ops:
  4.7 3.6 %dynamic-slice_bitcast_fusion = (bf16[1536,768]{1,0:T(8,128)(2,1)S(1)}, bf16[1536,768]{1,0:T(8,128)(2,1)S(1)}, bf16[1536,768]{1,0:T(8,128)(2,1)S(1)}) fusion(bf16[3,1536,768]{2,1,0:T(8,128)(2,1)} %param.7, s32[]{:T(128)S(6)} %select_n.52, s32[]{:T(128)S(6)} %select_n.51), kind=kLoop, calls=%fused_computation.41 | loop fusion | bytes 14155784 | tf_op jit(solution)/shard_map/jit(dynamic_index_in_dim)/squeeze | solution.py:62
  9.1 3.7 %collective-permute-start.2 = (bf16[512,384]{0,1:T(8,128)(2,1)S(1)}, bf16[512,384]{0,1:T(8,128)(2,1)S(1)}, u32[]{:S(2)}, u32[]{:S(2)}) collective-permute-start(bf16[512,384]{0,1:T(8,128)(2,1)S(1)} %convolution_convert_fusion), channel_id=1, source_target_pairs={{0,64},{64,0},{1,65},{65,1},{2,66},{66,2},{3,67},{67,3},{4,68},{68... | collective-permute-start | bytes 1179656 | tf_op jit(solution)/shard_map/ppermute | solution.py:35
  16.1 5.0 %collective-permute-done.2 = bf16[512,384]{0,1:T(8,128)(2,1)S(1)} collective-permute-done((bf16[512,384]{0,1:T(8,128)(2,1)S(1)}, bf16[512,384]{0,1:T(8,128)(2,1)S(1)}, u32[]{:S(2)}, u32[]{:S(2)}) %collective-permute-start.2) | collective-permute-done | bytes 393248 | tf_op jit(solution)/shard_map/ppermute | solution.py:35
  22.7 3.3 %collective-permute-start.3 = (bf16[512,384]{0,1:T(8,128)(2,1)}, bf16[512,384]{0,1:T(8,128)(2,1)S(1)}, u32[]{:S(2)}, u32[]{:S(2)}) collective-permute-start(bf16[512,384]{0,1:T(8,128)(2,1)} %add_convert_fusion.5), channel_id=1, source_target_pairs={{0,32},{16,48},{32,0},{48,16},{1,33},{17,49},{33,1},{49,17},{2,34}... | collective-permute-start | bytes 1179656 | tf_op jit(solution)/shard_map/ppermute | solution.py:39
  31.8 3.4 %collective-permute-start.1 = (bf16[512,384]{0,1:T(8,128)(2,1)S(1)}, bf16[512,384]{0,1:T(8,128)(2,1)S(1)}, u32[]{:S(2)}, u32[]{:S(2)}) collective-permute-start(bf16[512,384]{0,1:T(8,128)(2,1)S(1)} %add_convert_fusion.6), channel_id=1, source_target_pairs={{0,32},{16,48},{32,0},{48,16},{1,33},{17,49},{33,1},{49,17},{2,34}... | collective-permute-start | bytes 1179656 | tf_op jit(solution)/shard_map/ppermute | solution.py:39
  35.2 2.6 %fusion.60 = bf16[512,384]{0,1:T(8,128)(2,1)S(1)} fusion(f32[512,384]{0,1:T(8,128)S(1)} %copy-done.14, bf16[512,384]{0,1:T(8,128)(2,1)S(1)} %collective-permute-done.3, bf16[768,1536]{1,0:T(8,128)(2,1)} %param.8, bf16[1,512,1536]{2,1,0:T(8,128)(2,1)S(1)} %copy-done.7), kind=kOutput, calls=%fused_computation.97 | convolution fusion | flops 607911936 | bytes 4325376 | tf_op jit(solution)/shard_map/dot_general | solution.py:29
  39.3 3.5 %collective-permute-done.1 = bf16[512,384]{0,1:T(8,128)(2,1)S(1)} collective-permute-done((bf16[512,384]{0,1:T(8,128)(2,1)S(1)}, bf16[512,384]{0,1:T(8,128)(2,1)S(1)}, u32[]{:S(2)}, u32[]{:S(2)}) %collective-permute-start.1) | collective-permute-done | bytes 393248 | tf_op jit(solution)/shard_map/ppermute | solution.py:39
  44.0 3.1 %collective-permute-start.4 = (bf16[512,384]{0,1:T(8,128)(2,1)S(1)}, bf16[512,384]{0,1:T(8,128)(2,1)S(1)}, u32[]{:S(2)}, u32[]{:S(2)}) collective-permute-start(bf16[512,384]{0,1:T(8,128)(2,1)S(1)} %fusion.48), channel_id=1, source_target_pairs={{0,32},{16,48},{32,0},{48,16},{1,33},{17,49},{33,1},{49,17},{2,34}... | collective-permute-start | bytes 1179656 | tf_op jit(solution)/shard_map/ppermute | solution.py:39
  49.3 4.9 %collective-permute-start.9 = (bf16[1536,384]{1,0:T(8,128)(2,1)S(1)}, bf16[1536,384]{1,0:T(8,128)(2,1)S(1)}, u32[]{:S(2)}, u32[]{:S(2)}) collective-permute-start(bf16[1536,384]{1,0:T(8,128)(2,1)S(1)} %get-tuple-element.21), channel_id=1, source_target_pairs={{0,1},{1,0},{2,3},{3,2},{4,5},{5,4},{6,7},{7,6},{8,9},{9,8},{10,11... | collective-permute-start | bytes 3538952 | tf_op jit(solution)/shard_map/ppermute | solution.py:43
  54.3 2.9 %select_convert_fusion.3 = (bf16[1536,384]{1,0:T(8,128)(2,1)}, f32[1536,384]{1,0:T(8,128)}) fusion(f32[1536,384]{1,0:T(8,128)S(1)} %fusion.77, pred[]{:T(512)S(6)} %eq.8, bf16[1,512,1536]{2,1,0:T(8,128)(2,1)S(1)} %copy-done.7, f32[512,384]{0,1:T(8,128)S(1)} %copy-done.12, bf16[512,384]{0,1:T(8,128)(2,1)S(1)} %collective-permute-done.1), kind=kOutput, calls=%fused_computation.40 | convolution fusion | flops 606732288 | bytes 8650753 | tf_op jit(solution)/shard_map/dot_general | solution.py:23
  57.4 3.2 %fusion.61 = f32[512,1536]{1,0:T(8,128)S(1)} fusion(bf16[512,384]{0,1:T(8,128)(2,1)S(1)} %fusion.60, bf16[512,384]{0,1:T(8,128)(2,1)S(1)} %fusion.48, bf16[3,1536,768]{2,1,0:T(8,128)(2,1)} %param.7), kind=kOutput, calls=%fused_computation.98 | convolution fusion | flops 1209532416 | bytes 6291456 | tf_op jit(solution)/shard_map/dot_general | solution.py:29
  60.6 2.8 %collective-permute-start.7 = (bf16[512,384]{0,1:T(8,128)(2,1)S(1)}, bf16[512,384]{0,1:T(8,128)(2,1)S(1)}, u32[]{:S(2)}, u32[]{:S(2)}) collective-permute-start(bf16[512,384]{0,1:T(8,128)(2,1)S(1)} %collective-permute-done.5), channel_id=1, source_target_pairs={{0,64},{64,0},{1,65},{65,1},{2,66},{66,2},{3,67},{67,3},{4,68},{68... | collective-permute-start | bytes 1179656 | tf_op jit(solution)/shard_map/ppermute | solution.py:35
  66.2 2.5 %fusion.79 = f32[1536,384]{1,0:T(8,128)} fusion(bf16[512,1536]{1,0:T(8,128)(2,1)S(1)} %multiply_convert_fusion, bf16[512,384]{0,1:T(8,128)(2,1)S(1)} %collective-permute-done.4), kind=kOutput, calls=%fused_computation.132 | convolution fusion | flops 603979776 | bytes 4325376 | tf_op jit(solution)/shard_map/dot_general | solution.py:23
  68.7 4.0 %collective-permute-done.7 = bf16[512,384]{0,1:T(8,128)(2,1)S(1)} collective-permute-done((bf16[512,384]{0,1:T(8,128)(2,1)S(1)}, bf16[512,384]{0,1:T(8,128)(2,1)S(1)}, u32[]{:S(2)}, u32[]{:S(2)}) %collective-permute-start.7) | collective-permute-done | bytes 393248 | tf_op jit(solution)/shard_map/ppermute | solution.py:35
  72.6 8.4 %collective-permute-done.6 = bf16[512,384]{0,1:T(8,128)(2,1)S(1)} collective-permute-done((bf16[512,384]{0,1:T(8,128)(2,1)S(1)}, bf16[512,384]{0,1:T(8,128)(2,1)S(1)}, u32[]{:S(2)}, u32[]{:S(2)}) %collective-permute-start.6) | collective-permute-done | bytes 393248 | tf_op jit(solution)/shard_map/ppermute | solution.py:35
  81.1 6.2 %multiply_reduce_fusion = (f32[1536]{0:T(1024)}, f32[512]{0:T(512)S(1)}, f32[512,1536]{1,0:T(8,128)}) fusion(f32[512]{0:T(512)S(1)} %add_sqrt_fusion, bf16[1,512,1536]{2,1,0:T(8,128)(2,1)S(1)} %copy-done.5, f32[1536]{0:T(1024)S(1)} %copy-done.28, f32[512,1536]{1,0:T(8,128)S(1)} %convolution_add_fusion.2, bf16[1536,768]{1,0:T(8,128)(2,1)S(1)} %copy-done.20, ...), kind=kOutput, calls=%fused_computation.23 | convolution fusion | flops 1229977600 | bytes 11026432 | tf_op jit(solution)/shard_map/dot_general | solution.py:29
  88.3 2.8 %select_convert_fusion = (bf16[1536,384]{1,0:T(8,128)(2,1)}, f32[1536,384]{1,0:T(8,128)}) fusion(f32[1536,384]{1,0:T(8,128)S(1)} %fusion.80, pred[]{:T(512)S(6)} %eq.9, bf16[512,1536]{1,0:T(8,128)(2,1)S(1)} %multiply_convert_fusion, bf16[512,384]{0,1:T(8,128)(2,1)S(1)} %collective-permute-done.7), kind=kOutput, calls=%fused_computation.34 | convolution fusion | flops 604569600 | bytes 7864321 | tf_op jit(solution)/shard_map/dot_general | solution.py:23
  92.7 5.0 %all-to-all-start.1 = ((bf16[4,8,48,384]{3,2,1,0:T(8,128)(2,1)}), bf16[4,8,48,384]{3,2,1,0:T(8,128)(2,1)}, u32[]{:S(2)}, u32[]{:S(2)}) async-start(bf16[4,8,48,384]{3,2,1,0:T(8,128)(2,1)} %bitcast.99), calls=%async_computation.1 | async-start | bytes 2359296 | tf_op jit(solution)/shard_map/all_to_all | solution.py:85
  97.7 4.6 %select_convert_fusion.1 = (bf16[1536,384]{1,0:T(8,128)(2,1)}, f32[1536,384]{1,0:T(8,128)}) fusion(f32[1536,384]{1,0:T(8,128)} %fusion.79, pred[]{:T(512)S(6)} %eq.9, bf16[512,1536]{1,0:T(8,128)(2,1)S(1)} %multiply_convert_fusion, bf16[512,384]{0,1:T(8,128)(2,1)S(1)} %collective-permute-done.6), kind=kOutput, calls=%fused_computation.36 | convolution fusion | flops 604569600 | bytes 7864321 | tf_op jit(solution)/shard_map/dot_general | solution.py:23
  105.2 8.4 %all-to-all-done.1 = bf16[4,8,48,384]{3,2,1,0:T(8,128)(2,1)} async-done(((bf16[4,8,48,384]{3,2,1,0:T(8,128)(2,1)}), bf16[4,8,48,384]{3,2,1,0:T(8,128)(2,1)}, u32[]{:S(2)}, u32[]{:S(2)}) %all-to-all-start.1) | async-done | bytes 1179680 | tf_op jit(solution)/shard_map/all_to_all | solution.py:85
  113.6 4.3 %all-to-all-start = ((bf16[4,8,48,384]{3,2,1,0:T(8,128)(2,1)}), bf16[4,8,48,384]{3,2,1,0:T(8,128)(2,1)}, u32[]{:S(2)}, u32[]{:S(2)}) async-start(bf16[4,8,48,384]{3,2,1,0:T(8,128)(2,1)} %bitcast.100), calls=%async_computation | async-start | bytes 2359296 | tf_op jit(solution)/shard_map/all_to_all | solution.py:85
  119.3 2.3 %add_convert_fusion.1 = bf16[1536,384]{1,0:T(8,128)(2,1)S(1)} fusion(bf16[1536,384]{1,0:T(8,128)(2,1)} %collective-permute-done.11, f32[1536,384]{1,0:T(8,128)S(1)} %copy-done.4, f32[1536,384]{1,0:T(8,128)} %get-tuple-element.18, pred[]{:T(512)S(6)} %eq.9), kind=kLoop, calls=%fused_computation.33 | loop fusion | flops 2359296 | bytes 7077889 | tf_op jit(solution)/shard_map/convert_element_type | solution.py:108
  121.7 2.4 %reduce_sum.72 = bf16[8,48,384]{2,1,0:T(8,128)(2,1)} reduce(bf16[4,8,48,384]{3,2,1,0:T(8,128)(2,1)} %all-to-all-done.1, bf16[]{:T(256)} %constant.65.clone.1), dimensions={0}, to_apply=%region_3.4 | reduce | flops 442368 | bytes 1474562 | tf_op jit(solution)/shard_map/reduce_sum | solution.py:86
  124.1 8.7 %all-to-all-done = bf16[4,8,48,384]{3,2,1,0:T(8,128)(2,1)} async-done(((bf16[4,8,48,384]{3,2,1,0:T(8,128)(2,1)}), bf16[4,8,48,384]{3,2,1,0:T(8,128)(2,1)}, u32[]{:S(2)}, u32[]{:S(2)}) %all-to-all-start) | async-done | bytes 1179680 | tf_op jit(solution)/shard_map/all_to_all | solution.py:85
  132.8 2.2 %reduce_sum.71 = bf16[8,48,384]{2,1,0:T(8,128)(2,1)} reduce(bf16[4,8,48,384]{3,2,1,0:T(8,128)(2,1)} %all-to-all-done, bf16[]{:T(256)} %constant.65.clone.1), dimensions={0}, to_apply=%region_2.3 | reduce | flops 442368 | bytes 1474562 | tf_op jit(solution)/shard_map/reduce_sum | solution.py:86
  136.9 4.7 %all-to-all-start.2 = ((bf16[16,48,384]{2,1,0:T(8,128)(2,1)}), bf16[16,48,384]{2,1,0:T(8,128)(2,1)}, u32[]{:S(2)}, u32[]{:S(2)}) async-start(bf16[16,48,384]{2,1,0:T(8,128)(2,1)} %bitcast.110), calls=%async_computation.2 | async-start | bytes 1179648 | tf_op jit(solution)/shard_map/all_to_all | solution.py:88
  141.6 3.4 %add_convert_fusion.2 = bf16[1536,384]{1,0:T(8,128)(2,1)} fusion(bf16[1536,384]{1,0:T(8,128)(2,1)} %collective-permute-done.10, f32[1536,384]{1,0:T(8,128)S(1)} %copy-done, f32[1536,384]{1,0:T(8,128)} %get-tuple-element.20, pred[]{:T(512)S(6)} %eq.9), kind=kLoop, calls=%fused_computation.35 | loop fusion | flops 2359296 | bytes 7077889 | tf_op jit(solution)/shard_map/convert_element_type | solution.py:108
  151.4 7.9 %all-to-all-start.3 = ((bf16[64,160,128]{2,1,0:T(8,128)(2,1)}), bf16[64,160,128]{2,1,0:T(8,128)(2,1)}, u32[]{:S(2)}, u32[]{:S(2)}) async-start(bf16[64,160,128]{2,1,0:T(8,128)(2,1)} %fusion.15), calls=%async_computation.3 | async-start | bytes 5242880 | tf_op jit(solution)/shard_map/all_to_all | solution.py:115
  159.3 2.5 %convert_add_fusion = f32[512,1536]{1,0:T(8,128)S(1)} fusion(bf16[1,512,1536]{2,1,0:T(8,128)(2,1)S(1)} %copy-done.6, bf16[768,1536]{1,0:T(8,128)(2,1)} %param.8, f32[512,384]{0,1:T(8,128)S(1)} %copy-done.13, bf16[512,384]{0,1:T(8,128)(2,1)S(1)} %copy-done.26), kind=kOutput, calls=%fused_computation.3 | convolution fusion | flops 607715328 | bytes 7077888 | tf_op jit(solution)/shard_map/dot_general | solution.py:19
  161.9 2.3 %fusion.14 = bf16[1,512,1536]{2,1,0:T(8,128)(2,1)} fusion(f32[512,1536]{1,0:T(8,128)S(1)} %convert_add_fusion, bf16[768,1536]{1,0:T(8,128)(2,1)S(1)} %copy-done.18, f32[512,384]{0,1:T(8,128)S(1)} %copy-done.15, bf16[512,384]{0,1:T(8,128)(2,1)S(1)} %copy-done.24), kind=kOutput, calls=%fused_computation.30 | convolution fusion | flops 607715328 | bytes 7077888 | tf_op jit(solution)/shard_map/dot_general | solution.py:19
  168.2 21.6 %all-to-all-done.3 = bf16[64,160,128]{2,1,0:T(8,128)(2,1)} async-done(((bf16[64,160,128]{2,1,0:T(8,128)(2,1)}), bf16[64,160,128]{2,1,0:T(8,128)(2,1)}, u32[]{:S(2)}, u32[]{:S(2)}) %all-to-all-start.3) | async-done | bytes 2621472 | tf_op jit(solution)/shard_map/all_to_all | solution.py:115
  192.0 11.3 %all-gather = f32[1184,128]{1,0:T(8,128)S(1)} all-gather(f32[296,128]{1,0:T(8,128)S(1)} %select_maximum_fusion), channel_id=2, replica_groups=mesh['xh'=2,'y'=4,'z'=4,'xl'=2,'core'=2] {'xl','core'}, dimensions={0}, use_global_device_ids=true | all-gather | bytes 757760 | tf_op jit(solution)/shard_map/all_gather | solution.py:121
  (128 shorter events, 47.4 us)
Async XLA Ops:
  8.2 6.1 %copy-start.19 = (bf16[1536,768]{1,0:T(8,128)(2,1)}, bf16[1536,768]{1,0:T(8,128)(2,1)S(1)}, u32[]{:S(2)}) copy-start(bf16[1536,768]{1,0:T(8,128)(2,1)S(1)} %get-tuple-element.7) | copy-start | bytes 7077892
  8.3 12.9 %copy-start.21 = (bf16[1536,768]{1,0:T(8,128)(2,1)}, bf16[1536,768]{1,0:T(8,128)(2,1)S(1)}, u32[]{:S(2)}) copy-start(bf16[1536,768]{1,0:T(8,128)(2,1)S(1)} %get-tuple-element.9) | copy-start | bytes 7077892
  9.1 12.0 %collective-permute-start.2 = (bf16[512,384]{0,1:T(8,128)(2,1)S(1)}, bf16[512,384]{0,1:T(8,128)(2,1)S(1)}, u32[]{:S(2)}, u32[]{:S(2)}) collective-permute-start(bf16[512,384]{0,1:T(8,128)(2,1)S(1)} %convolution_convert_fusion), channel_id=1, source_target_pairs={{0,64},{64,0},{1,65},{65,1},{2,66},{66,2},{3,67},{67,3},{4,68},{68... | collective-permute-start | bytes 1179656 | tf_op jit(solution)/shard_map/ppermute | solution.py:35
  14.3 15.3 %collective-permute-start = (bf16[512,384]{0,1:T(8,128)(2,1)}, bf16[512,384]{0,1:T(8,128)(2,1)}, u32[]{:S(2)}, u32[]{:S(2)}) collective-permute-start(bf16[512,384]{0,1:T(8,128)(2,1)} %convolution_convert_fusion.1), channel_id=1, source_target_pairs={{0,64},{64,0},{1,65},{65,1},{2,66},{66,2},{3,67},{67,3},{4,68},{68... | collective-permute-start | bytes 1179656 | tf_op jit(solution)/shard_map/ppermute | solution.py:35
  22.7 12.5 %collective-permute-start.3 = (bf16[512,384]{0,1:T(8,128)(2,1)}, bf16[512,384]{0,1:T(8,128)(2,1)S(1)}, u32[]{:S(2)}, u32[]{:S(2)}) collective-permute-start(bf16[512,384]{0,1:T(8,128)(2,1)} %add_convert_fusion.5), channel_id=1, source_target_pairs={{0,32},{16,48},{32,0},{48,16},{1,33},{17,49},{33,1},{49,17},{2,34}... | collective-permute-start | bytes 1179656 | tf_op jit(solution)/shard_map/ppermute | solution.py:39
  27.8 7.4 %copy-start.7 = (bf16[1,512,1536]{2,1,0:T(8,128)(2,1)S(1)}, bf16[1,512,1536]{2,1,0:T(8,128)(2,1)}, u32[]{:S(2)}) copy-start(bf16[1,512,1536]{2,1,0:T(8,128)(2,1)} %param.9) | copy-start | bytes 4718596
  27.8 7.4 %copy-start.14 = (f32[512,384]{0,1:T(8,128)S(1)}, f32[512,384]{0,1:T(8,128)}, u32[]{:S(2)}) copy-start(f32[512,384]{0,1:T(8,128)} %fusion.26) | copy-start | bytes 2359300
  31.8 11.1 %collective-permute-start.1 = (bf16[512,384]{0,1:T(8,128)(2,1)S(1)}, bf16[512,384]{0,1:T(8,128)(2,1)S(1)}, u32[]{:S(2)}, u32[]{:S(2)}) collective-permute-start(bf16[512,384]{0,1:T(8,128)(2,1)S(1)} %add_convert_fusion.6), channel_id=1, source_target_pairs={{0,32},{16,48},{32,0},{48,16},{1,33},{17,49},{33,1},{49,17},{2,34}... | collective-permute-start | bytes 1179656 | tf_op jit(solution)/shard_map/ppermute | solution.py:39
  35.2 13.0 %copy-start.23 = (bf16[512,384]{0,1:T(8,128)(2,1)}, bf16[512,384]{0,1:T(8,128)(2,1)S(1)}, u32[]{:S(2)}) copy-start(bf16[512,384]{0,1:T(8,128)(2,1)S(1)} %collective-permute-done.3) | copy-start | bytes 1179652
  37.8 22.8 %collective-permute-start.5 = (bf16[512,384]{0,1:T(8,128)(2,1)S(1)}, bf16[512,384]{0,1:T(8,128)(2,1)S(1)}, u32[]{:S(2)}, u32[]{:S(2)}) collective-permute-start(bf16[512,384]{0,1:T(8,128)(2,1)S(1)} %fusion.60), channel_id=1, source_target_pairs={{0,32},{16,48},{32,0},{48,16},{1,33},{17,49},{33,1},{49,17},{2,34}... | collective-permute-start | bytes 1179656 | tf_op jit(solution)/shard_map/ppermute | solution.py:39
  42.9 11.4 %copy-start.25 = (bf16[512,384]{0,1:T(8,128)(2,1)}, bf16[512,384]{0,1:T(8,128)(2,1)S(1)}, u32[]{:S(2)}) copy-start(bf16[512,384]{0,1:T(8,128)(2,1)S(1)} %collective-permute-done.1) | copy-start | bytes 1179652
  44.0 19.4 %collective-permute-start.4 = (bf16[512,384]{0,1:T(8,128)(2,1)S(1)}, bf16[512,384]{0,1:T(8,128)(2,1)S(1)}, u32[]{:S(2)}, u32[]{:S(2)}) collective-permute-start(bf16[512,384]{0,1:T(8,128)(2,1)S(1)} %fusion.48), channel_id=1, source_target_pairs={{0,32},{16,48},{32,0},{48,16},{1,33},{17,49},{33,1},{49,17},{2,34}... | collective-permute-start | bytes 1179656 | tf_op jit(solution)/shard_map/ppermute | solution.py:39
  49.3 41.8 %collective-permute-start.9 = (bf16[1536,384]{1,0:T(8,128)(2,1)S(1)}, bf16[1536,384]{1,0:T(8,128)(2,1)S(1)}, u32[]{:S(2)}, u32[]{:S(2)}) collective-permute-start(bf16[1536,384]{1,0:T(8,128)(2,1)S(1)} %get-tuple-element.21), channel_id=1, source_target_pairs={{0,1},{1,0},{2,3},{3,2},{4,5},{5,4},{6,7},{7,6},{8,9},{9,8},{10,11... | collective-permute-start | bytes 3538952 | tf_op jit(solution)/shard_map/ppermute | solution.py:43
  57.2 6.5 %copy-start.22 = (bf16[1536,768]{1,0:T(8,128)(2,1)S(1)}, bf16[1536,768]{1,0:T(8,128)(2,1)}, u32[]{:S(2)}) copy-start(bf16[1536,768]{1,0:T(8,128)(2,1)} %copy-done.21) | copy-start | bytes 7077892
  57.2 45.2 %collective-permute-start.8 = (bf16[1536,384]{1,0:T(8,128)(2,1)}, bf16[1536,384]{1,0:T(8,128)(2,1)}, u32[]{:S(2)}, u32[]{:S(2)}) collective-permute-start(bf16[1536,384]{1,0:T(8,128)(2,1)} %get-tuple-element.23), channel_id=1, source_target_pairs={{0,1},{1,0},{2,3},{3,2},{4,5},{5,4},{6,7},{7,6},{8,9},{9,8},{10,11... | collective-permute-start | bytes 3538952 | tf_op jit(solution)/shard_map/ppermute | solution.py:43
  60.6 12.0 %collective-permute-start.7 = (bf16[512,384]{0,1:T(8,128)(2,1)S(1)}, bf16[512,384]{0,1:T(8,128)(2,1)S(1)}, u32[]{:S(2)}, u32[]{:S(2)}) collective-permute-start(bf16[512,384]{0,1:T(8,128)(2,1)S(1)} %collective-permute-done.5), channel_id=1, source_target_pairs={{0,64},{64,0},{1,65},{65,1},{2,66},{66,2},{3,67},{67,3},{4,68},{68... | collective-permute-start | bytes 1179656 | tf_op jit(solution)/shard_map/ppermute | solution.py:35
  63.5 17.6 %collective-permute-start.6 = (bf16[512,384]{0,1:T(8,128)(2,1)S(1)}, bf16[512,384]{0,1:T(8,128)(2,1)S(1)}, u32[]{:S(2)}, u32[]{:S(2)}) collective-permute-start(bf16[512,384]{0,1:T(8,128)(2,1)S(1)} %collective-permute-done.4), channel_id=1, source_target_pairs={{0,64},{64,0},{1,65},{65,1},{2,66},{66,2},{3,67},{67,3},{4,68},{68... | collective-permute-start | bytes 1179656 | tf_op jit(solution)/shard_map/ppermute | solution.py:35
  66.2 22.2 %copy-start.3 = (f32[1536,384]{1,0:T(8,128)}, f32[1536,384]{1,0:T(8,128)S(1)}, u32[]{:S(2)}) copy-start(f32[1536,384]{1,0:T(8,128)S(1)} %fusion.80) | copy-start | bytes 7077892
  66.2 14.9 %copy-start.20 = (bf16[1536,768]{1,0:T(8,128)(2,1)S(1)}, bf16[1536,768]{1,0:T(8,128)(2,1)}, u32[]{:S(2)}) copy-start(bf16[1536,768]{1,0:T(8,128)(2,1)} %copy-done.19) | copy-start | bytes 7077892
  66.2 14.9 %copy-start.28 = (f32[1536]{0:T(1024)S(1)}, f32[1536]{0:T(1024)}, u32[]{:S(2)}) copy-start(f32[1536]{0:T(1024)} %param.6) | copy-start | bytes 18436
  87.2 30.6 %collective-permute-start.12 = (f32[1536]{0:T(1024)}, f32[1536]{0:T(1024)}, u32[]{:S(2)}, u32[]{:S(2)}) collective-permute-start(f32[1536]{0:T(1024)} %get-tuple-element.5), channel_id=1, source_target_pairs={{0,1},{1,0},{2,3},{3,2},{4,5},{5,4},{6,7},{7,6},{8,9},{9,8},{10,11... | collective-permute-start | bytes 18440 | tf_op jit(solution)/shard_map/ppermute | solution.py:43
  91.2 28.1 %collective-permute-start.11 = (bf16[1536,384]{1,0:T(8,128)(2,1)}, bf16[1536,384]{1,0:T(8,128)(2,1)}, u32[]{:S(2)}, u32[]{:S(2)}) collective-permute-start(bf16[1536,384]{1,0:T(8,128)(2,1)} %get-tuple-element.17), channel_id=1, source_target_pairs={{0,1},{1,0},{2,3},{3,2},{4,5},{5,4},{6,7},{7,6},{8,9},{9,8},{10,11... | collective-permute-start | bytes 3538952 | tf_op jit(solution)/shard_map/ppermute | solution.py:43
  92.7 20.9 %all-to-all-start.1 = ((bf16[4,8,48,384]{3,2,1,0:T(8,128)(2,1)}), bf16[4,8,48,384]{3,2,1,0:T(8,128)(2,1)}, u32[]{:S(2)}, u32[]{:S(2)}) async-start(bf16[4,8,48,384]{3,2,1,0:T(8,128)(2,1)} %bitcast.99), calls=%async_computation.1 | async-start | bytes 2359296 | tf_op jit(solution)/shard_map/all_to_all | solution.py:85
  102.3 39.3 %collective-permute-start.10 = (bf16[1536,384]{1,0:T(8,128)(2,1)}, bf16[1536,384]{1,0:T(8,128)(2,1)}, u32[]{:S(2)}, u32[]{:S(2)}) collective-permute-start(bf16[1536,384]{1,0:T(8,128)(2,1)} %get-tuple-element.19), channel_id=1, source_target_pairs={{0,1},{1,0},{2,3},{3,2},{4,5},{5,4},{6,7},{7,6},{8,9},{9,8},{10,11... | collective-permute-start | bytes 3538952 | tf_op jit(solution)/shard_map/ppermute | solution.py:43
  104.0 15.4 %copy-start.4 = (f32[1536,384]{1,0:T(8,128)S(1)}, f32[1536,384]{1,0:T(8,128)}, u32[]{:S(2)}) copy-start(f32[1536,384]{1,0:T(8,128)} %copy-done.3) | copy-start | bytes 7077892
  113.6 19.2 %all-to-all-start = ((bf16[4,8,48,384]{3,2,1,0:T(8,128)(2,1)}), bf16[4,8,48,384]{3,2,1,0:T(8,128)(2,1)}, u32[]{:S(2)}, u32[]{:S(2)}) async-start(bf16[4,8,48,384]{3,2,1,0:T(8,128)(2,1)} %bitcast.100), calls=%async_computation | async-start | bytes 2359296 | tf_op jit(solution)/shard_map/all_to_all | solution.py:85
  121.7 20.0 %copy-start = (f32[1536,384]{1,0:T(8,128)S(1)}, f32[1536,384]{1,0:T(8,128)}, u32[]{:S(2)}) copy-start(f32[1536,384]{1,0:T(8,128)} %fusion.79) | copy-start | bytes 7077892
  136.9 14.4 %all-to-all-start.2 = ((bf16[16,48,384]{2,1,0:T(8,128)(2,1)}), bf16[16,48,384]{2,1,0:T(8,128)(2,1)}, u32[]{:S(2)}, u32[]{:S(2)}) async-start(bf16[16,48,384]{2,1,0:T(8,128)(2,1)} %bitcast.110), calls=%async_computation.2 | async-start | bytes 1179648 | tf_op jit(solution)/shard_map/all_to_all | solution.py:88
  151.4 7.9 %copy-start.6 = (bf16[1,512,1536]{2,1,0:T(8,128)(2,1)S(1)}, bf16[1,512,1536]{2,1,0:T(8,128)(2,1)}, u32[]{:S(2)}) copy-start(bf16[1,512,1536]{2,1,0:T(8,128)(2,1)} %param.5) | copy-start | bytes 4718596
  151.4 7.9 %copy-start.13 = (f32[512,384]{0,1:T(8,128)S(1)}, f32[512,384]{0,1:T(8,128)}, u32[]{:S(2)}) copy-start(f32[512,384]{0,1:T(8,128)} %fusion.31) | copy-start | bytes 2359300
  151.4 7.9 %copy-start.26 = (bf16[512,384]{0,1:T(8,128)(2,1)S(1)}, bf16[512,384]{0,1:T(8,128)(2,1)}, u32[]{:S(2)}) copy-start(bf16[512,384]{0,1:T(8,128)(2,1)} %copy-done.25) | copy-start | bytes 1179652
  151.4 38.4 %all-to-all-start.3 = ((bf16[64,160,128]{2,1,0:T(8,128)(2,1)}), bf16[64,160,128]{2,1,0:T(8,128)(2,1)}, u32[]{:S(2)}, u32[]{:S(2)}) async-start(bf16[64,160,128]{2,1,0:T(8,128)(2,1)} %fusion.15), calls=%async_computation.3 | async-start | bytes 5242880 | tf_op jit(solution)/shard_map/all_to_all | solution.py:115
  (14 other events, 44.1 us)

commit v3 on v1

v3 whole, which is shorter than its diff:
```python
import functools

import jax
import jax.numpy as jnp
from jax import lax
from jax.experimental import pallas as pl
from jax.experimental.pallas import tpu as pltpu
from jax.sharding import Mesh, PartitionSpec as P

F32 = jnp.float32
BF16 = jnp.bfloat16
PLANE = ("xh", "yh", "yl", "xl")
GROUP = ("xh", "yh")
Q = 128
N = 512
C = 1536
H = 768
HALF = 384
SMEM = pl.BlockSpec(memory_space=pltpu.SMEM)
ANY = pl.BlockSpec(memory_space=pl.ANY)
VMEM = pl.BlockSpec(memory_space=pltpu.VMEM)


def dot(left, right):
    return jnp.dot(left, right, preferred_element_type=F32)


def contract_cols(left, right):
    return lax.dot_general(
        left, right, (((1,), (1,)), ((), ())), preferred_element_type=F32
    )


def gelu_both(value):
    line = 0.7978845608028654 * value
    bent = line * (1.0 + 0.044715 * (value * value))
    tanh = jnp.tanh(bent)
    half = 0.5 + 0.5 * tanh
    return value * half, half + (1.0 - tanh * tanh) * (1.5 * bent - line)


def params(mebibytes):
    return pltpu.CompilerParams(vmem_limit_bytes=mebibytes * 1024 * 1024)


def cost(flops, size):
    return pl.CostEstimate(flops=flops, bytes_accessed=size, transcendentals=0)


def taps_in(odd_ref, weights_ref, held, sems):
    odd = odd_ref[0]
    return [
        pltpu.make_async_copy(weights_ref.at[tap], held.at[i], sems.at[i])
        for i, tap in enumerate((2 * odd, 1, 2 - 2 * odd))
    ]


def pack_kernel(
    me_ref, stream_ref, cotan_ref, point_ref, p0, p1, p2, p3, turned_ref,
    rows_in, turned, point, grads, in_sems, point_sem, out_sems,
):
    me = me_ref[0]
    weights = pltpu.make_async_copy(point_ref, point, point_sem)
    cotans, streams = [], []
    for k in range(4):
        rows = pl.ds(pl.multiple_of(lax.bitwise_xor(me, k) * Q, Q), Q)
        at = pl.ds(k * Q, Q)
        cotans.append(pltpu.make_async_copy(cotan_ref.at[rows], turned.at[at], in_sems.at[k]))
        streams.append(pltpu.make_async_copy(stream_ref.at[rows], rows_in.at[at], in_sems.at[4 + k]))
    for copy in cotans + [weights] + streams:
        copy.start()
    for copy in cotans:
        copy.wait()
    outs = [pltpu.make_async_copy(turned, turned_ref, out_sems.at[8])]
    outs[0].start()
    weights.wait()
    grads[...] = contract_cols(turned[...], point[...]).astype(BF16)
    for k, out in enumerate((p0, p1, p2, p3)):
        at = pl.ds(k * Q, Q)
        streams[k].wait()
        outs.append(pltpu.make_async_copy(rows_in.at[at], out.at[:, pl.ds(0, C)], out_sems.at[k]))
        outs.append(pltpu.make_async_copy(grads.at[at], out.at[:, pl.ds(C, H)], out_sems.at[4 + k]))
    for copy in outs[1:]:
        copy.start()
    for copy in outs:
        copy.wait()


def pack(me, stream, cotan, point_kernel):
    shape = jax.ShapeDtypeStruct
    return pl.pallas_call(
        pack_kernel,
        in_specs=[SMEM] + [ANY] * 3,
        out_specs=[ANY] * 5,
        out_shape=[shape((Q, C + H), BF16)] * 4 + [shape((N, C), BF16)],
        scratch_shapes=[
            pltpu.VMEM((N, C), BF16),
            pltpu.VMEM((N, C), BF16),
            pltpu.VMEM((H, C), BF16),
            pltpu.VMEM((N, H), BF16),
            pltpu.SemaphoreType.DMA((8,)),
            pltpu.SemaphoreType.DMA,
            pltpu.SemaphoreType.DMA((9,)),
        ],
        compiler_params=params(56),
        cost_estimate=cost(2 * N * C * H, 8_000_000),
        name="pack",
    )(me, stream, cotan, point_kernel)


def forward_kernel(
    odd_ref, core_ref, p0, p1, p2, p3, gain_ref, weights_ref,
    act_out, slope_out, inv_out, m0, m1, m2, m3, all_ref, kept_ref, away_ref,
    packed, ring, held, slope_in, inv_in, sems, in_sems, out_sems,
):
    ins = [
        pltpu.make_async_copy(source, packed.at[k], in_sems.at[k])
        for k, source in enumerate((p0, p1, p2, p3))
    ]
    copies = taps_in(odd_ref, weights_ref, held, sems)
    for copy in ins + copies:
        copy.start()
    core = core_ref[0]
    step = 32
    for k in range(4):
        ins[k].wait()

        def some(i, carry, k=k):
            at = pl.ds(pl.multiple_of(i * step, step), step)
            rows = packed[k, at, :C].astype(F32)
            inv = lax.rsqrt(jnp.mean(rows * rows, axis=-1, keepdims=True) + 1e-06)
            act, slope = gelu_both(rows * inv * gain_ref[...])
            here = pl.ds(pl.multiple_of(k * Q + i * step, step), step)
            slope_in[here, :] = slope
            inv_in[here, :] = jnp.broadcast_to(inv, (step, 128))
            ring[pl.ds(pl.multiple_of((k + 1) * Q + i * step, step), step), :] = act.astype(BF16)
            return carry

        lax.fori_loop(0, Q // step, some, 0)
    outs = [
        pltpu.make_async_copy(ring.at[pl.ds(Q, N)], act_out, out_sems.at[0]),
        pltpu.make_async_copy(slope_in, slope_out, out_sems.at[1]),
        pltpu.make_async_copy(inv_in, inv_out, out_sems.at[2]),
    ]
    for copy in outs:
        copy.start()
    ring[:Q] = ring[4 * Q:5 * Q]
    ring[5 * Q:] = ring[Q:2 * Q]
    for copy in copies:
        copy.wait()
    for n in range(3):
        cols = slice(n * 256, (n + 1) * 256)
        pre = dot(ring[Q:5 * Q], held[1, :, cols])
        pre = pre + dot(ring[:4 * Q], held[0, :, cols])
        pre = pre + dot(ring[2 * Q:], held[2, :, cols])
        mid, slope = gelu_both(pre)
        for k, out in enumerate((m0, m1, m2, m3)):
            at = slice(k * Q, (k + 1) * Q)
            out[:, cols] = mid[at].astype(BF16)
            grad = packed[k, :, C + n * 256:C + n * 256 + 256].astype(F32)
            all_ref[at, cols] = (grad * slope[at]).astype(BF16)
    low, high = all_ref[:, :HALF], all_ref[:, HALF:]
    kept_ref[...] = jnp.where(core == 0, low, high)
    away_ref[...] = jnp.where(core == 0, high, low)
    for copy in outs:
        copy.wait()


def forward(odd, core, pieces, gain, weights):
    shape = jax.ShapeDtypeStruct
    return pl.pallas_call(
        forward_kernel,
        in_specs=[SMEM] * 2 + [ANY] * 4 + [VMEM, ANY],
        out_specs=[ANY] * 3 + [VMEM] * 7,
        out_shape=[shape((N, C), BF16), shape((N, C), F32), shape((N, 128), F32)]
        + [shape((Q, H), BF16)] * 4
        + [shape((N, H), BF16), shape((N, HALF), BF16), shape((N, HALF), BF16)],
        scratch_shapes=[
            pltpu.VMEM((4, Q, C + H), BF16),
            pltpu.VMEM((6 * Q, C), BF16),
            pltpu.VMEM((3, C, H), BF16),
            pltpu.VMEM((N, C), F32),
            pltpu.VMEM((N, 128), F32),
            pltpu.SemaphoreType.DMA((3,)),
            pltpu.SemaphoreType.DMA((4,)),
            pltpu.SemaphoreType.DMA((3,)),
        ],
        compiler_params=params(56),
        cost_estimate=cost(6 * N * C * H, 20_000_000),
        name="forward",
    )(odd, core, *pieces, gain, weights)


def backward_kernel(
    odd_ref, grad_ref, p0, p1, p2, p3, gain_ref, slope_hbm, inv_hbm, weights_ref,
    b0, b1, b2, b3, share_ref,
    ring, held, total, slope_ref, inv_ref, rows_in, sems, in_sems,
):
    copies = taps_in(odd_ref, weights_ref, held, sems)
    copies = [copies[1], copies[0], copies[2]]
    for copy in copies:
        copy.start()
    ins = [
        pltpu.make_async_copy(slope_hbm, slope_ref, in_sems.at[0]),
        pltpu.make_async_copy(inv_hbm, inv_ref, in_sems.at[1]),
    ] + [
        pltpu.make_async_copy(source.at[:, pl.ds(0, C)], rows_in.at[k], in_sems.at[2 + k])
        for k, source in enumerate((p0, p1, p2, p3))
    ]
    for copy in ins:
        copy.start()
    ring[Q:5 * Q] = grad_ref[...]
    ring[:Q] = grad_ref[3 * Q:]
    ring[5 * Q:] = grad_ref[:Q]
    for i, copy in enumerate(copies):
        copy.wait()
        tap = (1, 0, 2)[i]
        first = (1, 2, 0)[i] * Q
        for n in range(6):
            cols = slice(n * 256, (n + 1) * 256)
            value = contract_cols(ring[first:first + N], held[tap, cols])
            total[:, cols] = value if i == 0 else total[:, cols] + value
    for copy in ins:
        copy.wait()
    step = 32
    share = jnp.zeros((8, C), F32)
    for k, out in enumerate((b0, b1, b2, b3)):

        def some(i, share, k=k, out=out):
            at = pl.ds(pl.multiple_of(i * step, step), step)
            here = pl.ds(pl.multiple_of(k * Q + i * step, step), step)
            inv = inv_ref[here, :1]
            hat = rows_in[k, at, :].astype(F32) * inv
            norm_grad = total[here, :] * slope_ref[here, :]
            product = norm_grad * hat
            mean = jnp.mean(product * gain_ref[...], axis=-1, keepdims=True)
            out[at, :] = ((norm_grad * gain_ref[...] - hat * mean) * inv).astype(BF16)
            return share + product.reshape(step // 8, 8, C).sum(0)

        share = lax.fori_loop(0, Q // step, some, share)
    share_ref[...] = jnp.sum(share, axis=0, keepdims=True)


def backward(odd, grads, pieces, gain, slope, inv, weights):
    shape = jax.ShapeDtypeStruct
    return pl.pallas_call(
        backward_kernel,
        in_specs=[SMEM, VMEM] + [ANY] * 4 + [VMEM] + [ANY] * 3,
        out_specs=[VMEM] * 5,
        out_shape=[shape((Q, C), BF16)] * 4 + [shape((1, C), F32)],
        scratch_shapes=[
            pltpu.VMEM((6 * Q, H), BF16),
            pltpu.VMEM((3, C, H), BF16),
            pltpu.VMEM((N, C), F32),
            pltpu.VMEM((N, C), F32),
            pltpu.VMEM((N, 128), F32),
            pltpu.VMEM((4, Q, C), BF16),
            pltpu.SemaphoreType.DMA((3,)),
            pltpu.SemaphoreType.DMA((6,)),
        ],
        compiler_params=params(56),
        cost_estimate=cost(6 * N * C * H, 20_000_000),
        name="backward",
    )(odd, grads, *pieces, gain, slope, inv, weights)


def kernel_share_kernel(odd_ref, own_ref, other_ref, kept_ref, came_ref, out_ref, right, ring):
    @pl.when(pl.program_id(0) == 0)
    def _():
        odd = odd_ref[0]
        for i, source in enumerate((kept_ref, came_ref)):
            ring[Q:5 * Q] = source[...]
            ring[:Q] = source[3 * Q:]
            ring[5 * Q:] = source[:Q]
            rows = slice(i * N, (i + 1) * N)
            near = pl.multiple_of(jnp.where(odd == 0, 2 * Q, 0), Q)
            far = pl.multiple_of(jnp.where(odd == 0, 0, 2 * Q), Q)
            right[rows, :HALF] = ring[pl.ds(near, N), :]
            right[rows, HALF:2 * HALF] = source[...]
            right[rows, 2 * HALF:] = ring[pl.ds(far, N), :]

    value = dot(own_ref[...], right[:N]) + dot(other_ref[...], right[N:])
    value = value.astype(BF16)
    for t in range(3):
        for b in range(3):
            at = t * HALF + b * 128
            part = value[:, at:at + 128].reshape(2, 4, 48, 128)
            for z in range(4):
                out_ref[z, :, t, 48 * b:48 * b + 48, :] = part[:, z]


def kernel_shares(odd, own, other, kept, came):
    whole = pl.BlockSpec((N, HALF), lambda i: (0, 0))
    part = pl.BlockSpec((C // 4, N), lambda i: (i, 0))
    return pl.pallas_call(
        kernel_share_kernel,
        grid=(4,),
        in_specs=[SMEM, part, part, whole, whole],
        out_specs=pl.BlockSpec((4, 2, 3, 144, 128), lambda i: (0, i, 0, 0, 0)),
        out_shape=jax.ShapeDtypeStruct((4, 8, 3, 144, 128), BF16),
        scratch_shapes=[pltpu.VMEM((2 * N, 3 * HALF), BF16), pltpu.VMEM((6 * Q, HALF), BF16)],
        compiler_params=params(56),
        cost_estimate=cost(6 * N * C * H, 10_000_000),
        name="kernel_shares",
    )(odd, own, other, kept, came)


def point_share_kernel(own_ref, other_ref, kept_ref, came_ref, gain_ref, out_ref):
    out_ref[:, :, 144:, :] = gain_ref[...]
    value = dot(own_ref[...], kept_ref[...]) + dot(other_ref[...], came_ref[...])
    value = value.astype(BF16)
    for b in range(3):
        part = value[:, b * 128:b * 128 + 128].reshape(2, 4, 48, 128)
        for z in range(4):
            out_ref[z, :, 48 * b:48 * b + 48, :] = part[:, z]


def point_shares(own, other, kept, came, gain):
    whole = pl.BlockSpec((N, HALF), lambda i: (0, 0))
    part = pl.BlockSpec((C // 4, N), lambda i: (i, 0))
    return pl.pallas_call(
        point_share_kernel,
        grid=(4,),
        in_specs=[part, part, whole, whole, pl.BlockSpec((4, 2, 16, 128), lambda i: (0, i, 0, 0))],
        out_specs=pl.BlockSpec((4, 2, 160, 128), lambda i: (0, i, 0, 0)),
        out_shape=jax.ShapeDtypeStruct((4, 8, 160, 128), BF16),
        compiler_params=params(56),
        cost_estimate=cost(2 * N * C * H, 6_000_000),
        name="point_shares",
    )(own, other, kept, came, gain)


def swap_core(value):
    return lax.ppermute(value, "core", [(0, 1), (1, 0)])


def exchange(pieces):
    return [pieces[0]] + [
        lax.ppermute(pieces[k], GROUP, [(i, i ^ k) for i in range(4)]) for k in (1, 2, 3)
    ]


def restored(pieces, me):
    pairs = []
    for a, b in (pieces[:2], pieces[2:]):
        turn = (me & 1) == 1
        pairs.append(jnp.stack([jnp.where(turn, b, a), jnp.where(turn, a, b)]))
    low, high = pairs
    turn = (me & 2) == 2
    out = jnp.concatenate([jnp.where(turn, high, low), jnp.where(turn, low, high)])
    return out.reshape(N, out.shape[2])


def shards(stream, norm_gain_vector, conv_kernel, point_kernel, out_grad):
    core = lax.axis_index("core").astype(jnp.int32)
    odd = lax.axis_index("yh").astype(jnp.int32)
    me = 2 * lax.axis_index("xh") + odd
    core_word, odd_word = core.reshape(1), odd.reshape(1)
    gain_row = norm_gain_vector.reshape(1, C)
    cotan = out_grad[0]

    packed = pack(me.reshape(1), stream[0], cotan, point_kernel)
    pieces = exchange(packed[:4])
    cotan_cols = packed[4].T
    cotan_other = swap_core(cotan_cols)

    act, slope_in, inv, m0, m1, m2, m3, pre_grad, kept, away = forward(
        odd_word, core_word, pieces, gain_row, conv_kernel
    )
    act_cols = act.T
    act_other = swap_core(act_cols)
    came = swap_core(away)
    shares = kernel_shares(odd_word, act_cols, act_other, kept, came)
    shares, pre_grad, *mid = lax.optimization_barrier((shares, pre_grad, m0, m1, m2, m3))
    shares = lax.all_to_all(shares, "z", 0, 0, tiled=True)
    mid = exchange(mid)
    b0, b1, b2, b3, gain = backward(
        odd_word, pre_grad, pieces, gain_row, slope_in, inv, conv_kernel
    )
    gain, *mid = lax.optimization_barrier((gain, *mid))
    back = exchange([b0, b1, b2, b3])

    mid = jnp.concatenate(mid)
    low, high = mid[:, :HALF], mid[:, HALF:]
    mid_kept = jnp.where(core == 0, low, high)
    mid_came = swap_core(jnp.where(core == 0, high, low))
    gain = gain.astype(BF16).reshape(8, 4, 1, 48).transpose(1, 0, 2, 3)
    gain = jnp.pad(gain, ((0, 0), (0, 0), (0, 15), (0, 80)))
    point_part = point_shares(cotan_cols, cotan_other, mid_kept, mid_came, gain)
    shares, point_part = lax.optimization_barrier((shares, point_part))
    point_part = lax.all_to_all(point_part, "z", 0, 0, tiled=True)
    shares = jnp.sum(shares.astype(F32), axis=0).astype(BF16)
    point_part = jnp.sum(point_part.astype(F32), axis=0).astype(BF16)
    first = [shares[:, 0], shares[:, 1], point_part[:, 144:]]
    second = [shares[:, 2], point_part]
    plane = jnp.stack([jnp.concatenate(first, 1), jnp.concatenate(second, 1)], 1)
    plane, *back = lax.optimization_barrier((plane, *back))
    got = lax.all_to_all(plane.reshape(16, 304, 128), PLANE, 0, 0, tiled=True)

    stream_out = dot(mid, point_kernel).reshape(4, Q, C)
    stream_out = restored([stream_out[k] for k in range(4)], me)
    stream_out = (stream[0].astype(F32) + stream_out).astype(BF16)
    stream_grad = (cotan.astype(F32) + restored(back, me).astype(F32)).astype(BF16)

    total = jnp.sum(got.astype(F32), axis=0)[:296]
    whole = lax.all_gather(total, ("xl", "core"))
    gain_grad = whole[0, 288, :48] + whole[1, 288, :48]
    whole = whole[:, :288].reshape(2, 2, 2, 3, 48, 128).transpose(0, 2, 4, 1, 3, 5)
    whole = whole.reshape(4, 48, H)
    kernel_grad = jnp.stack([whole[0], whole[1], whole[2]])
    return (stream_out[None], stream_grad[None], kernel_grad, whole[3].T, gain_grad)


def solution(mesh):
    fine = Mesh(
        mesh.devices.reshape(2, 2, 2, 4, 2, 2), ("xh", "yh", "yl", "z", "xl", "core")
    )
    ctx, rep = ("xh", "yh", "yl", "z"), ("xl", "core")
    placed = (P(rep, ctx, None), P(), P(), P(), P(rep, ctx, None))
    return jax.shard_map(
        shards,
        mesh=fine,
        in_specs=placed,
        out_specs=(
            P(rep, ctx, None),
            P(rep, ctx, None),
            P(None, ctx, None),
            P(None, ctx),
            P(ctx),
        ),
        check_vma=False,
    )
```

time: 209 us -> 177 us (0.85)
  blocking collectives: 53.9 us -> 9.9 us
  Pallas kernels: 0 us -> 43 us
  matrix products: 35.3 us -> 1.38 us
  waiting for transfers between devices: 63.6 us -> 51.1 us
  local copies, waits for them, and re-layouts: 4.12 us -> 14 us
  starting transfers between devices: 33.8 us -> 38.6 us
    unnamed x1 -> x0, blocking collectives: 45.9 us -> none
    pallas_call x0 -> x5, Pallas kernels: none -> 43 us  [the longest x1 12.2 us: backward(): pl.pallas_call(backward_kernel, in_specs=[SMEM, VMEM] + [ANY] * 4 + [VMEM...]
    ppermute x8 -> x13, waiting for transfers between devices: 56.4 us -> 28.3 us  [the longest x9 24.8 us: exchange(): lax.ppermute(pieces[k], GROUP, [(i, i ^ k) for i in range(4)])]
    dot_general x8 -> x0, matrix products: 19.1 us -> none  [the longest x4 11.6 us: contract_cols(): lax.dot_general(left, right, (((1,), (1,)), ((), ())), preferred_element_...]
    all_to_all x2 -> x3, waiting for transfers between devices: 7.21 us -> 22.8 us  [the longest x1 12.7 us: shards(): got = lax.all_to_all(plane.reshape(16, 304, 128), PLANE, 0, 0, tiled=True)]
    dot_general x4 -> x1, matrix products: 16.2 us -> 1.38 us  [dot(): return jnp.dot(left, right, preferred_element_type=F32)]
    ppermute x8 -> x13, starting transfers between devices: 12.3 us -> 22.2 us  [the longest x9 18 us: exchange(): lax.ppermute(pieces[k], GROUP, [(i, i ^ k) for i in range(4)])]
    all_to_all x2 -> x3, starting transfers between devices: 21.4 us -> 16.4 us  [the longest x1 6.85 us: shards(): got = lax.all_to_all(plane.reshape(16, 304, 128), PLANE, 0, 0, tiled=True)]
  transfers between devices with their start and end apart: 10 -> 16, of which waited for: 5 -> 6; matrix products, arithmetic and copies ran while one was open for 18% -> 13% of each run, Pallas kernels for 0% -> 10%
where the time goes in v3:
time: 177 us
  waiting for transfers between devices  51.1 us (29%)
  Pallas kernels  43 us (24%)
  starting transfers between devices  38.6 us (22%)
  other arithmetic  17.7 us (10%)
  local copies, waits for them, and re-layouts  14 us (8%)
  blocking collectives  9.9 us (6%)
    ppermute x9, waiting for transfers between devices, exchange(): lax.ppermute(pieces[k], GROUP, [(i, i ^ k) for i in range(4)])  24.8 us
    ppermute x9, starting transfers between devices, exchange(): lax.ppermute(pieces[k], GROUP, [(i, i ^ k) for i in range(4)])  18 us
    all_to_all x1, waiting for transfers between devices, shards(): got = lax.all_to_all(plane.reshape(16, 304, 128), PLANE, 0, 0, tiled=True)  12.7 us
    pallas_call x1, Pallas kernels, backward(): pl.pallas_call(backward_kernel, in_specs=[SMEM, VMEM] + [ANY] * 4 + [VMEM...  12.2 us
    pallas_call x1, Pallas kernels, forward(): pl.pallas_call(forward_kernel, in_specs=[SMEM] * 2 + [ANY] * 4 + [VMEM, A...  12 us
    all_to_all x1, waiting for transfers between devices, shards(): point_part = lax.all_to_all(point_part, 'z', 0, 0, tiled=True)  10.1 us
    all_gather x1, blocking collectives, shards(): whole = lax.all_gather(total, ('xl', 'core'))  9.9 us
    pallas_call x1, Pallas kernels, kernel_shares(): pl.pallas_call(kernel_share_kernel, grid=(4,), in_specs=[SMEM, part, part...  7.67 us
  transfers between devices with their start and end apart: 16, of which 6 were waited for; matrix products, arithmetic and copies ran while one was open for 13% of the time, Pallas kernels for 10%

profile of v3, /device:TPU:1, one launch (start us, length us, event | category | flops | bytes accessed | tf_op | source)
XLA Modules:
  0.0 176.6 jit_solution(12430472312337669384)
XLA Ops:
  0.6 5.9 %pack.1 = (bf16[128,2304]{1,0:T(8,128)(2,1)}, bf16[128,2304]{1,0:T(8,128)(2,1)}, bf16[128,2304]{1,0:T(8,128)(2,1)}, bf16[128,2304]{1,0:T(8,128)(2,1)}, bf16[512,1536]{1,0:T(8,128)(2,1)}) custom-call(s32[1]{0:T(128)} %bitcast.2.me_ref, bf16[512,1536]{1,0:T(8,128)(2,1)} %bitcast.65, bf16[512,1536]{1,0:T(8,128)(2,1)} %bitcast.66, bf16[768,1536]{1,0:T(8,128)(2,1)} %point_ref.1), custom_call_target="tpu_custom_call" | custom-call | flops 1207959552 | bytes 8000000 | tf_op jit(solution)/shard_map/pack/pallas_call | solution.py:91
  6.6 3.8 %collective-permute-start = (bf16[128,2304]{1,0:T(8,128)(2,1)}, bf16[128,2304]{1,0:T(8,128)(2,1)S(1)}, u32[]{:S(2)}, u32[]{:S(2)}) collective-permute-start(bf16[128,2304]{1,0:T(8,128)(2,1)} %get-tuple-element.44), channel_id=1, source_target_pairs={{0,32},{32,0},{64,96},{96,64},{1,33},{33,1},{65,97},{97,65},{2,34}... | collective-permute-start | bytes 1769480 | tf_op jit(solution)/shard_map/ppermute | solution.py:339
  10.4 2.7 %collective-permute-start.1 = (bf16[128,2304]{1,0:T(8,128)(2,1)}, bf16[128,2304]{1,0:T(8,128)(2,1)S(1)}, u32[]{:S(2)}, u32[]{:S(2)}) collective-permute-start(bf16[128,2304]{1,0:T(8,128)(2,1)} %get-tuple-element.45), channel_id=1, source_target_pairs={{0,64},{32,96},{64,0},{96,32},{1,65},{33,97},{65,1},{97,33},{2,66}... | collective-permute-start | bytes 1769480 | tf_op jit(solution)/shard_map/ppermute | solution.py:339
  13.8 9.6 %collective-permute-done.p1 = bf16[128,2304]{1,0:T(8,128)(2,1)S(1)} collective-permute-done((bf16[128,2304]{1,0:T(8,128)(2,1)}, bf16[128,2304]{1,0:T(8,128)(2,1)S(1)}, u32[]{:S(2)}, u32[]{:S(2)}) %collective-permute-start) | collective-permute-done | bytes 589856 | tf_op jit(solution)/shard_map/ppermute | solution.py:339
  23.4 2.6 %collective-permute-done.1.p2 = bf16[128,2304]{1,0:T(8,128)(2,1)S(1)} collective-permute-done((bf16[128,2304]{1,0:T(8,128)(2,1)}, bf16[128,2304]{1,0:T(8,128)(2,1)S(1)}, u32[]{:S(2)}, u32[]{:S(2)}) %collective-permute-start.1) | collective-permute-done | bytes 589856 | tf_op jit(solution)/shard_map/ppermute | solution.py:339
  26.0 12.6 %collective-permute-done.2.p3 = bf16[128,2304]{1,0:T(8,128)(2,1)S(1)} collective-permute-done((bf16[128,2304]{1,0:T(8,128)(2,1)}, bf16[128,2304]{1,0:T(8,128)(2,1)S(1)}, u32[]{:S(2)}, u32[]{:S(2)}) %collective-permute-start.2) | collective-permute-done | bytes 589856 | tf_op jit(solution)/shard_map/ppermute | solution.py:339
  39.5 12.0 %forward.1 = (bf16[512,1536]{1,0:T(8,128)(2,1)}, f32[512,1536]{1,0:T(8,128)}, f32[512,128]{1,0:T(8,128)}, bf16[128,768]{1,0:T(8,128)(2,1)}, bf16[128,768]{1,0:T(...) custom-call(s32[1]{0:T(128)} %bitcast.odd_ref, ...), custom_call_target="tpu_custom_call" | custom-call | flops 3623878656 | bytes 20000000 | tf_op jit(solution)/shard_map/forward/pallas_call | solution.py:171
  51.4 1.8 %copy.19 = bf16[512,1536]{0,1:T(8,128)(2,1)S(1)} copy(bf16[512,1536]{1,0:T(8,128)(2,1)} %get-tuple-element.47) | data formatting | bytes 3145728 | tf_op jit(solution)/shard_map/forward/pallas_call | solution.py:171
  53.2 1.8 %collective-permute-start.3 = (bf16[1536,512]{1,0:T(8,128)(2,1)S(1)}, bf16[1536,512]{1,0:T(8,128)(2,1)S(1)}, u32[]{:S(2)}, u32[]{:S(2)}) collective-permute-start(bf16[1536,512]{1,0:T(8,128)(2,1)S(1)} %bitcast.71), channel_id=1, source_target_pairs={{0,1},{1,0},{2,3},{3,2},{4,5},{5,4},{6,7},{7,6},{8,9},{9,8},{10,11... | collective-permute-start | bytes 4718600 | tf_op jit(solution)/shard_map/ppermute | solution.py:334
  55.2 3.5 %collective-permute-done.4.came_ref = bf16[512,384]{1,0:T(8,128)(2,1)S(1)} collective-permute-done((bf16[512,384]{1,0:T(8,128)(2,1)S(1)}, bf16[512,384]{1,0:T(8,128)(2,1)S(1)}, u32[]{:S(2)}, u32[]{:S(2)}) %collective-permute-start.4) | collective-permute-done | bytes 393248 | tf_op jit(solution)/shard_map/ppermute | solution.py:334
  60.0 7.7 %kernel_shares.1 = bf16[4,8,3,144,128]{4,3,2,1,0:T(8,128)(2,1)} custom-call(s32[1]{0:T(128)} %bitcast.odd_ref, bf16[1536,512]{1,0:T(8,128)(2,1)} %bitcast.72, bf16[1536,512]{1,0:T(8,128)(2,1)} %copy-done.11, bf16[512,384]{1,0:T(8,128)(2,1)} %get-tuple-element.48.kept_ref, bf16[512,384]{1,0:T(8,128)(2,1)} %copy-done.13), custom_call_target="tpu_custom_call" | custom-call | flops 3623878656 | bytes 10000000 | tf_op jit(solution)/shard_map/kernel_shares/pallas_call | solution.py:295
  67.6 5.0 %all-to-all-start = ((bf16[4,8,3,144,128]{4,3,2,1,0:T(8,128)(2,1)}), bf16[4,8,3,144,128]{4,3,2,1,0:T(8,128)(2,1)S(1)}, u32[]{:S(2)}, u32[]{:S(2)}) async-start(bf16[4,8,3,144,128]{4,3,2,1,0:T(8,128)(2,1)} %kernel_shares.1), calls=%async_computation | async-start | bytes 7077888 | tf_op jit(solution)/shard_map/all_to_all | solution.py:375
  72.7 2.7 %copy.20 = bf16[512,1536]{0,1:T(8,128)(2,1)} copy(bf16[512,1536]{1,0:T(8,128)(2,1)} %get-tuple-element.68) | data formatting | bytes 3145728 | tf_op jit(solution)/shard_map/pack/pallas_call | solution.py:91
  76.0 2.9 %collective-permute-start.5 = (bf16[128,768]{1,0:T(8,128)(2,1)}, bf16[128,768]{1,0:T(8,128)(2,1)S(1)}, u32[]{:S(2)}, u32[]{:S(2)}) collective-permute-start(bf16[128,768]{1,0:T(8,128)(2,1)} %get-tuple-element.60), channel_id=1, source_target_pairs={{0,32},{32,0},{64,96},{96,64},{1,33},{33,1},{65,97},{97,65},{2,34}... | collective-permute-start | bytes 589832 | tf_op jit(solution)/shard_map/ppermute | solution.py:339
  78.8 2.8 %collective-permute-start.6 = (bf16[128,768]{1,0:T(8,128)(2,1)}, bf16[128,768]{1,0:T(8,128)(2,1)S(1)}, u32[]{:S(2)}, u32[]{:S(2)}) collective-permute-start(bf16[128,768]{1,0:T(8,128)(2,1)} %get-tuple-element.61), channel_id=1, source_target_pairs={{0,64},{32,96},{64,0},{96,32},{1,65},{33,97},{65,1},{97,33},{2,66}... | collective-permute-start | bytes 589832 | tf_op jit(solution)/shard_map/ppermute | solution.py:339
  81.6 12.2 %backward.1 = (bf16[128,1536]{1,0:T(8,128)(2,1)}, bf16[128,1536]{1,0:T(8,128)(2,1)}, bf16[128,1536]{1,0:T(8,128)(2,1)}, bf16[128,1536]{1,0:T(8,128)(2,1)}, f32[1,1536]{1,0:T(1,128)}) custom-call(s32[1]{0:T(128)} %bitcast.odd_ref, bf16[512,768]{1,0:T(8,128)(2,1)} %get-tuple-element.55.grad_ref, bf16[128,2304]{1,0:T(8,128)(2,1)} %get-tuple-element.43.p0, ...), custom_call_target="tpu_custom_call" | custom-call | flops 3623878656 | bytes 20000000 | tf_op jit(solution)/shard_map/backward/pallas_call | solution.py:246
  93.9 3.0 %collective-permute-start.10 = (bf16[128,1536]{1,0:T(8,128)(2,1)}, bf16[128,1536]{1,0:T(8,128)(2,1)}, u32[]{:S(2)}, u32[]{:S(2)}) collective-permute-start(bf16[128,1536]{1,0:T(8,128)(2,1)} %get-tuple-element.73), channel_id=1, source_target_pairs={{0,32},{32,0},{64,96},{96,64},{1,33},{33,1},{65,97},{97,65},{2,34}... | collective-permute-start | bytes 1179656 | tf_op jit(solution)/shard_map/ppermute | solution.py:339
  96.8 2.8 %collective-permute-start.11 = (bf16[128,1536]{1,0:T(8,128)(2,1)}, bf16[128,1536]{1,0:T(8,128)(2,1)}, u32[]{:S(2)}, u32[]{:S(2)}) collective-permute-start(bf16[128,1536]{1,0:T(8,128)(2,1)} %get-tuple-element.74), channel_id=1, source_target_pairs={{0,64},{32,96},{64,0},{96,32},{1,65},{33,97},{65,1},{97,33},{2,66}... | collective-permute-start | bytes 1179656 | tf_op jit(solution)/shard_map/ppermute | solution.py:339
  100.7 1.7 collective-permute-start.9
  103.8 1.8 %select_bitcast_fusion.3 = (f32[1,128,1536]{2,1,0:T(8,128)}, f32[1,128,1536]{2,1,0:T(8,128)}, f32[1,128,1536]{2,1,0:T(8,128)}, f32[1,128,1536]{2,1,0:T(8,128)}) fusion(f32[512,1536]{1,0:T(8,128)S(1)} %fusion.5, pred[]{:T(512)S(6)} %eq.7), kind=kLoop, calls=%fused_computation.18 | loop fusion | flops 786432 | bytes 6291457 | tf_op jit(solution)/shard_map/stack | solution.py:347
  106.5 3.8 %fusion.3 = (f32[2,128,1536]{2,1,0:T(8,128)}, f32[2,128,1536]{2,1,0:T(8,128)}) fusion(f32[1,128,1536]{2,1,0:T(8,128)} %get-tuple-element.85, f32[1,128,1536]{2,1,0:T(8,128)} %get-tuple-element.84, f32[1,128,1536]{2,1,0:T(8,128)} %get-tuple-element.86, f32[1,128,1536]{2,1,0:T(8,128)} %get-tuple-element.83, pred[]{:T(512)S(6)} %eq.6), kind=kLoop, calls=%fused_computation.10 | loop fusion | flops 1572864 | bytes 6291457 | tf_op jit(solution)/shard_map/jit(_where)/select_n | solution.py:350
  110.3 5.2 %point_shares.1 = bf16[4,8,160,128]{3,2,1,0:T(8,128)(2,1)} custom-call(bf16[1536,512]{1,0:T(8,128)(2,1)} %bitcast.63, bf16[1536,512]{1,0:T(8,128)(2,1)} %collective-permute-done.8.other_ref, bf16[512,384]{1,0:T(8,128)(2,1)} %get-tuple-element.97.kept_ref, bf16[512,384]{1,0:T(8,128)(2,1)} %collective-permute-done.9.came_ref, bf16[4,8,16,128]{3,2,1,0:T(8,128)(2,1)} %pad.4.gain_ref), custom_call_target="tpu_custom_call" | custom-call | flops 1207959552 | bytes 6000000 | tf_op jit(solution)/shard_map/point_shares/pallas_call | solution.py:321
  115.5 4.5 %all-to-all-start.1 = ((bf16[4,8,160,128]{3,2,1,0:T(8,128)(2,1)}), bf16[4,8,160,128]{3,2,1,0:T(8,128)(2,1)}, u32[]{:S(2)}, u32[]{:S(2)}) async-start(bf16[4,8,160,128]{3,2,1,0:T(8,128)(2,1)} %point_shares.1), calls=%async_computation.1 | async-start | bytes 2621440 | tf_op jit(solution)/shard_map/all_to_all | solution.py:391
  120.0 2.2 %pad_maximum_fusion = f32[4,128,1536]{2,1,0:T(8,128)S(1)} fusion(f32[2,128,1536]{2,1,0:T(8,128)} %get-tuple-element.82, f32[2,128,1536]{2,1,0:T(8,128)} %get-tuple-element.81), kind=kLoop, calls=%fused_computation | loop fusion | flops 786432 | bytes 6291456 | tf_op jit(solution)/shard_map/concatenate | solution.py:350
  122.4 1.6 fusion.1
  124.0 1.7 reduce_sum.33
  126.8 10.1 %all-to-all-done.1 = bf16[4,8,160,128]{3,2,1,0:T(8,128)(2,1)} async-done(((bf16[4,8,160,128]{3,2,1,0:T(8,128)(2,1)}), bf16[4,8,160,128]{3,2,1,0:T(8,128)(2,1)}, u32[]{:S(2)}, u32[]{:S(2)}) %all-to-all-start.1) | async-done | bytes 1310752 | tf_op jit(solution)/shard_map/all_to_all | solution.py:391
  137.0 1.5 reduce_sum.34
  139.9 6.9 %all-to-all-start.2 = ((bf16[16,304,128]{2,1,0:T(8,128)(2,1)}), bf16[16,304,128]{2,1,0:T(8,128)(2,1)S(1)}, u32[]{:S(2)}, u32[]{:S(2)}) async-start(bf16[16,304,128]{2,1,0:T(8,128)(2,1)} %bitcast.23), calls=%async_computation.2 | async-start | bytes 2490368 | tf_op jit(solution)/shard_map/all_to_all | solution.py:398
  149.7 1.5 fusion
  151.2 12.7 %all-to-all-done.2 = bf16[16,304,128]{2,1,0:T(8,128)(2,1)S(1)} async-done(((bf16[16,304,128]{2,1,0:T(8,128)(2,1)}), bf16[16,304,128]{2,1,0:T(8,128)(2,1)S(1)}, u32[]{:S(2)}, u32[]{:S(2)}) %all-to-all-start.2) | async-done | bytes 1245216 | tf_op jit(solution)/shard_map/all_to_all | solution.py:398
  164.1 9.9 %all-gather = f32[1184,128]{1,0:T(8,128)S(1)} all-gather(f32[296,128]{1,0:T(8,128)S(1)} %slice.81), channel_id=2, replica_groups=mesh['xh'=2,'yh'=2,'yl'=2,'z'=4,'xl'=2,'core'=2] {'xl','core'}, dimensions={0}, use_global_device_ids=true | all-gather | bytes 757760 | tf_op jit(solution)/shard_map/all_gather | solution.py:406
  (71 shorter events, 15.3 us)
Async XLA Ops:
  0.6 12.5 %copy-start.9 = (f32[1536]{0:T(1024)S(1)}, f32[1536]{0:T(1024)}, u32[]{:S(2)}) copy-start(f32[1536]{0:T(1024)} %param.6) | copy-start | bytes 18436
  6.6 16.8 %collective-permute-start = (bf16[128,2304]{1,0:T(8,128)(2,1)}, bf16[128,2304]{1,0:T(8,128)(2,1)S(1)}, u32[]{:S(2)}, u32[]{:S(2)}) collective-permute-start(bf16[128,2304]{1,0:T(8,128)(2,1)} %get-tuple-element.44), channel_id=1, source_target_pairs={{0,32},{32,0},{64,96},{96,64},{1,33},{33,1},{65,97},{97,65},{2,34}... | collective-permute-start | bytes 1769480 | tf_op jit(solution)/shard_map/ppermute | solution.py:339
  10.4 15.6 %collective-permute-start.1 = (bf16[128,2304]{1,0:T(8,128)(2,1)}, bf16[128,2304]{1,0:T(8,128)(2,1)S(1)}, u32[]{:S(2)}, u32[]{:S(2)}) collective-permute-start(bf16[128,2304]{1,0:T(8,128)(2,1)} %get-tuple-element.45), channel_id=1, source_target_pairs={{0,64},{32,96},{64,0},{96,32},{1,65},{33,97},{65,1},{97,33},{2,66}... | collective-permute-start | bytes 1769480 | tf_op jit(solution)/shard_map/ppermute | solution.py:339
  13.1 25.4 %collective-permute-start.2 = (bf16[128,2304]{1,0:T(8,128)(2,1)}, bf16[128,2304]{1,0:T(8,128)(2,1)S(1)}, u32[]{:S(2)}, u32[]{:S(2)}) collective-permute-start(bf16[128,2304]{1,0:T(8,128)(2,1)} %get-tuple-element.46), channel_id=1, source_target_pairs={{0,96},{32,64},{64,32},{96,0},{1,97},{33,65},{65,33},{97,1},{2,98}... | collective-permute-start | bytes 1769480 | tf_op jit(solution)/shard_map/ppermute | solution.py:339
  23.4 15.2 %copy-start.4 = (bf16[128,2304]{1,0:T(8,128)(2,1)}, bf16[128,2304]{1,0:T(8,128)(2,1)S(1)}, u32[]{:S(2)}) copy-start(bf16[128,2304]{1,0:T(8,128)(2,1)S(1)} %collective-permute-done.p1) | copy-start | bytes 1769476
  26.0 12.6 %copy-start.5 = (bf16[128,2304]{1,0:T(8,128)(2,1)}, bf16[128,2304]{1,0:T(8,128)(2,1)S(1)}, u32[]{:S(2)}) copy-start(bf16[128,2304]{1,0:T(8,128)(2,1)S(1)} %collective-permute-done.1.p2) | copy-start | bytes 1769476
  38.6 0.9 copy-start.6
  51.4 3.6 %copy-start.12 = (bf16[512,384]{1,0:T(8,128)(2,1)S(1)}, bf16[512,384]{1,0:T(8,128)(2,1)}, u32[]{:S(2)}) copy-start(bf16[512,384]{1,0:T(8,128)(2,1)} %get-tuple-element.49) | copy-start | bytes 1179652
  53.2 5.4 %copy-start.3 = (bf16[512,1536]{0,1:T(8,128)(2,1)}, bf16[512,1536]{0,1:T(8,128)(2,1)S(1)}, u32[]{:S(2)}) copy-start(bf16[512,1536]{0,1:T(8,128)(2,1)S(1)} %copy.19) | copy-start | bytes 4718596
  53.2 5.4 %collective-permute-start.3 = (bf16[1536,512]{1,0:T(8,128)(2,1)S(1)}, bf16[1536,512]{1,0:T(8,128)(2,1)S(1)}, u32[]{:S(2)}, u32[]{:S(2)}) collective-permute-start(bf16[1536,512]{1,0:T(8,128)(2,1)S(1)} %bitcast.71), channel_id=1, source_target_pairs={{0,1},{1,0},{2,3},{3,2},{4,5},{5,4},{6,7},{7,6},{8,9},{9,8},{10,11... | collective-permute-start | bytes 4718600 | tf_op jit(solution)/shard_map/ppermute | solution.py:334
  55.1 3.6 %collective-permute-start.4 = (bf16[512,384]{1,0:T(8,128)(2,1)S(1)}, bf16[512,384]{1,0:T(8,128)(2,1)S(1)}, u32[]{:S(2)}, u32[]{:S(2)}) collective-permute-start(bf16[512,384]{1,0:T(8,128)(2,1)S(1)} %copy-done.12), channel_id=1, source_target_pairs={{0,1},{1,0},{2,3},{3,2},{4,5},{5,4},{6,7},{7,6},{8,9},{9,8},{10,11... | collective-permute-start | bytes 1179656 | tf_op jit(solution)/shard_map/ppermute | solution.py:334
  58.6 0.8 copy-start.13
  58.7 1.3 copy-start.11
  67.6 47.8 %all-to-all-start = ((bf16[4,8,3,144,128]{4,3,2,1,0:T(8,128)(2,1)}), bf16[4,8,3,144,128]{4,3,2,1,0:T(8,128)(2,1)S(1)}, u32[]{:S(2)}, u32[]{:S(2)}) async-start(bf16[4,8,3,144,128]{4,3,2,1,0:T(8,128)(2,1)} %kernel_shares.1), calls=%async_computation | async-start | bytes 7077888 | tf_op jit(solution)/shard_map/all_to_all | solution.py:375
  75.3 35.0 %collective-permute-start.8 = (bf16[1536,512]{1,0:T(8,128)(2,1)}, bf16[1536,512]{1,0:T(8,128)(2,1)}, u32[]{:S(2)}, u32[]{:S(2)}) collective-permute-start(bf16[1536,512]{1,0:T(8,128)(2,1)} %bitcast.62), channel_id=1, source_target_pairs={{0,1},{1,0},{2,3},{3,2},{4,5},{5,4},{6,7},{7,6},{8,9},{9,8},{10,11... | collective-permute-start | bytes 4718600 | tf_op jit(solution)/shard_map/ppermute | solution.py:334
  76.0 20.9 %collective-permute-start.5 = (bf16[128,768]{1,0:T(8,128)(2,1)}, bf16[128,768]{1,0:T(8,128)(2,1)S(1)}, u32[]{:S(2)}, u32[]{:S(2)}) collective-permute-start(bf16[128,768]{1,0:T(8,128)(2,1)} %get-tuple-element.60), channel_id=1, source_target_pairs={{0,32},{32,0},{64,96},{96,64},{1,33},{33,1},{65,97},{97,65},{2,34}... | collective-permute-start | bytes 589832 | tf_op jit(solution)/shard_map/ppermute | solution.py:339
  78.8 20.8 %collective-permute-start.6 = (bf16[128,768]{1,0:T(8,128)(2,1)}, bf16[128,768]{1,0:T(8,128)(2,1)S(1)}, u32[]{:S(2)}, u32[]{:S(2)}) collective-permute-start(bf16[128,768]{1,0:T(8,128)(2,1)} %get-tuple-element.61), channel_id=1, source_target_pairs={{0,64},{32,96},{64,0},{96,32},{1,65},{33,97},{65,1},{97,33},{2,66}... | collective-permute-start | bytes 589832 | tf_op jit(solution)/shard_map/ppermute | solution.py:339
  81.6 18.0 %collective-permute-start.7 = (bf16[128,768]{1,0:T(8,128)(2,1)}, bf16[128,768]{1,0:T(8,128)(2,1)S(1)}, u32[]{:S(2)}, u32[]{:S(2)}) collective-permute-start(bf16[128,768]{1,0:T(8,128)(2,1)} %get-tuple-element.62), channel_id=1, source_target_pairs={{0,96},{32,64},{64,32},{96,0},{1,97},{33,65},{65,33},{97,1},{2,98}... | collective-permute-start | bytes 589832 | tf_op jit(solution)/shard_map/ppermute | solution.py:339
  81.6 18.0 %copy-start.8 = (bf16[128,768]{1,0:T(8,128)(2,1)S(1)}, bf16[128,768]{1,0:T(8,128)(2,1)}, u32[]{:S(2)}) copy-start(bf16[128,768]{1,0:T(8,128)(2,1)} %get-tuple-element.63) | copy-start | bytes 589828
  93.9 44.8 %collective-permute-start.10 = (bf16[128,1536]{1,0:T(8,128)(2,1)}, bf16[128,1536]{1,0:T(8,128)(2,1)}, u32[]{:S(2)}, u32[]{:S(2)}) collective-permute-start(bf16[128,1536]{1,0:T(8,128)(2,1)} %get-tuple-element.73), channel_id=1, source_target_pairs={{0,32},{32,0},{64,96},{96,64},{1,33},{33,1},{65,97},{97,65},{2,34}... | collective-permute-start | bytes 1179656 | tf_op jit(solution)/shard_map/ppermute | solution.py:339
  96.8 41.9 %collective-permute-start.11 = (bf16[128,1536]{1,0:T(8,128)(2,1)}, bf16[128,1536]{1,0:T(8,128)(2,1)}, u32[]{:S(2)}, u32[]{:S(2)}) collective-permute-start(bf16[128,1536]{1,0:T(8,128)(2,1)} %get-tuple-element.74), channel_id=1, source_target_pairs={{0,64},{32,96},{64,0},{96,32},{1,65},{33,97},{65,1},{97,33},{2,66}... | collective-permute-start | bytes 1179656 | tf_op jit(solution)/shard_map/ppermute | solution.py:339
  99.6 39.1 %collective-permute-start.12 = (bf16[128,1536]{1,0:T(8,128)(2,1)}, bf16[128,1536]{1,0:T(8,128)(2,1)}, u32[]{:S(2)}, u32[]{:S(2)}) collective-permute-start(bf16[128,1536]{1,0:T(8,128)(2,1)} %get-tuple-element.75), channel_id=1, source_target_pairs={{0,96},{32,64},{64,32},{96,0},{1,97},{33,65},{65,33},{97,1},{2,98}... | collective-permute-start | bytes 1179656 | tf_op jit(solution)/shard_map/ppermute | solution.py:339
  99.6 2.8 %copy-start.2 = (bf16[768,1536]{1,0:T(8,128)(2,1)S(1)}, bf16[768,1536]{1,0:T(8,128)(2,1)}, u32[]{:S(2)}) copy-start(bf16[768,1536]{1,0:T(8,128)(2,1)} %point_ref.1) | copy-start | bytes 7077892
  100.7 9.6 %collective-permute-start.9 = (bf16[512,384]{1,0:T(8,128)(2,1)}, bf16[512,384]{1,0:T(8,128)(2,1)}, u32[]{:S(2)}, u32[]{:S(2)}) collective-permute-start(bf16[512,384]{1,0:T(8,128)(2,1)} %get-tuple-element.96), channel_id=1, source_target_pairs={{0,1},{1,0},{2,3},{3,2},{4,5},{5,4},{6,7},{7,6},{8,9},{9,8},{10,11... | collective-permute-start | bytes 1179656 | tf_op jit(solution)/shard_map/ppermute | solution.py:334
  103.8 1.8 %copy-start.10 = (f32[1,1536]{1,0:T(1,128)S(1)}, f32[1,1536]{1,0:T(1,128)}, u32[]{:S(2)}) copy-start(f32[1,1536]{1,0:T(1,128)} %get-tuple-element.69) | copy-start | bytes 18436
  115.5 21.5 %all-to-all-start.1 = ((bf16[4,8,160,128]{3,2,1,0:T(8,128)(2,1)}), bf16[4,8,160,128]{3,2,1,0:T(8,128)(2,1)}, u32[]{:S(2)}, u32[]{:S(2)}) async-start(bf16[4,8,160,128]{3,2,1,0:T(8,128)(2,1)} %point_shares.1), calls=%async_computation.1 | async-start | bytes 2621440 | tf_op jit(solution)/shard_map/all_to_all | solution.py:391
  120.0 2.4 %copy-start = (bf16[1,512,1536]{2,1,0:T(8,128)(2,1)S(1)}, bf16[1,512,1536]{2,1,0:T(8,128)(2,1)}, u32[]{:S(2)}) copy-start(bf16[1,512,1536]{2,1,0:T(8,128)(2,1)} %param.5) | copy-start | bytes 4718596
  139.9 6.9 %copy-start.7 = (bf16[128,1536]{1,0:T(8,128)(2,1)S(1)}, bf16[128,1536]{1,0:T(8,128)(2,1)}, u32[]{:S(2)}) copy-start(bf16[128,1536]{1,0:T(8,128)(2,1)} %get-tuple-element.79) | copy-start | bytes 1179652
  139.9 24.0 %all-to-all-start.2 = ((bf16[16,304,128]{2,1,0:T(8,128)(2,1)}), bf16[16,304,128]{2,1,0:T(8,128)(2,1)S(1)}, u32[]{:S(2)}, u32[]{:S(2)}) async-start(bf16[16,304,128]{2,1,0:T(8,128)(2,1)} %bitcast.23), calls=%async_computation.2 | async-start | bytes 2490368 | tf_op jit(solution)/shard_map/all_to_all | solution.py:398
  148.3 1.4 copy-start.1

commit v4 on v3

--- a/solution.py
+++ b/solution.py
@@ -23,6 +23,12 @@
 
 def dot(left, right):
     return jnp.dot(left, right, preferred_element_type=F32)
+
+
+def contract_rows(left, right):
+    return lax.dot_general(
+        left, right, (((0,), (0,)), ((), ())), preferred_element_type=F32
+    )
 
 
 def contract_cols(left, right):
@@ -121,7 +127,7 @@
     for copy in ins + copies:
         copy.start()
     core = core_ref[0]
-    step = 32
+    step = 64
     for k in range(4):
         ins[k].wait()
 
@@ -222,7 +228,7 @@
             total[:, cols] = value if i == 0 else total[:, cols] + value
     for copy in ins:
         copy.wait()
-    step = 32
+    step = 64
     share = jnp.zeros((8, C), F32)
     for k, out in enumerate((b0, b1, b2, b3)):
 
@@ -259,151 +265,328 @@
             pltpu.SemaphoreType.DMA((6,)),
         ],
         compiler_params=params(56),
-        cost_estimate=cost(6 * N * C * H, 20_000_000),
+        cost_estimate=cost(1_000_000, 100_000),
         name="backward",
     )(odd, grads, *pieces, gain, slope, inv, weights)
 
 
-def kernel_share_kernel(odd_ref, own_ref, other_ref, kept_ref, came_ref, out_ref, right, ring):
-    @pl.when(pl.program_id(0) == 0)
-    def _():
-        odd = odd_ref[0]
-        for i, source in enumerate((kept_ref, came_ref)):
-            ring[Q:5 * Q] = source[...]
-            ring[:Q] = source[3 * Q:]
-            ring[5 * Q:] = source[:Q]
-            rows = slice(i * N, (i + 1) * N)
-            near = pl.multiple_of(jnp.where(odd == 0, 2 * Q, 0), Q)
-            far = pl.multiple_of(jnp.where(odd == 0, 0, 2 * Q), Q)
-            right[rows, :HALF] = ring[pl.ds(near, N), :]
-            right[rows, HALF:2 * HALF] = source[...]
-            right[rows, 2 * HALF:] = ring[pl.ds(far, N), :]
-
-    value = dot(own_ref[...], right[:N]) + dot(other_ref[...], right[N:])
-    value = value.astype(BF16)
-    for t in range(3):
-        for b in range(3):
-            at = t * HALF + b * 128
-            part = value[:, at:at + 128].reshape(2, 4, 48, 128)
-            for z in range(4):
-                out_ref[z, :, t, 48 * b:48 * b + 48, :] = part[:, z]
+def load_columns(own_hbm, other_hbm, own, other, sems):
+    ins = []
+    for i in range(4):
+        cols = pl.ds(i * HALF, HALF)
+        ins.append((
+            pltpu.make_async_copy(own_hbm.at[:, cols], own.at[i], sems.at[2 * i]),
+            pltpu.make_async_copy(other_hbm.at[:, cols], other.at[i], sems.at[2 * i + 1]),
+        ))
+        for copy in ins[-1]:
+            copy.start()
+    return ins
+
+
+def kernel_share_kernel(
+    odd_ref, own_hbm, other_hbm, kept_ref, came_ref, out_ref,
+    own, other, right, ring, value, in_sems, out_sems,
+):
+    ins = load_columns(own_hbm, other_hbm, own, other, in_sems)
+    odd = odd_ref[0]
+    near = pl.multiple_of(jnp.where(odd == 0, 2 * Q, 0), Q)
+    far = pl.multiple_of(jnp.where(odd == 0, 0, 2 * Q), Q)
+    for i, source in enumerate((kept_ref, came_ref)):
+        ring[Q:5 * Q] = source[...]
+        ring[:Q] = source[3 * Q:]
+        ring[5 * Q:] = source[:Q]
+        rows = slice(i * N, (i + 1) * N)
+        right[rows, :HALF] = ring[pl.ds(near, N), :]
+        right[rows, HALF:2 * HALF] = source[...]
+        right[rows, 2 * HALF:] = ring[pl.ds(far, N), :]
+    outs = []
+    for i in range(4):
+        for copy in ins[i]:
+            copy.wait()
+        part = contract_rows(own[i], right[:N]) + contract_rows(other[i], right[N:])
+        part = part.astype(BF16)
+        for b in range(9):
+            value[2 * i:2 * i + 2, :, 48 * b:48 * b + 48, :] = part[
+                :, 128 * b:128 * b + 128
+            ].reshape(2, 4, 48, 128)
+        for g in (2 * i, 2 * i + 1):
+            outs.append(
+                pltpu.make_async_copy(value.at[g], out_ref.at[:, g], out_sems.at[g])
+            )
+            outs[-1].start()
+    for copy in outs:
+        copy.wait()
 
 
 def kernel_shares(odd, own, other, kept, came):
-    whole = pl.BlockSpec((N, HALF), lambda i: (0, 0))
-    part = pl.BlockSpec((C // 4, N), lambda i: (i, 0))
     return pl.pallas_call(
         kernel_share_kernel,
-        grid=(4,),
-        in_specs=[SMEM, part, part, whole, whole],
-        out_specs=pl.BlockSpec((4, 2, 3, 144, 128), lambda i: (0, i, 0, 0, 0)),
-        out_shape=jax.ShapeDtypeStruct((4, 8, 3, 144, 128), BF16),
-        scratch_shapes=[pltpu.VMEM((2 * N, 3 * HALF), BF16), pltpu.VMEM((6 * Q, HALF), BF16)],
+        in_specs=[SMEM, ANY, ANY, VMEM, VMEM],
+        out_specs=ANY,
+        out_shape=jax.ShapeDtypeStruct((4, 8, 432, 128), BF16),
+        scratch_shapes=[
+            pltpu.VMEM((4, N, HALF), BF16),
+            pltpu.VMEM((4, N, HALF), BF16),
+            pltpu.VMEM((2 * N, 3 * HALF), BF16),
+            pltpu.VMEM((6 * Q, HALF), BF16),
+            pltpu.VMEM((8, 4, 432, 128), BF16),
+            pltpu.SemaphoreType.DMA((8,)),
+            pltpu.SemaphoreType.DMA((8,)),
+        ],
         compiler_params=params(56),
         cost_estimate=cost(6 * N * C * H, 10_000_000),
         name="kernel_shares",
     )(odd, own, other, kept, came)
 
 
-def point_share_kernel(own_ref, other_ref, kept_ref, came_ref, gain_ref, out_ref):
-    out_ref[:, :, 144:, :] = gain_ref[...]
-    value = dot(own_ref[...], kept_ref[...]) + dot(other_ref[...], came_ref[...])
-    value = value.astype(BF16)
-    for b in range(3):
-        part = value[:, b * 128:b * 128 + 128].reshape(2, 4, 48, 128)
-        for z in range(4):
-            out_ref[z, :, 48 * b:48 * b + 48, :] = part[:, z]
-
-
-def point_shares(own, other, kept, came, gain):
-    whole = pl.BlockSpec((N, HALF), lambda i: (0, 0))
-    part = pl.BlockSpec((C // 4, N), lambda i: (i, 0))
+def point_share_kernel(
+    z_ref, own_hbm, other_hbm, kept_ref, came_ref, gain_ref, d0, d1, d2, d3,
+    own, other, value, in_sems, out_sems,
+):
+    ins = load_columns(own_hbm, other_hbm, own, other, in_sems)
+    value[:, :, 144:] = gain_ref[...]
+    outs = []
+    for i in range(4):
+        for copy in ins[i]:
+            copy.wait()
+        part = contract_rows(own[i], kept_ref[...]) + contract_rows(other[i], came_ref[...])
+        part = part.astype(BF16)
+        for b in range(3):
+            value[2 * i:2 * i + 2, :, 48 * b:48 * b + 48, :] = part[
+                :, 128 * b:128 * b + 128
+            ].reshape(2, 4, 48, 128)
+        for g in (2 * i, 2 * i + 1):
+            for d, out in enumerate((d0, d1, d2, d3)):
+                source = value.at[g, lax.rem(z_ref[0] + d, 4)]
+                outs.append(pltpu.make_async_copy(source, out.at[g], out_sems.at[len(outs)]))
+                outs[-1].start()
+    for copy in outs:
+        copy.wait()
+
+
+def point_shares(z, own, other, kept, came, gain):
     return pl.pallas_call(
         point_share_kernel,
-        grid=(4,),
-        in_specs=[part, part, whole, whole, pl.BlockSpec((4, 2, 16, 128), lambda i: (0, i, 0, 0))],
-        out_specs=pl.BlockSpec((4, 2, 160, 128), lambda i: (0, i, 0, 0)),
-        out_shape=jax.ShapeDtypeStruct((4, 8, 160, 128), BF16),
+        in_specs=[SMEM, ANY, ANY, VMEM, VMEM, VMEM],
+        out_specs=[ANY] * 4,
+        out_shape=[jax.ShapeDtypeStruct((8, 160, 128), BF16)] * 4,
+        scratch_shapes=[
+            pltpu.VMEM((4, N, HALF), BF16),
+            pltpu.VMEM((4, N, HALF), BF16),
+            pltpu.VMEM((8, 4, 160, 128), BF16),
+            pltpu.SemaphoreType.DMA((8,)),
+            pltpu.SemaphoreType.DMA((32,)),
+        ],
         compiler_params=params(56),
         cost_estimate=cost(2 * N * C * H, 6_000_000),
         name="point_shares",
-    )(own, other, kept, came, gain)
+    )(z, own, other, kept, came, gain)
+
+
+def four_sum(a, b, c, d):
+    return ((a.astype(F32) + b.astype(F32)) + (c.astype(F32) + d.astype(F32))).astype(BF16)
+
+
+def tap_sum_kernel(shares_ref, out_ref):
+    out_ref[...] = four_sum(*[shares_ref[i] for i in range(4)])
+
+
+def tap_sums(shares):
+    return pl.pallas_call(
+        tap_sum_kernel,
+        grid=(4,),
+        in_specs=[pl.BlockSpec((4, 2, 432, 128), lambda g: (0, g, 0, 0))],
+        out_specs=pl.BlockSpec((2, 432, 128), lambda g: (g, 0, 0)),
+        out_shape=jax.ShapeDtypeStruct((8, 432, 128), BF16),
+        compiler_params=params(32),
+        cost_estimate=cost(3_000_000, 5_000_000),
+        name="tap_sums",
+    )(shares)
+
+
+def plane_kernel(taps_ref, d0, d1, d2, d3, out_ref):
+    point = four_sum(d0[...], d1[...], d2[...], d3[...])
+    out_ref[:, 0, :288] = taps_ref[:, :288]
+    out_ref[:, 1, :144] = taps_ref[:, 288:]
+    out_ref[:, 1, 144:288] = point[:, :144]
+    for chip in range(2):
+        out_ref[:, chip, 288:] = point[:, 144:]
+
+
+def plane_shares(taps, points):
+    return pl.pallas_call(
+        plane_kernel,
+        in_specs=[VMEM] * 5,
+        out_specs=VMEM,
+        out_shape=jax.ShapeDtypeStruct((8, 2, 304, 128), BF16),
+        compiler_params=params(32),
+        cost_estimate=cost(1_000_000, 3_000_000),
+        name="plane_shares",
+    )(taps, *points)
+
+
+def home_rows(me_ref, k):
+    return pl.ds(pl.multiple_of(lax.bitwise_xor(me_ref[0], k) * Q, Q), Q)
+
+
+def stream_out_kernel(
+    me_ref, m0, m1, m2, m3, point_ref, stream_ref, out_ref,
+    mid, point, rows, result, in_sems, out_sems,
+):
+    ins = [pltpu.make_async_copy(point_ref, point, in_sems.at[8])]
+    for k, source in enumerate((m0, m1, m2, m3)):
+        at = pl.ds(k * Q, Q)
+        ins.append(pltpu.make_async_copy(source, mid.at[at], in_sems.at[k]))
+        ins.append(
+            pltpu.make_async_copy(stream_ref.at[home_rows(me_ref, k)], rows.at[at], in_sems.at[4 + k])
+        )
+    for copy in ins:
+        copy.start()
+    for copy in ins:
+        copy.wait()
+    for n in range(6):
+        cols = slice(n * 256, (n + 1) * 256)
+        result[:, cols] = (rows[:, cols].astype(F32) + dot(mid[...], point[:, cols])).astype(BF16)
+    outs = [
+        pltpu.make_async_copy(
+            result.at[pl.ds(k * Q, Q)], out_ref.at[home_rows(me_ref, k)], out_sems.at[k]
+        )
+        for k in range(4)
+    ]
+    for copy in outs:
+        copy.start()
+    for copy in outs:
+        copy.wait()
+
+
+def home_stream_out(me, mid, point_kernel, stream):
+    return pl.pallas_call(
+        stream_out_kernel,
+        in_specs=[SMEM] + [ANY] * 6,
+        out_specs=ANY,
+        out_shape=jax.ShapeDtypeStruct((N, C), BF16),
+        scratch_shapes=[
+            pltpu.VMEM((N, H), BF16),
+            pltpu.VMEM((H, C), BF16),
+            pltpu.VMEM((N, C), BF16),
+            pltpu.VMEM((N, C), BF16),
+            pltpu.SemaphoreType.DMA((9,)),
+            pltpu.SemaphoreType.DMA((4,)),
+        ],
+        compiler_params=params(56),
+        cost_estimate=cost(2 * N * C * H, 6_000_000),
+        name="stream_out",
+    )(me, *mid, point_kernel, stream)
+
+
+def stream_grad_kernel(
+    me_ref, b0, b1, b2, b3, cotan_ref, out_ref, back, rows, in_sems, out_sems
+):
+    ins = []
+    for k, source in enumerate((b0, b1, b2, b3)):
+        ins.append((
+            pltpu.make_async_copy(source, back.at[k], in_sems.at[k]),
+            pltpu.make_async_copy(cotan_ref.at[home_rows(me_ref, k)], rows.at[k], in_sems.at[4 + k]),
+        ))
+        for copy in ins[-1]:
+            copy.start()
+    outs = []
+    for k in range(4):
+        for copy in ins[k]:
+            copy.wait()
+        rows[k] = (rows[k].astype(F32) + back[k].astype(F32)).astype(BF16)
+        outs.append(
+            pltpu.make_async_copy(rows.at[k], out_ref.at[home_rows(me_ref, k)], out_sems.at[k])
+        )
+        outs[-1].start()
+    for copy in outs:
+        copy.wait()
+
+
+def home_stream_grad(me, back, cotan):
+    return pl.pallas_call(
+        stream_grad_kernel,
+        in_specs=[SMEM] + [ANY] * 5,
+        out_specs=ANY,
+        out_shape=jax.ShapeDtypeStruct((N, C), BF16),
+        scratch_shapes=[
+            pltpu.VMEM((4, Q, C), BF16),
+            pltpu.VMEM((4, Q, C), BF16),
+            pltpu.SemaphoreType.DMA((8,)),
+            pltpu.SemaphoreType.DMA((4,)),
+        ],
+        compiler_params=params(56),
+        cost_estimate=cost(2 * N * C, 5_000_000),
+        name="stream_grad",
+    )(me, *back, cotan)
 
 
 def swap_core(value):
     return lax.ppermute(value, "core", [(0, 1), (1, 0)])
 
 
+def partner(value, k):
+    return lax.ppermute(value, GROUP, [(i, i ^ k) for i in range(4)])
+
+
 def exchange(pieces):
-    return [pieces[0]] + [
-        lax.ppermute(pieces[k], GROUP, [(i, i ^ k) for i in range(4)]) for k in (1, 2, 3)
-    ]
-
-
-def restored(pieces, me):
-    pairs = []
-    for a, b in (pieces[:2], pieces[2:]):
-        turn = (me & 1) == 1
-        pairs.append(jnp.stack([jnp.where(turn, b, a), jnp.where(turn, a, b)]))
-    low, high = pairs
-    turn = (me & 2) == 2
-    out = jnp.concatenate([jnp.where(turn, high, low), jnp.where(turn, low, high)])
-    return out.reshape(N, out.shape[2])
+    return [pieces[0]] + [partner(pieces[k], k) for k in range(1, len(pieces))]
 
 
 def shards(stream, norm_gain_vector, conv_kernel, point_kernel, out_grad):
     core = lax.axis_index("core").astype(jnp.int32)
     odd = lax.axis_index("yh").astype(jnp.int32)
     me = 2 * lax.axis_index("xh") + odd
-    core_word, odd_word = core.reshape(1), odd.reshape(1)
+    z = lax.axis_index("z").astype(jnp.int32)
+    core_word, odd_word, z_word = core.reshape(1), odd.reshape(1), z.reshape(1)
     gain_row = norm_gain_vector.reshape(1, C)
     cotan = out_grad[0]
 
     packed = pack(me.reshape(1), stream[0], cotan, point_kernel)
     pieces = exchange(packed[:4])
-    cotan_cols = packed[4].T
-    cotan_other = swap_core(cotan_cols)
+    cotan_turned = packed[4]
+    cotan_other = swap_core(cotan_turned)
 
     act, slope_in, inv, m0, m1, m2, m3, pre_grad, kept, away = forward(
         odd_word, core_word, pieces, gain_row, conv_kernel
     )
-    act_cols = act.T
-    act_other = swap_core(act_cols)
+    act_other = swap_core(act)
     came = swap_core(away)
-    shares = kernel_shares(odd_word, act_cols, act_other, kept, came)
-    shares, pre_grad, *mid = lax.optimization_barrier((shares, pre_grad, m0, m1, m2, m3))
+    shares = kernel_shares(odd_word, act, act_other, kept, came)
+    shares, pre_grad, m0, m1, m2, m3 = lax.optimization_barrier(
+        (shares, pre_grad, m0, m1, m2, m3)
+    )
     shares = lax.all_to_all(shares, "z", 0, 0, tiled=True)
-    mid = exchange(mid)
+    mid = exchange([m0, m1, m2, m3])
     b0, b1, b2, b3, gain = backward(
         odd_word, pre_grad, pieces, gain_row, slope_in, inv, conv_kernel
     )
+    back = exchange([b0, b1, b2, b3])
     gain, *mid = lax.optimization_barrier((gain, *mid))
-    back = exchange([b0, b1, b2, b3])
-
-    mid = jnp.concatenate(mid)
-    low, high = mid[:, :HALF], mid[:, HALF:]
+    mid_home = jnp.concatenate(mid)
+    low, high = mid_home[:, :HALF], mid_home[:, HALF:]
     mid_kept = jnp.where(core == 0, low, high)
     mid_came = swap_core(jnp.where(core == 0, high, low))
-    gain = gain.astype(BF16).reshape(8, 4, 1, 48).transpose(1, 0, 2, 3)
+    gain = gain.astype(BF16).reshape(8, 4, 1, 48)
     gain = jnp.pad(gain, ((0, 0), (0, 0), (0, 15), (0, 80)))
-    point_part = point_shares(cotan_cols, cotan_other, mid_kept, mid_came, gain)
-    shares, point_part = lax.optimization_barrier((shares, point_part))
-    point_part = lax.all_to_all(point_part, "z", 0, 0, tiled=True)
-    shares = jnp.sum(shares.astype(F32), axis=0).astype(BF16)
-    point_part = jnp.sum(point_part.astype(F32), axis=0).astype(BF16)
-    first = [shares[:, 0], shares[:, 1], point_part[:, 144:]]
-    second = [shares[:, 2], point_part]
-    plane = jnp.stack([jnp.concatenate(first, 1), jnp.concatenate(second, 1)], 1)
-    plane, *back = lax.optimization_barrier((plane, *back))
-    got = lax.all_to_all(plane.reshape(16, 304, 128), PLANE, 0, 0, tiled=True)
-
-    stream_out = dot(mid, point_kernel).reshape(4, Q, C)
-    stream_out = restored([stream_out[k] for k in range(4)], me)
-    stream_out = (stream[0].astype(F32) + stream_out).astype(BF16)
-    stream_grad = (cotan.astype(F32) + restored(back, me).astype(F32)).astype(BF16)
-
-    total = jnp.sum(got.astype(F32), axis=0)[:296]
-    whole = lax.all_gather(total, ("xl", "core"))
+    points = list(
+        point_shares(z_word, cotan_turned, cotan_other, mid_kept, mid_came, gain)
+    )
+    points[0], points[1], points[2], points[3], back[1], back[2], *mid = lax.optimization_barrier(
+        (*points, back[1], back[2], *mid)
+    )
+    points = [points[0]] + [
+        lax.ppermute(points[d], "z", [(i, (i + d) % 4) for i in range(4)]) for d in (1, 2, 3)
+    ]
+    stream_out = home_stream_out(me.reshape(1), mid, point_kernel, stream[0])
+    shares, stream_out = lax.optimization_barrier((shares, stream_out))
+    taps = tap_sums(shares)
+    stream_grad = home_stream_grad(me.reshape(1), back, cotan)
+    taps, stream_grad, *points = lax.optimization_barrier((taps, stream_grad, *points))
+    plane = plane_shares(taps, points).reshape(16, 304, 128)
+    plane = lax.all_to_all(plane, PLANE, 0, 0, tiled=True)
+    plane = jnp.sum(plane.astype(F32), axis=0)[:296]
+    whole = lax.all_gather(plane, ("xl", "core"))
     gain_grad = whole[0, 288, :48] + whole[1, 288, :48]
     whole = whole[:, :288].reshape(2, 2, 2, 3, 48, 128).transpose(0, 2, 4, 1, 3, 5)
     whole = whole.reshape(4, 48, H)

time: 177 us -> 166 us (0.938)
  blocking collectives: 9.9 us -> 33.7 us
  waiting for transfers between devices: 51.1 us -> 34.2 us
  other arithmetic: 17.7 us -> 2.28 us
  Pallas kernels: 43 us -> 53.1 us
  starting transfers between devices: 38.6 us -> 31.7 us
  local copies, waits for them, and re-layouts: 14 us -> 9.19 us
    all_to_all x0 -> x1, blocking collectives: none -> 24.3 us  [shards(): plane = lax.all_to_all(plane, PLANE, 0, 0, tiled=True)]
    all_to_all x2 -> x0, waiting for transfers between devices: 22.8 us -> none  [the longest x1 12.7 us: shards(): got = lax.all_to_all(plane.reshape(16, 304, 128), PLANE, 0, 0, tiled=True)]
    pallas_call x2 -> x6, Pallas kernels: 12.9 us -> 24.6 us  [the longest x1 8.97 us: kernel_shares(): pl.pallas_call(kernel_share_kernel, in_specs=[SMEM, ANY, ANY, VMEM, VMEM]...]
    all_to_all x2 -> x0, starting transfers between devices: 11.4 us -> none  [the longest x1 6.85 us: shards(): got = lax.all_to_all(plane.reshape(16, 304, 128), PLANE, 0, 0, tiled=True)]
    ppermute x9 -> x12, waiting for transfers between devices: 24.8 us -> 30.5 us  [the longest x9 29.3 us: partner(): return lax.ppermute(value, GROUP, [(i, i ^ k) for i in range(4)])]
    ppermute x9 -> x12, starting transfers between devices: 18 us -> 23.2 us  [the longest x9 17.9 us: partner(): return lax.ppermute(value, GROUP, [(i, i ^ k) for i in range(4)])]
    pallas_call x2 -> x0, local copies, waits for them, and re-layouts: 4.43 us -> none  [the longest x1 2.66 us: pack(): pl.pallas_call(pack_kernel, in_specs=[SMEM] + [ANY] * 3, out_specs=[ANY]...]
    select_n x2 -> x0, other arithmetic: 3.95 us -> none  [restored(): jnp.where(turn, high, low)]
  transfers between devices with their start and end apart: 16 -> 17, of which waited for: 6 -> 8; matrix products, arithmetic and copies ran while one was open for 13% -> 4% of each run, Pallas kernels for 10% -> 15%
where the time goes in v4:
time: 166 us; the launch traced here: 165 us
  Pallas kernels  53.1 us (32%)
  waiting for transfers between devices  34.2 us (21%)
  blocking collectives  33.7 us (20%)
  starting transfers between devices  31.7 us (19%)
  local copies, waits for them, and re-layouts  9.19 us (6%)
  other arithmetic  2.28 us (1%)
    ppermute x9, waiting for transfers between devices, partner(): return lax.ppermute(value, GROUP, [(i, i ^ k) for i in range(4)])  29.3 us
    all_to_all x1, blocking collectives, shards(): plane = lax.all_to_all(plane, PLANE, 0, 0, tiled=True)  24.3 us
    ppermute x9, starting transfers between devices, partner(): return lax.ppermute(value, GROUP, [(i, i ^ k) for i in range(4)])  17.9 us
    pallas_call x1, Pallas kernels, forward(): pl.pallas_call(forward_kernel, in_specs=[SMEM] * 2 + [ANY] * 4 + [VMEM, A...  11.6 us
    pallas_call x1, Pallas kernels, backward(): pl.pallas_call(backward_kernel, in_specs=[SMEM, VMEM] + [ANY] * 4 + [VMEM...  11 us
    all_gather x1, blocking collectives, shards(): whole = lax.all_gather(plane, ('xl', 'core'))  9.4 us
    pallas_call x1, Pallas kernels, kernel_shares(): pl.pallas_call(kernel_share_kernel, in_specs=[SMEM, ANY, ANY, VMEM, VMEM]...  8.97 us
    pallas_call x1, Pallas kernels, pack(): pl.pallas_call(pack_kernel, in_specs=[SMEM] + [ANY] * 3, out_specs=[ANY]...  5.9 us
  transfers between devices with their start and end apart: 17, of which 8 were waited for; matrix products, arithmetic and copies ran while one was open for 4% of the time, Pallas kernels for 15%

profile of v4, /device:TPU:1, one launch (start us, length us, event | category | flops | bytes accessed | tf_op | source)
XLA Modules:
  0.0 165.1 jit_solution(14004668418448194717)
XLA Ops:
  0.6 5.9 %pack.1 = (bf16[128,2304]{1,0:T(8,128)(2,1)}, bf16[128,2304]{1,0:T(8,128)(2,1)}, bf16[128,2304]{1,0:T(8,128)(2,1)}, bf16[128,2304]{1,0:T(8,128)(2,1)}, bf16[512,1536]{1,0:T(8,128)(2,1)}) custom-call(s32[1]{0:T(128)} %bitcast.2.me_ref, bf16[512,1536]{1,0:T(8,128)(2,1)} %bitcast.23, bf16[512,1536]{1,0:T(8,128)(2,1)} %bitcast.21, bf16[768,1536]{1,0:T(8,128)(2,1)} %point_ref.3), custom_call_target="tpu_custom_call" | custom-call | flops 1207959552 | bytes 8000000 | tf_op jit(solution)/shard_map/pack/pallas_call | solution.py:97
  6.6 3.8 %collective-permute-start = (bf16[128,2304]{1,0:T(8,128)(2,1)}, bf16[128,2304]{1,0:T(8,128)(2,1)S(1)}, u32[]{:S(2)}, u32[]{:S(2)}) collective-permute-start(bf16[128,2304]{1,0:T(8,128)(2,1)} %get-tuple-element.59), channel_id=1, source_target_pairs={{0,32},{32,0},{64,96},{96,64},{1,33},{33,1},{65,97},{97,65},{2,34}... | collective-permute-start | bytes 1769480 | tf_op jit(solution)/shard_map/ppermute | solution.py:529
  10.4 2.7 %collective-permute-start.1 = (bf16[128,2304]{1,0:T(8,128)(2,1)}, bf16[128,2304]{1,0:T(8,128)(2,1)S(1)}, u32[]{:S(2)}, u32[]{:S(2)}) collective-permute-start(bf16[128,2304]{1,0:T(8,128)(2,1)} %get-tuple-element.60), channel_id=1, source_target_pairs={{0,64},{32,96},{64,0},{96,32},{1,65},{33,97},{65,1},{97,33},{2,66}... | collective-permute-start | bytes 1769480 | tf_op jit(solution)/shard_map/ppermute | solution.py:529
  13.8 9.6 %collective-permute-done.p1 = bf16[128,2304]{1,0:T(8,128)(2,1)S(1)} collective-permute-done((bf16[128,2304]{1,0:T(8,128)(2,1)}, bf16[128,2304]{1,0:T(8,128)(2,1)S(1)}, u32[]{:S(2)}, u32[]{:S(2)}) %collective-permute-start) | collective-permute-done | bytes 589856 | tf_op jit(solution)/shard_map/ppermute | solution.py:529
  23.4 2.6 %collective-permute-done.1.p2 = bf16[128,2304]{1,0:T(8,128)(2,1)S(1)} collective-permute-done((bf16[128,2304]{1,0:T(8,128)(2,1)}, bf16[128,2304]{1,0:T(8,128)(2,1)S(1)}, u32[]{:S(2)}, u32[]{:S(2)}) %collective-permute-start.1) | collective-permute-done | bytes 589856 | tf_op jit(solution)/shard_map/ppermute | solution.py:529
  26.0 12.6 %collective-permute-done.2.p3 = bf16[128,2304]{1,0:T(8,128)(2,1)S(1)} collective-permute-done((bf16[128,2304]{1,0:T(8,128)(2,1)}, bf16[128,2304]{1,0:T(8,128)(2,1)S(1)}, u32[]{:S(2)}, u32[]{:S(2)}) %collective-permute-start.2) | collective-permute-done | bytes 589856 | tf_op jit(solution)/shard_map/ppermute | solution.py:529
  39.4 11.6 %forward.1 = (bf16[512,1536]{1,0:T(8,128)(2,1)}, f32[512,1536]{1,0:T(8,128)}, f32[512,128]{1,0:T(8,128)}, bf16[128,768]{1,0:T(8,128)(2,1)}, bf16[128,768]{1,0:T(...) custom-call(s32[1]{0:T(128)} %bitcast.odd_ref, ...), custom_call_target="tpu_custom_call" | custom-call | flops 3623878656 | bytes 20000000 | tf_op jit(solution)/shard_map/forward/pallas_call | solution.py:177
  51.0 1.8 %collective-permute-start.3 = (bf16[512,1536]{1,0:T(8,128)(2,1)}, bf16[512,1536]{1,0:T(8,128)(2,1)S(1)}, u32[]{:S(2)}, u32[]{:S(2)}) collective-permute-start(bf16[512,1536]{1,0:T(8,128)(2,1)} %get-tuple-element.62.own_hbm), channel_id=1, source_target_pairs={{0,1},{1,0},{2,3},{3,2},{4,5},{5,4},{6,7},{7,6},{8,9},{9,8},{10,11... | collective-permute-start | bytes 4718600 | tf_op jit(solution)/shard_map/ppermute | solution.py:525
  52.9 3.7 %collective-permute-done.4.came_ref = bf16[512,384]{1,0:T(8,128)(2,1)S(1)} collective-permute-done((bf16[512,384]{1,0:T(8,128)(2,1)}, bf16[512,384]{1,0:T(8,128)(2,1)S(1)}, u32[]{:S(2)}, u32[]{:S(2)}) %collective-permute-start.4) | collective-permute-done | bytes 393248 | tf_op jit(solution)/shard_map/ppermute | solution.py:525
  57.9 9.0 %kernel_shares.1 = bf16[4,8,432,128]{3,2,1,0:T(8,128)(2,1)} custom-call(s32[1]{0:T(128)} %bitcast.odd_ref, bf16[512,1536]{1,0:T(8,128)(2,1)} %get-tuple-element.62.own_hbm, bf16[512,1536]{1,0:T(8,128)(2,1)} %copy-done.7, bf16[512,384]{1,0:T(8,128)(2,1)} %get-tuple-element.63.kept_ref, bf16[512,384]{1,0:T(8,128)(2,1)} %copy-done.8), custom_call_target="tpu_custom_call" | custom-call | flops 3623878656 | bytes 10000000 | tf_op jit(solution)/shard_map/kernel_shares/pallas_call | solution.py:322
  66.9 5.0 %all-to-all-start = ((bf16[4,8,432,128]{3,2,1,0:T(8,128)(2,1)}), bf16[4,8,432,128]{3,2,1,0:T(8,128)(2,1)S(1)}, u32[]{:S(2)}, u32[]{:S(2)}) async-start(bf16[4,8,432,128]{3,2,1,0:T(8,128)(2,1)} %kernel_shares.1), calls=%async_computation | async-start | bytes 7077888 | tf_op jit(solution)/shard_map/all_to_all | solution.py:559
  72.6 2.9 %collective-permute-start.6 = (bf16[128,768]{1,0:T(8,128)(2,1)}, bf16[128,768]{1,0:T(8,128)(2,1)}, u32[]{:S(2)}, u32[]{:S(2)}) collective-permute-start(bf16[128,768]{1,0:T(8,128)(2,1)} %get-tuple-element.77), channel_id=1, source_target_pairs={{0,32},{32,0},{64,96},{96,64},{1,33},{33,1},{65,97},{97,65},{2,34}... | collective-permute-start | bytes 589832 | tf_op jit(solution)/shard_map/ppermute | solution.py:529
  75.5 2.8 %collective-permute-start.7 = (bf16[128,768]{1,0:T(8,128)(2,1)}, bf16[128,768]{1,0:T(8,128)(2,1)}, u32[]{:S(2)}, u32[]{:S(2)}) collective-permute-start(bf16[128,768]{1,0:T(8,128)(2,1)} %get-tuple-element.78), channel_id=1, source_target_pairs={{0,64},{32,96},{64,0},{96,32},{1,65},{33,97},{65,1},{97,33},{2,66}... | collective-permute-start | bytes 589832 | tf_op jit(solution)/shard_map/ppermute | solution.py:529
  78.2 11.0 %backward.1 = (bf16[128,1536]{1,0:T(8,128)(2,1)}, bf16[128,1536]{1,0:T(8,128)(2,1)}, bf16[128,1536]{1,0:T(8,128)(2,1)}, bf16[128,1536]{1,0:T(8,128)(2,1)}, f32[1,1536]{1,0:T(1,128)}) custom-call(s32[1]{0:T(128)} %bitcast.odd_ref, bf16[512,768]{1,0:T(8,128)(2,1)} %get-tuple-element.72.grad_ref, bf16[128,2304]{1,0:T(8,128)(2,1)} %get-tuple-element.58.p0, ...), custom_call_target="tpu_custom_call" | custom-call | flops 1000000 | bytes 100000 | tf_op jit(solution)/shard_map/backward/pallas_call | solution.py:252
  89.3 0.9 constant_dynamic-update-slice_fusion.2
  90.3 0.9 constant_dynamic-update-slice_fusion.1
  91.2 0.9 constant_dynamic-update-slice_fusion
  92.2 1.0 broadcast_select_fusion
  93.1 0.8 collective-permute-start.9
  94.0 2.9 %collective-permute-start.10 = (bf16[128,1536]{1,0:T(8,128)(2,1)}, bf16[128,1536]{1,0:T(8,128)(2,1)}, u32[]{:S(2)}, u32[]{:S(2)}) collective-permute-start(bf16[128,1536]{1,0:T(8,128)(2,1)} %get-tuple-element.89), channel_id=1, source_target_pairs={{0,32},{32,0},{64,96},{96,64},{1,33},{33,1},{65,97},{97,65},{2,34}... | collective-permute-start | bytes 1179656 | tf_op jit(solution)/shard_map/ppermute | solution.py:529
  96.8 2.8 %collective-permute-start.11 = (bf16[128,1536]{1,0:T(8,128)(2,1)}, bf16[128,1536]{1,0:T(8,128)(2,1)}, u32[]{:S(2)}, u32[]{:S(2)}) collective-permute-start(bf16[128,1536]{1,0:T(8,128)(2,1)} %get-tuple-element.90), channel_id=1, source_target_pairs={{0,64},{32,96},{64,0},{96,32},{1,65},{33,97},{65,1},{97,33},{2,66}... | collective-permute-start | bytes 1179656 | tf_op jit(solution)/shard_map/ppermute | solution.py:529
  101.7 5.8 %point_shares.1 = (bf16[8,160,128]{2,1,0:T(8,128)(2,1)}, bf16[8,160,128]{2,1,0:T(8,128)(2,1)}, bf16[8,160,128]{2,1,0:T(8,128)(2,1)}, bf16[8,160,128]{2,1,0:T(8,128)(2,1)}) custom-call(s32[1]{0:T(128)} %bitcast.5.z_ref, bf16[512,1536]{1,0:T(8,128)(2,1)} %get-tuple-element.71.own_hbm, bf16[512,1536]{1,0:T(8,128)(2,1)} %collective-permute-done.5.other_hbm, ...), custom_call_target="tpu_custom_call" | custom-call | flops 1207959552 | bytes 6000000 | tf_op jit(solution)/shard_map/point_shares/pallas_call | solution.py:368
  107.5 1.5 collective-permute-done.11.b2
  109.1 1.7 %collective-permute-start.13 = (bf16[8,160,128]{2,1,0:T(8,128)(2,1)}, bf16[8,160,128]{2,1,0:T(8,128)(2,1)}, u32[]{:S(2)}, u32[]{:S(2)}) collective-permute-start(bf16[8,160,128]{2,1,0:T(8,128)(2,1)} %get-tuple-element.102), channel_id=1, source_target_pairs={{0,4},{4,8},{8,12},{12,0},{1,5},{5,9},{9,13},{13,1},{2,6},{6,10},{... | collective-permute-start | bytes 983048 | tf_op jit(solution)/shard_map/ppermute | solution.py:579
  110.8 2.4 %collective-permute-start.14 = (bf16[8,160,128]{2,1,0:T(8,128)(2,1)}, bf16[8,160,128]{2,1,0:T(8,128)(2,1)}, u32[]{:S(2)}, u32[]{:S(2)}) collective-permute-start(bf16[8,160,128]{2,1,0:T(8,128)(2,1)} %get-tuple-element.103), channel_id=1, source_target_pairs={{0,8},{4,12},{8,0},{12,4},{1,9},{5,13},{9,1},{13,5},{2,10},{6,14},... | collective-permute-start | bytes 983048 | tf_op jit(solution)/shard_map/ppermute | solution.py:579
  113.2 1.2 collective-permute-start.15
  114.4 2.9 %collective-permute-done.12.b3 = bf16[128,1536]{1,0:T(8,128)(2,1)} collective-permute-done((bf16[128,1536]{1,0:T(8,128)(2,1)}, bf16[128,1536]{1,0:T(8,128)(2,1)}, u32[]{:S(2)}, u32[]{:S(2)}) %collective-permute-start.12) | collective-permute-done | bytes 393248 | tf_op jit(solution)/shard_map/ppermute | solution.py:529
  117.3 2.8 %stream_grad.1 = bf16[512,1536]{1,0:T(8,128)(2,1)} custom-call(s32[1]{0:T(128)} %bitcast.2.me_ref, bf16[128,1536]{1,0:T(8,128)(2,1)} %get-tuple-element.97.b0, bf16[128,1536]{1,0:T(8,128)(2,1)} %collective-permute-done.10.b1, bf16[128,1536]{1,0:T(8,128)(2,1)} %collective-permute-done.11.b2, bf16[128,1536]{1,0:T(8,128)(2,1)} %collective-permute-done.12.b3, ...), custom_call_target="tpu_custom_call" | custom-call | flops 1572864 | bytes 5000000 | tf_op jit(solution)/shard_map/stream_grad/pallas_call | solution.py:507
  120.1 4.9 %stream_out.1 = bf16[512,1536]{1,0:T(8,128)(2,1)} custom-call(s32[1]{0:T(128)} %bitcast.2.me_ref, bf16[128,768]{1,0:T(8,128)(2,1)} %get-tuple-element.91.m0, bf16[128,768]{1,0:T(8,128)(2,1)} %collective-permute-done.6.m1, bf16[128,768]{1,0:T(8,128)(2,1)} %collective-permute-done.7.m2, bf16[128,768]{1,0:T(8,128)(2,1)} %collective-permute-done.8.m3, ...), custom_call_target="tpu_custom_call" | custom-call | flops 1207959552 | bytes 6000000 | tf_op jit(solution)/shard_map/stream_out/pallas_call | solution.py:463
  127.1 1.4 plane_shares.1
  128.5 24.3 %all_to_all.10 = bf16[16,304,128]{2,1,0:T(8,128)(2,1)S(1)} all-to-all(bf16[16,304,128]{2,1,0:T(8,128)(2,1)S(1)} %bitcast.20), channel_id=1, replica_groups=mesh['xh'=2,'yh'=2,'yl'=2,'z'=4,'xl'=2,'core'=2] {'xh','yh','yl','xl'}, dimensions={0} | all-to-all | bytes 2490368 | tf_op jit(solution)/shard_map/all_to_all | solution.py:587
  153.0 9.4 %all-gather = f32[1184,128]{1,0:T(8,128)S(1)} all-gather(f32[296,128]{1,0:T(8,128)S(1)} %slice.37), channel_id=2, replica_groups=mesh['xh'=2,'yh'=2,'yl'=2,'z'=4,'xl'=2,'core'=2] {'xl','core'}, dimensions={0}, use_global_device_ids=true | all-gather | bytes 757760 | tf_op jit(solution)/shard_map/all_gather | solution.py:589
  (48 shorter events, 10.5 us)
Async XLA Ops:
  0.6 12.5 %copy-start.5 = (f32[1536]{0:T(1024)S(1)}, f32[1536]{0:T(1024)}, u32[]{:S(2)}) copy-start(f32[1536]{0:T(1024)} %param.6) | copy-start | bytes 18436
  6.6 16.8 %collective-permute-start = (bf16[128,2304]{1,0:T(8,128)(2,1)}, bf16[128,2304]{1,0:T(8,128)(2,1)S(1)}, u32[]{:S(2)}, u32[]{:S(2)}) collective-permute-start(bf16[128,2304]{1,0:T(8,128)(2,1)} %get-tuple-element.59), channel_id=1, source_target_pairs={{0,32},{32,0},{64,96},{96,64},{1,33},{33,1},{65,97},{97,65},{2,34}... | collective-permute-start | bytes 1769480 | tf_op jit(solution)/shard_map/ppermute | solution.py:529
  10.4 15.6 %collective-permute-start.1 = (bf16[128,2304]{1,0:T(8,128)(2,1)}, bf16[128,2304]{1,0:T(8,128)(2,1)S(1)}, u32[]{:S(2)}, u32[]{:S(2)}) collective-permute-start(bf16[128,2304]{1,0:T(8,128)(2,1)} %get-tuple-element.60), channel_id=1, source_target_pairs={{0,64},{32,96},{64,0},{96,32},{1,65},{33,97},{65,1},{97,33},{2,66}... | collective-permute-start | bytes 1769480 | tf_op jit(solution)/shard_map/ppermute | solution.py:529
  13.1 25.4 %collective-permute-start.2 = (bf16[128,2304]{1,0:T(8,128)(2,1)}, bf16[128,2304]{1,0:T(8,128)(2,1)S(1)}, u32[]{:S(2)}, u32[]{:S(2)}) collective-permute-start(bf16[128,2304]{1,0:T(8,128)(2,1)} %get-tuple-element.61), channel_id=1, source_target_pairs={{0,96},{32,64},{64,32},{96,0},{1,97},{33,65},{65,33},{97,1},{2,98}... | collective-permute-start | bytes 1769480 | tf_op jit(solution)/shard_map/ppermute | solution.py:529
  23.4 15.2 %copy-start.2 = (bf16[128,2304]{1,0:T(8,128)(2,1)}, bf16[128,2304]{1,0:T(8,128)(2,1)S(1)}, u32[]{:S(2)}) copy-start(bf16[128,2304]{1,0:T(8,128)(2,1)S(1)} %collective-permute-done.p1) | copy-start | bytes 1769476
  26.0 12.6 %copy-start.3 = (bf16[128,2304]{1,0:T(8,128)(2,1)}, bf16[128,2304]{1,0:T(8,128)(2,1)S(1)}, u32[]{:S(2)}) copy-start(bf16[128,2304]{1,0:T(8,128)(2,1)S(1)} %collective-permute-done.1.p2) | copy-start | bytes 1769476
  38.6 0.8 copy-start.4
  51.0 5.6 %collective-permute-start.3 = (bf16[512,1536]{1,0:T(8,128)(2,1)}, bf16[512,1536]{1,0:T(8,128)(2,1)S(1)}, u32[]{:S(2)}, u32[]{:S(2)}) collective-permute-start(bf16[512,1536]{1,0:T(8,128)(2,1)} %get-tuple-element.62.own_hbm), channel_id=1, source_target_pairs={{0,1},{1,0},{2,3},{3,2},{4,5},{5,4},{6,7},{7,6},{8,9},{9,8},{10,11... | collective-permute-start | bytes 4718600 | tf_op jit(solution)/shard_map/ppermute | solution.py:525
  52.8 3.8 %collective-permute-start.4 = (bf16[512,384]{1,0:T(8,128)(2,1)}, bf16[512,384]{1,0:T(8,128)(2,1)S(1)}, u32[]{:S(2)}, u32[]{:S(2)}) collective-permute-start(bf16[512,384]{1,0:T(8,128)(2,1)} %get-tuple-element.64), channel_id=1, source_target_pairs={{0,1},{1,0},{2,3},{3,2},{4,5},{5,4},{6,7},{7,6},{8,9},{9,8},{10,11... | collective-permute-start | bytes 1179656 | tf_op jit(solution)/shard_map/ppermute | solution.py:525
  56.6 0.7 copy-start.8
  56.6 1.3 copy-start.7
  66.9 58.1 %all-to-all-start = ((bf16[4,8,432,128]{3,2,1,0:T(8,128)(2,1)}), bf16[4,8,432,128]{3,2,1,0:T(8,128)(2,1)S(1)}, u32[]{:S(2)}, u32[]{:S(2)}) async-start(bf16[4,8,432,128]{3,2,1,0:T(8,128)(2,1)} %kernel_shares.1), calls=%async_computation | async-start | bytes 7077888 | tf_op jit(solution)/shard_map/all_to_all | solution.py:559
  71.9 29.8 %collective-permute-start.5 = (bf16[512,1536]{1,0:T(8,128)(2,1)}, bf16[512,1536]{1,0:T(8,128)(2,1)}, u32[]{:S(2)}, u32[]{:S(2)}) collective-permute-start(bf16[512,1536]{1,0:T(8,128)(2,1)} %get-tuple-element.71.own_hbm), channel_id=1, source_target_pairs={{0,1},{1,0},{2,3},{3,2},{4,5},{5,4},{6,7},{7,6},{8,9},{9,8},{10,11... | collective-permute-start | bytes 4718600 | tf_op jit(solution)/shard_map/ppermute | solution.py:525
  72.6 16.7 %collective-permute-start.6 = (bf16[128,768]{1,0:T(8,128)(2,1)}, bf16[128,768]{1,0:T(8,128)(2,1)}, u32[]{:S(2)}, u32[]{:S(2)}) collective-permute-start(bf16[128,768]{1,0:T(8,128)(2,1)} %get-tuple-element.77), channel_id=1, source_target_pairs={{0,32},{32,0},{64,96},{96,64},{1,33},{33,1},{65,97},{97,65},{2,34}... | collective-permute-start | bytes 589832 | tf_op jit(solution)/shard_map/ppermute | solution.py:529
  75.5 13.8 %collective-permute-start.7 = (bf16[128,768]{1,0:T(8,128)(2,1)}, bf16[128,768]{1,0:T(8,128)(2,1)}, u32[]{:S(2)}, u32[]{:S(2)}) collective-permute-start(bf16[128,768]{1,0:T(8,128)(2,1)} %get-tuple-element.78), channel_id=1, source_target_pairs={{0,64},{32,96},{64,0},{96,32},{1,65},{33,97},{65,1},{97,33},{2,66}... | collective-permute-start | bytes 589832 | tf_op jit(solution)/shard_map/ppermute | solution.py:529
  78.2 11.0 %collective-permute-start.8 = (bf16[128,768]{1,0:T(8,128)(2,1)}, bf16[128,768]{1,0:T(8,128)(2,1)}, u32[]{:S(2)}, u32[]{:S(2)}) collective-permute-start(bf16[128,768]{1,0:T(8,128)(2,1)} %get-tuple-element.79), channel_id=1, source_target_pairs={{0,96},{32,64},{64,32},{96,0},{1,97},{33,65},{65,33},{97,1},{2,98}... | collective-permute-start | bytes 589832 | tf_op jit(solution)/shard_map/ppermute | solution.py:529
  78.2 11.0 %copy-start.1 = (bf16[128,768]{1,0:T(8,128)(2,1)S(1)}, bf16[128,768]{1,0:T(8,128)(2,1)}, u32[]{:S(2)}) copy-start(bf16[128,768]{1,0:T(8,128)(2,1)} %get-tuple-element.91.m0) | copy-start | bytes 589828
  89.3 10.3 %copy-start.6 = (f32[1,1536]{1,0:T(1,128)S(1)}, f32[1,1536]{1,0:T(1,128)}, u32[]{:S(2)}) copy-start(f32[1,1536]{1,0:T(1,128)} %get-tuple-element.84) | copy-start | bytes 18436
  93.1 8.6 %collective-permute-start.9 = (bf16[512,384]{1,0:T(8,128)(2,1)}, bf16[512,384]{1,0:T(8,128)(2,1)}, u32[]{:S(2)}, u32[]{:S(2)}) collective-permute-start(bf16[512,384]{1,0:T(8,128)(2,1)} %get-tuple-element.111), channel_id=1, source_target_pairs={{0,1},{1,0},{2,3},{3,2},{4,5},{5,4},{6,7},{7,6},{8,9},{9,8},{10,11... | collective-permute-start | bytes 1179656 | tf_op jit(solution)/shard_map/ppermute | solution.py:525
  94.0 13.6 %collective-permute-start.10 = (bf16[128,1536]{1,0:T(8,128)(2,1)}, bf16[128,1536]{1,0:T(8,128)(2,1)}, u32[]{:S(2)}, u32[]{:S(2)}) collective-permute-start(bf16[128,1536]{1,0:T(8,128)(2,1)} %get-tuple-element.89), channel_id=1, source_target_pairs={{0,32},{32,0},{64,96},{96,64},{1,33},{33,1},{65,97},{97,65},{2,34}... | collective-permute-start | bytes 1179656 | tf_op jit(solution)/shard_map/ppermute | solution.py:529
  96.8 12.2 %collective-permute-start.11 = (bf16[128,1536]{1,0:T(8,128)(2,1)}, bf16[128,1536]{1,0:T(8,128)(2,1)}, u32[]{:S(2)}, u32[]{:S(2)}) collective-permute-start(bf16[128,1536]{1,0:T(8,128)(2,1)} %get-tuple-element.90), channel_id=1, source_target_pairs={{0,64},{32,96},{64,0},{96,32},{1,65},{33,97},{65,1},{97,33},{2,66}... | collective-permute-start | bytes 1179656 | tf_op jit(solution)/shard_map/ppermute | solution.py:529
  99.6 17.7 %collective-permute-start.12 = (bf16[128,1536]{1,0:T(8,128)(2,1)}, bf16[128,1536]{1,0:T(8,128)(2,1)}, u32[]{:S(2)}, u32[]{:S(2)}) collective-permute-start(bf16[128,1536]{1,0:T(8,128)(2,1)} %get-tuple-element.100), channel_id=1, source_target_pairs={{0,96},{32,64},{64,32},{96,0},{1,97},{33,65},{65,33},{97,1},{2,98}... | collective-permute-start | bytes 1179656 | tf_op jit(solution)/shard_map/ppermute | solution.py:529
  109.1 16.7 %collective-permute-start.13 = (bf16[8,160,128]{2,1,0:T(8,128)(2,1)}, bf16[8,160,128]{2,1,0:T(8,128)(2,1)}, u32[]{:S(2)}, u32[]{:S(2)}) collective-permute-start(bf16[8,160,128]{2,1,0:T(8,128)(2,1)} %get-tuple-element.102), channel_id=1, source_target_pairs={{0,4},{4,8},{8,12},{12,0},{1,5},{5,9},{9,13},{13,1},{2,6},{6,10},{... | collective-permute-start | bytes 983048 | tf_op jit(solution)/shard_map/ppermute | solution.py:579
  110.8 15.7 %collective-permute-start.14 = (bf16[8,160,128]{2,1,0:T(8,128)(2,1)}, bf16[8,160,128]{2,1,0:T(8,128)(2,1)}, u32[]{:S(2)}, u32[]{:S(2)}) collective-permute-start(bf16[8,160,128]{2,1,0:T(8,128)(2,1)} %get-tuple-element.103), channel_id=1, source_target_pairs={{0,8},{4,12},{8,0},{12,4},{1,9},{5,13},{9,1},{13,5},{2,10},{6,14},... | collective-permute-start | bytes 983048 | tf_op jit(solution)/shard_map/ppermute | solution.py:579
  113.2 13.9 %collective-permute-start.15 = (bf16[8,160,128]{2,1,0:T(8,128)(2,1)}, bf16[8,160,128]{2,1,0:T(8,128)(2,1)}, u32[]{:S(2)}, u32[]{:S(2)}) collective-permute-start(bf16[8,160,128]{2,1,0:T(8,128)(2,1)} %get-tuple-element.104), channel_id=1, source_target_pairs={{0,12},{4,0},{8,4},{12,8},{1,13},{5,1},{9,5},{13,9},{2,14},{6,2},{... | collective-permute-start | bytes 983048 | tf_op jit(solution)/shard_map/ppermute | solution.py:579
  125.0 2.0 %copy-start = (bf16[8,160,128]{2,1,0:T(8,128)(2,1)S(1)}, bf16[8,160,128]{2,1,0:T(8,128)(2,1)}, u32[]{:S(2)}) copy-start(bf16[8,160,128]{2,1,0:T(8,128)(2,1)} %get-tuple-element.107.d0) | copy-start | bytes 983044

commit v5 on v4

--- a/solution.py
+++ b/solution.py
@@ -61,62 +61,9 @@
     ]
 
 
-def pack_kernel(
-    me_ref, stream_ref, cotan_ref, point_ref, p0, p1, p2, p3, turned_ref,
-    rows_in, turned, point, grads, in_sems, point_sem, out_sems,
-):
-    me = me_ref[0]
-    weights = pltpu.make_async_copy(point_ref, point, point_sem)
-    cotans, streams = [], []
-    for k in range(4):
-        rows = pl.ds(pl.multiple_of(lax.bitwise_xor(me, k) * Q, Q), Q)
-        at = pl.ds(k * Q, Q)
-        cotans.append(pltpu.make_async_copy(cotan_ref.at[rows], turned.at[at], in_sems.at[k]))
-        streams.append(pltpu.make_async_copy(stream_ref.at[rows], rows_in.at[at], in_sems.at[4 + k]))
-    for copy in cotans + [weights] + streams:
-        copy.start()
-    for copy in cotans:
-        copy.wait()
-    outs = [pltpu.make_async_copy(turned, turned_ref, out_sems.at[8])]
-    outs[0].start()
-    weights.wait()
-    grads[...] = contract_cols(turned[...], point[...]).astype(BF16)
-    for k, out in enumerate((p0, p1, p2, p3)):
-        at = pl.ds(k * Q, Q)
-        streams[k].wait()
-        outs.append(pltpu.make_async_copy(rows_in.at[at], out.at[:, pl.ds(0, C)], out_sems.at[k]))
-        outs.append(pltpu.make_async_copy(grads.at[at], out.at[:, pl.ds(C, H)], out_sems.at[4 + k]))
-    for copy in outs[1:]:
-        copy.start()
-    for copy in outs:
-        copy.wait()
-
-
-def pack(me, stream, cotan, point_kernel):
-    shape = jax.ShapeDtypeStruct
-    return pl.pallas_call(
-        pack_kernel,
-        in_specs=[SMEM] + [ANY] * 3,
-        out_specs=[ANY] * 5,
-        out_shape=[shape((Q, C + H), BF16)] * 4 + [shape((N, C), BF16)],
-        scratch_shapes=[
-            pltpu.VMEM((N, C), BF16),
-            pltpu.VMEM((N, C), BF16),
-            pltpu.VMEM((H, C), BF16),
-            pltpu.VMEM((N, H), BF16),
-            pltpu.SemaphoreType.DMA((8,)),
-            pltpu.SemaphoreType.DMA,
-            pltpu.SemaphoreType.DMA((9,)),
-        ],
-        compiler_params=params(56),
-        cost_estimate=cost(2 * N * C * H, 8_000_000),
-        name="pack",
-    )(me, stream, cotan, point_kernel)
-
-
 def forward_kernel(
-    odd_ref, core_ref, p0, p1, p2, p3, gain_ref, weights_ref,
-    act_out, slope_out, inv_out, m0, m1, m2, m3, all_ref, kept_ref, away_ref,
+    odd_ref, p0, p3, p1, p2, gain_ref, weights_ref,
+    act_out, slope_out, inv_out, m0, m1, m2, m3, slope_ref,
     packed, ring, held, slope_in, inv_in, sems, in_sems, out_sems,
 ):
     ins = [
@@ -126,14 +73,13 @@
     copies = taps_in(odd_ref, weights_ref, held, sems)
     for copy in ins + copies:
         copy.start()
-    core = core_ref[0]
     step = 64
     for k in range(4):
         ins[k].wait()
 
         def some(i, carry, k=k):
             at = pl.ds(pl.multiple_of(i * step, step), step)
-            rows = packed[k, at, :C].astype(F32)
+            rows = packed[k, at, :].astype(F32)
             inv = lax.rsqrt(jnp.mean(rows * rows, axis=-1, keepdims=True) + 1e-06)
             act, slope = gelu_both(rows * inv * gain_ref[...])
             here = pl.ds(pl.multiple_of(k * Q + i * step, step), step)
@@ -160,29 +106,25 @@
         pre = pre + dot(ring[:4 * Q], held[0, :, cols])
         pre = pre + dot(ring[2 * Q:], held[2, :, cols])
         mid, slope = gelu_both(pre)
+        slope_ref[:, cols] = slope
         for k, out in enumerate((m0, m1, m2, m3)):
             at = slice(k * Q, (k + 1) * Q)
             out[:, cols] = mid[at].astype(BF16)
-            grad = packed[k, :, C + n * 256:C + n * 256 + 256].astype(F32)
-            all_ref[at, cols] = (grad * slope[at]).astype(BF16)
-    low, high = all_ref[:, :HALF], all_ref[:, HALF:]
-    kept_ref[...] = jnp.where(core == 0, low, high)
-    away_ref[...] = jnp.where(core == 0, high, low)
     for copy in outs:
         copy.wait()
 
 
-def forward(odd, core, pieces, gain, weights):
+def forward(odd, pieces, gain, weights):
     shape = jax.ShapeDtypeStruct
     return pl.pallas_call(
         forward_kernel,
-        in_specs=[SMEM] * 2 + [ANY] * 4 + [VMEM, ANY],
-        out_specs=[ANY] * 3 + [VMEM] * 7,
+        in_specs=[SMEM] + [ANY] * 4 + [VMEM, ANY],
+        out_specs=[ANY] * 3 + [VMEM] * 5,
         out_shape=[shape((N, C), BF16), shape((N, C), F32), shape((N, 128), F32)]
         + [shape((Q, H), BF16)] * 4
-        + [shape((N, H), BF16), shape((N, HALF), BF16), shape((N, HALF), BF16)],
+        + [shape((N, H), F32)],
         scratch_shapes=[
-            pltpu.VMEM((4, Q, C + H), BF16),
+            pltpu.VMEM((4, Q, C), BF16),
             pltpu.VMEM((6 * Q, C), BF16),
             pltpu.VMEM((3, C, H), BF16),
             pltpu.VMEM((N, C), F32),
@@ -194,7 +136,32 @@
         compiler_params=params(56),
         cost_estimate=cost(6 * N * C * H, 20_000_000),
         name="forward",
-    )(odd, core, *pieces, gain, weights)
+    )(odd, pieces[0], pieces[3], pieces[1], pieces[2], gain, weights)
+
+
+def pre_grad_kernel(me_ref, core_ref, grad_ref, slope_ref, all_ref, kept_ref, away_ref):
+    me, core = me_ref[0], core_ref[0]
+    for k in range(4):
+        at = slice(k * Q, (k + 1) * Q)
+        grad = grad_ref[lax.bitwise_xor(me, k)].astype(F32)
+        value = (grad * slope_ref[at, :]).astype(BF16)
+        all_ref[at, :] = value
+        low, high = value[:, :HALF], value[:, HALF:]
+        kept_ref[at, :] = jnp.where(core == 0, low, high)
+        away_ref[at, :] = jnp.where(core == 0, high, low)
+
+
+def pre_grads(me, core, grads, slope):
+    shape = jax.ShapeDtypeStruct
+    return pl.pallas_call(
+        pre_grad_kernel,
+        in_specs=[SMEM] * 2 + [VMEM] * 2,
+        out_specs=[VMEM] * 3,
+        out_shape=[shape((N, H), BF16), shape((N, HALF), BF16), shape((N, HALF), BF16)],
+        compiler_params=params(56),
+        cost_estimate=cost(30_000_000_000, 5_000_000),
+        name="pre_grads",
+    )(me, core, grads, slope)
 
 
 def backward_kernel(
@@ -210,7 +177,7 @@
         pltpu.make_async_copy(slope_hbm, slope_ref, in_sems.at[0]),
         pltpu.make_async_copy(inv_hbm, inv_ref, in_sems.at[1]),
     ] + [
-        pltpu.make_async_copy(source.at[:, pl.ds(0, C)], rows_in.at[k], in_sems.at[2 + k])
+        pltpu.make_async_copy(source, rows_in.at[k], in_sems.at[2 + k])
         for k, source in enumerate((p0, p1, p2, p3))
     ]
     for copy in ins:
@@ -270,13 +237,13 @@
     )(odd, grads, *pieces, gain, slope, inv, weights)
 
 
-def load_columns(own_hbm, other_hbm, own, other, sems):
+def load_columns(own_hbm, other_hbm, both, sems):
     ins = []
     for i in range(4):
         cols = pl.ds(i * HALF, HALF)
         ins.append((
-            pltpu.make_async_copy(own_hbm.at[:, cols], own.at[i], sems.at[2 * i]),
-            pltpu.make_async_copy(other_hbm.at[:, cols], other.at[i], sems.at[2 * i + 1]),
+            pltpu.make_async_copy(own_hbm.at[:, cols], both.at[i, pl.ds(0, N)], sems.at[2 * i]),
+            pltpu.make_async_copy(other_hbm.at[:, cols], both.at[i, pl.ds(N, N)], sems.at[2 * i + 1]),
         ))
         for copy in ins[-1]:
             copy.start()
@@ -285,26 +252,31 @@
 
 def kernel_share_kernel(
     odd_ref, own_hbm, other_hbm, kept_ref, came_ref, out_ref,
-    own, other, right, ring, value, in_sems, out_sems,
+    both, right, rings, value, ring_sems, in_sems, out_sems,
 ):
-    ins = load_columns(own_hbm, other_hbm, own, other, in_sems)
+    rows_in = [
+        pltpu.make_async_copy(source, rings.at[i, pl.ds(Q, N)], ring_sems.at[i])
+        for i, source in enumerate((kept_ref, came_ref))
+    ]
+    for copy in rows_in:
+        copy.start()
+    ins = load_columns(own_hbm, other_hbm, both, in_sems)
     odd = odd_ref[0]
     near = pl.multiple_of(jnp.where(odd == 0, 2 * Q, 0), Q)
     far = pl.multiple_of(jnp.where(odd == 0, 0, 2 * Q), Q)
-    for i, source in enumerate((kept_ref, came_ref)):
-        ring[Q:5 * Q] = source[...]
-        ring[:Q] = source[3 * Q:]
-        ring[5 * Q:] = source[:Q]
+    for i in range(2):
+        rows_in[i].wait()
+        rings[i, :Q] = rings[i, 4 * Q:5 * Q]
+        rings[i, 5 * Q:] = rings[i, Q:2 * Q]
         rows = slice(i * N, (i + 1) * N)
-        right[rows, :HALF] = ring[pl.ds(near, N), :]
-        right[rows, HALF:2 * HALF] = source[...]
-        right[rows, 2 * HALF:] = ring[pl.ds(far, N), :]
+        right[rows, :HALF] = rings[i, pl.ds(near, N), :]
+        right[rows, HALF:2 * HALF] = rings[i, Q:5 * Q]
+        right[rows, 2 * HALF:] = rings[i, pl.ds(far, N), :]
     outs = []
     for i in range(4):
         for copy in ins[i]:
             copy.wait()
-        part = contract_rows(own[i], right[:N]) + contract_rows(other[i], right[N:])
-        part = part.astype(BF16)
+        part = contract_rows(both[i], right[...]).astype(BF16)
         for b in range(9):
             value[2 * i:2 * i + 2, :, 48 * b:48 * b + 48, :] = part[
                 :, 128 * b:128 * b + 128
@@ -321,15 +293,15 @@
 def kernel_shares(odd, own, other, kept, came):
     return pl.pallas_call(
         kernel_share_kernel,
-        in_specs=[SMEM, ANY, ANY, VMEM, VMEM],
+        in_specs=[SMEM] + [ANY] * 4,
         out_specs=ANY,
         out_shape=jax.ShapeDtypeStruct((4, 8, 432, 128), BF16),
         scratch_shapes=[
-            pltpu.VMEM((4, N, HALF), BF16),
-            pltpu.VMEM((4, N, HALF), BF16),
+            pltpu.VMEM((4, 2 * N, HALF), BF16),
             pltpu.VMEM((2 * N, 3 * HALF), BF16),
-            pltpu.VMEM((6 * Q, HALF), BF16),
+            pltpu.VMEM((2, 6 * Q, HALF), BF16),
             pltpu.VMEM((8, 4, 432, 128), BF16),
+            pltpu.SemaphoreType.DMA((2,)),
             pltpu.SemaphoreType.DMA((8,)),
             pltpu.SemaphoreType.DMA((8,)),
         ],
@@ -340,17 +312,31 @@
 
 
 def point_share_kernel(
-    z_ref, own_hbm, other_hbm, kept_ref, came_ref, gain_ref, d0, d1, d2, d3,
-    own, other, value, in_sems, out_sems,
+    z_ref, me_ref, own_hbm, other_hbm, kept_ref, came_ref, gain_ref, d0, d1, d2, d3,
+    both, right, value, in_sems, out_sems,
 ):
-    ins = load_columns(own_hbm, other_hbm, own, other, in_sems)
+    ins = []
+    for i in range(4):
+        cols = pl.ds(i * HALF, HALF)
+        ins.append([
+            pltpu.make_async_copy(
+                source.at[home_rows(me_ref, k), cols],
+                both.at[i, pl.ds(side * N + k * Q, Q)],
+                in_sems.at[8 * i + 4 * side + k],
+            )
+            for side, source in enumerate((own_hbm, other_hbm))
+            for k in range(4)
+        ])
+        for copy in ins[-1]:
+            copy.start()
     value[:, :, 144:] = gain_ref[...]
+    right[:N] = kept_ref[...]
+    right[N:] = came_ref[...]
     outs = []
     for i in range(4):
         for copy in ins[i]:
             copy.wait()
-        part = contract_rows(own[i], kept_ref[...]) + contract_rows(other[i], came_ref[...])
-        part = part.astype(BF16)
+        part = contract_rows(both[i], right[...]).astype(BF16)
         for b in range(3):
             value[2 * i:2 * i + 2, :, 48 * b:48 * b + 48, :] = part[
                 :, 128 * b:128 * b + 128
@@ -364,23 +350,23 @@
         copy.wait()
 
 
-def point_shares(z, own, other, kept, came, gain):
+def point_shares(z, me, own, other, kept, came, gain):
     return pl.pallas_call(
         point_share_kernel,
-        in_specs=[SMEM, ANY, ANY, VMEM, VMEM, VMEM],
+        in_specs=[SMEM, SMEM, ANY, ANY, VMEM, VMEM, VMEM],
         out_specs=[ANY] * 4,
         out_shape=[jax.ShapeDtypeStruct((8, 160, 128), BF16)] * 4,
         scratch_shapes=[
-            pltpu.VMEM((4, N, HALF), BF16),
-            pltpu.VMEM((4, N, HALF), BF16),
+            pltpu.VMEM((4, 2 * N, HALF), BF16),
+            pltpu.VMEM((2 * N, HALF), BF16),
             pltpu.VMEM((8, 4, 160, 128), BF16),
-            pltpu.SemaphoreType.DMA((8,)),
+            pltpu.SemaphoreType.DMA((32,)),
             pltpu.SemaphoreType.DMA((32,)),
         ],
         compiler_params=params(56),
         cost_estimate=cost(2 * N * C * H, 6_000_000),
         name="point_shares",
-    )(z, own, other, kept, came, gain)
+    )(z, me, own, other, kept, came, gain)
 
 
 def four_sum(a, b, c, d):
@@ -542,14 +528,19 @@
     gain_row = norm_gain_vector.reshape(1, C)
     cotan = out_grad[0]
 
-    packed = pack(me.reshape(1), stream[0], cotan, point_kernel)
-    pieces = exchange(packed[:4])
-    cotan_turned = packed[4]
-    cotan_other = swap_core(cotan_turned)
-
-    act, slope_in, inv, m0, m1, m2, m3, pre_grad, kept, away = forward(
-        odd_word, core_word, pieces, gain_row, conv_kernel
-    )
+    me_word = me.reshape(1)
+    quarters = stream[0].reshape(4, Q, C)
+    pieces = exchange([lax.dynamic_index_in_dim(quarters, me ^ k, 0, False) for k in range(4)])
+    mid_grad = contract_cols(cotan, point_kernel).astype(BF16).reshape(4, Q, H)
+    _, *pieces = lax.optimization_barrier((mid_grad, *pieces))
+    mid_grad = lax.all_to_all(mid_grad, GROUP, 0, 0, tiled=True)
+    cotan_other = swap_core(cotan)
+
+    act, slope_in, inv, m0, m1, m2, m3, slope = forward(
+        odd_word, pieces, gain_row, conv_kernel
+    )
+    mid_grad, slope = lax.optimization_barrier((mid_grad, slope))
+    pre_grad, kept, away = pre_grads(me_word, core_word, mid_grad, slope)
     act_other = swap_core(act)
     came = swap_core(away)
     shares = kernel_shares(odd_word, act, act_other, kept, came)
@@ -570,7 +561,7 @@
     gain = gain.astype(BF16).reshape(8, 4, 1, 48)
     gain = jnp.pad(gain, ((0, 0), (0, 0), (0, 15), (0, 80)))
     points = list(
-        point_shares(z_word, cotan_turned, cotan_other, mid_kept, mid_came, gain)
+        point_shares(z_word, me_word, cotan, cotan_other, mid_kept, mid_came, gain)
     )
     points[0], points[1], points[2], points[3], back[1], back[2], *mid = lax.optimization_barrier(
         (*points, back[1], back[2], *mid)
@@ -578,10 +569,10 @@
     points = [points[0]] + [
         lax.ppermute(points[d], "z", [(i, (i + d) % 4) for i in range(4)]) for d in (1, 2, 3)
     ]
-    stream_out = home_stream_out(me.reshape(1), mid, point_kernel, stream[0])
+    stream_out = home_stream_out(me_word, mid, point_kernel, stream[0])
     shares, stream_out = lax.optimization_barrier((shares, stream_out))
     taps = tap_sums(shares)
-    stream_grad = home_stream_grad(me.reshape(1), back, cotan)
+    stream_grad = home_stream_grad(me_word, back, cotan)
     taps, stream_grad, *points = lax.optimization_barrier((taps, stream_grad, *points))
     plane = plane_shares(taps, points).reshape(16, 304, 128)
     plane = lax.all_to_all(plane, PLANE, 0, 0, tiled=True)

time: 166 us -> 157 us (0.946)
  waiting for transfers between devices: 34.2 us -> 12.9 us
  starting transfers between devices: 31.7 us -> 39.8 us
  matrix products: 0 us -> 3.73 us
  local copies, waits for them, and re-layouts: 9.19 us -> 12.3 us
  Pallas kernels: 53.1 us -> 50.1 us
    ppermute x9, waiting for transfers between devices: 29.3 us -> 9.8 us  [partner(): return lax.ppermute(value, GROUP, [(i, i ^ k) for i in range(4)])]
    all_to_all x0 -> x1, starting transfers between devices: none -> 6.78 us  [shards(): mid_grad = lax.all_to_all(mid_grad, GROUP, 0, 0, tiled=True)]
    dot_general x0 -> x1, matrix products: none -> 3.73 us  [contract_cols(): lax.dot_general(left, right, (((1,), (1,)), ((), ())), preferred_element_...]
    pallas_call x4, Pallas kernels: 32.3 us -> 29.2 us  [the longest x1 11.3 us: forward(): pl.pallas_call(forward_kernel, in_specs=[SMEM] + [ANY] * 4 + [VMEM, ANY],...]
    squeeze x0 -> x1, local copies, waits for them, and re-layouts: none -> 2.36 us  [shards(): lax.dynamic_index_in_dim(quarters, me ^ k, 0, False)]
    ppermute x4, waiting for transfers between devices: 3.72 us -> 1.92 us  [swap_core(): return lax.ppermute(value, 'core', [(0, 1), (1, 0)])]
    unnamed x21 -> x25, local copies, waits for them, and re-layouts: 4.05 us -> 4.82 us
  transfers between devices with their start and end apart: 17 -> 18, of which waited for: 8 -> 6; matrix products, arithmetic and copies ran while one was open for 4% -> 7% of each run, Pallas kernels for 15% -> 26%
where the time goes in v5:
time: 157 us; the launch traced here: 156 us
  Pallas kernels  50.1 us (32%)
  starting transfers between devices  39.8 us (25%)
  blocking collectives  34 us (22%)
  waiting for transfers between devices  12.9 us (8%)
  local copies, waits for them, and re-layouts  12.3 us (8%)
  matrix products  3.73 us (2%)
  other arithmetic  2.27 us (1%)
    all_to_all x1, blocking collectives, shards(): plane = lax.all_to_all(plane, PLANE, 0, 0, tiled=True)  24.9 us
    ppermute x9, starting transfers between devices, partner(): return lax.ppermute(value, GROUP, [(i, i ^ k) for i in range(4)])  18.7 us
    pallas_call x1, Pallas kernels, forward(): pl.pallas_call(forward_kernel, in_specs=[SMEM] + [ANY] * 4 + [VMEM, ANY],...  11.3 us
    pallas_call x1, Pallas kernels, backward(): pl.pallas_call(backward_kernel, in_specs=[SMEM, VMEM] + [ANY] * 4 + [VMEM...  11 us
    ppermute x9, waiting for transfers between devices, partner(): return lax.ppermute(value, GROUP, [(i, i ^ k) for i in range(4)])  9.8 us
    all_gather x1, blocking collectives, shards(): whole = lax.all_gather(plane, ('xl', 'core'))  9.19 us
    pallas_call x1, Pallas kernels, kernel_shares(): pl.pallas_call(kernel_share_kernel, in_specs=[SMEM] + [ANY] * 4, out_spec...  8.81 us
    all_to_all x1, starting transfers between devices, shards(): mid_grad = lax.all_to_all(mid_grad, GROUP, 0, 0, tiled=True)  6.78 us
  transfers between devices with their start and end apart: 18, of which 6 were waited for; matrix products, arithmetic and copies ran while one was open for 7% of the time, Pallas kernels for 26%

profile of v5, /device:TPU:1, one launch (start us, length us, event | category | flops | bytes accessed | tf_op | source)
XLA Modules:
  0.0 155.9 jit_solution(5864223051351028727)
XLA Ops:
  0.7 2.4 %dynamic-slice_bitcast_fusion = (bf16[128,1536]{1,0:T(8,128)(2,1)S(1)}, bf16[128,1536]{1,0:T(8,128)(2,1)S(1)}, bf16[128,1536]{1,0:T(8,128)(2,1)S(1)}, bf16[128,1536]{1,0:T(8,128)(2,1)}) fusion(bf16[4,128,1536]{2,1,0:T(8,128)(2,1)} %bitcast.34, s32[]{:T(128)S(6)} %select_n.28, s32[]{:T(128)S(6)} %select_n.27, s32[]{:T(128)S(6)} %select_n.26, s32[]{:T(128)S(6)} %select_n.25), kind=kLoop, calls=%fused_computation.3 | loop fusion | bytes 3145744 | tf_op jit(solution)/shard_map/jit(dynamic_index_in_dim)/squeeze | solution.py:533
  3.0 3.7 %collective-permute-start = (bf16[128,1536]{1,0:T(8,128)(2,1)S(1)}, bf16[128,1536]{1,0:T(8,128)(2,1)S(1)}, u32[]{:S(2)}, u32[]{:S(2)}) collective-permute-start(bf16[128,1536]{1,0:T(8,128)(2,1)S(1)} %get-tuple-element.117), channel_id=1, source_target_pairs={{0,32},{32,0},{64,96},{96,64},{1,33},{33,1},{65,97},{97,65},{2,34}... | collective-permute-start | bytes 1179656 | tf_op jit(solution)/shard_map/ppermute | solution.py:515
  6.8 2.7 %collective-permute-start.1 = (bf16[128,1536]{1,0:T(8,128)(2,1)S(1)}, bf16[128,1536]{1,0:T(8,128)(2,1)S(1)}, u32[]{:S(2)}, u32[]{:S(2)}) collective-permute-start(bf16[128,1536]{1,0:T(8,128)(2,1)S(1)} %get-tuple-element.116), channel_id=1, source_target_pairs={{0,64},{32,96},{64,0},{96,32},{1,65},{33,97},{65,1},{97,33},{2,66}... | collective-permute-start | bytes 1179656 | tf_op jit(solution)/shard_map/ppermute | solution.py:515
  9.5 3.7 %convolution_convert_fusion = bf16[512,768]{1,0:T(8,128)(2,1)} fusion(bf16[768,1536]{1,0:T(8,128)(2,1)S(1)} %copy-done.1, bf16[1,512,1536]{2,1,0:T(8,128)(2,1)} %param.9), kind=kOutput, calls=%fused_computation.1 | convolution fusion | flops 1208352768 | bytes 4718592 | tf_op jit(solution)/shard_map/dot_general | solution.py:35
  13.2 6.8 %all-to-all-start = ((bf16[4,128,768]{2,1,0:T(8,128)(2,1)}), bf16[4,128,768]{2,1,0:T(8,128)(2,1)S(1)}, u32[]{:S(2)}, u32[]{:S(2)}) async-start(bf16[4,128,768]{2,1,0:T(8,128)(2,1)} %bitcast.2), calls=%async_computation | async-start | bytes 1572864 | tf_op jit(solution)/shard_map/all_to_all | solution.py:536
  20.6 5.5 %collective-permute-done.2.p3 = bf16[128,1536]{1,0:T(8,128)(2,1)S(1)} collective-permute-done((bf16[128,1536]{1,0:T(8,128)(2,1)S(1)}, bf16[128,1536]{1,0:T(8,128)(2,1)S(1)}, u32[]{:S(2)}, u32[]{:S(2)}) %collective-permute-start.2) | collective-permute-done | bytes 393248 | tf_op jit(solution)/shard_map/ppermute | solution.py:515
  26.9 11.3 %forward.1 = (bf16[512,1536]{1,0:T(8,128)(2,1)}, f32[512,1536]{1,0:T(8,128)}, f32[512,128]{1,0:T(8,128)}, bf16[128,768]{1,0:T(8,128)(2,1)}, bf16[128,768]{1,0:T(...) custom-call(s32[1]{0:T(128)} %bitcast.odd_ref, ...), custom_call_target="tpu_custom_call" | custom-call | flops 3623878656 | bytes 20000000 | tf_op jit(solution)/shard_map/forward/pallas_call | solution.py:119
  38.1 2.7 %collective-permute-start.3 = (bf16[512,1536]{1,0:T(8,128)(2,1)}, bf16[512,1536]{1,0:T(8,128)(2,1)S(1)}, u32[]{:S(2)}, u32[]{:S(2)}) collective-permute-start(bf16[512,1536]{1,0:T(8,128)(2,1)} %get-tuple-element.64.own_hbm), channel_id=1, source_target_pairs={{0,1},{1,0},{2,3},{3,2},{4,5},{5,4},{6,7},{7,6},{8,9},{9,8},{10,11... | collective-permute-start | bytes 4718600 | tf_op jit(solution)/shard_map/ppermute | solution.py:511
  41.7 3.1 %pre_grads.1 = (bf16[512,768]{1,0:T(8,128)(2,1)}, bf16[512,384]{1,0:T(8,128)(2,1)}, bf16[512,384]{1,0:T(8,128)(2,1)}) custom-call(s32[1]{0:T(128)} %bitcast.8.me_ref, s32[1]{0:T(128)} %bitcast.9.core_ref, bf16[4,128,768]{2,1,0:T(8,128)(2,1)} %copy-done.3, f32[512,768]{1,0:T(8,128)} %get-tuple-element.67.slope_ref), custom_call_target="tpu_custom_call" | custom-call | flops 30000001024 | bytes 5000000 | tf_op jit(solution)/shard_map/pre_grads/pallas_call | solution.py:156
  44.8 1.9 %collective-permute-done.4.came_ref = bf16[512,384]{1,0:T(8,128)(2,1)S(1)} collective-permute-done((bf16[512,384]{1,0:T(8,128)(2,1)}, bf16[512,384]{1,0:T(8,128)(2,1)S(1)}, u32[]{:S(2)}, u32[]{:S(2)}) %collective-permute-start.4) | collective-permute-done | bytes 393248 | tf_op jit(solution)/shard_map/ppermute | solution.py:511
  48.0 8.8 %kernel_shares.1 = bf16[4,8,432,128]{3,2,1,0:T(8,128)(2,1)} custom-call(s32[1]{0:T(128)} %bitcast.odd_ref, bf16[512,1536]{1,0:T(8,128)(2,1)} %get-tuple-element.64.own_hbm, bf16[512,1536]{1,0:T(8,128)(2,1)} %copy-done.9, bf16[512,384]{1,0:T(8,128)(2,1)} %get-tuple-element.68.kept_ref, bf16[512,384]{1,0:T(8,128)(2,1)} %copy-done.10), custom_call_target="tpu_custom_call" | custom-call | flops 3623878656 | bytes 10000000 | tf_op jit(solution)/shard_map/kernel_shares/pallas_call | solution.py:294
  56.8 5.1 %all-to-all-start.1 = ((bf16[4,8,432,128]{3,2,1,0:T(8,128)(2,1)}), bf16[4,8,432,128]{3,2,1,0:T(8,128)(2,1)S(1)}, u32[]{:S(2)}, u32[]{:S(2)}) async-start(bf16[4,8,432,128]{3,2,1,0:T(8,128)(2,1)} %kernel_shares.1), calls=%async_computation.1 | async-start | bytes 7077888 | tf_op jit(solution)/shard_map/all_to_all | solution.py:550
  62.4 3.7 %collective-permute-start.6 = (bf16[128,768]{1,0:T(8,128)(2,1)}, bf16[128,768]{1,0:T(8,128)(2,1)}, u32[]{:S(2)}, u32[]{:S(2)}) collective-permute-start(bf16[128,768]{1,0:T(8,128)(2,1)} %get-tuple-element.81), channel_id=1, source_target_pairs={{0,32},{32,0},{64,96},{96,64},{1,33},{33,1},{65,97},{97,65},{2,34}... | collective-permute-start | bytes 589832 | tf_op jit(solution)/shard_map/ppermute | solution.py:515
  66.1 2.7 %collective-permute-start.7 = (bf16[128,768]{1,0:T(8,128)(2,1)}, bf16[128,768]{1,0:T(8,128)(2,1)}, u32[]{:S(2)}, u32[]{:S(2)}) collective-permute-start(bf16[128,768]{1,0:T(8,128)(2,1)} %get-tuple-element.82), channel_id=1, source_target_pairs={{0,64},{32,96},{64,0},{96,32},{1,65},{33,97},{65,1},{97,33},{2,66}... | collective-permute-start | bytes 589832 | tf_op jit(solution)/shard_map/ppermute | solution.py:515
  68.8 11.0 %backward.1 = (bf16[128,1536]{1,0:T(8,128)(2,1)}, bf16[128,1536]{1,0:T(8,128)(2,1)}, bf16[128,1536]{1,0:T(8,128)(2,1)}, bf16[128,1536]{1,0:T(8,128)(2,1)}, f32[1,1536]{1,0:T(1,128)}) custom-call(s32[1]{0:T(128)} %bitcast.odd_ref, bf16[512,768]{1,0:T(8,128)(2,1)} %get-tuple-element.76.grad_ref, bf16[128,1536]{1,0:T(8,128)(2,1)} %get-tuple-element.60.p0, ...), custom_call_target="tpu_custom_call" | custom-call | flops 1000000 | bytes 100000 | tf_op jit(solution)/shard_map/backward/pallas_call | solution.py:219
  79.9 0.9 constant_dynamic-update-slice_fusion.2
  80.8 0.9 constant_dynamic-update-slice_fusion.1
  81.8 0.9 constant_dynamic-update-slice_fusion
  82.7 1.0 broadcast_select_fusion
  84.5 3.1 %collective-permute-start.10 = (bf16[128,1536]{1,0:T(8,128)(2,1)}, bf16[128,1536]{1,0:T(8,128)(2,1)}, u32[]{:S(2)}, u32[]{:S(2)}) collective-permute-start(bf16[128,1536]{1,0:T(8,128)(2,1)} %get-tuple-element.93), channel_id=1, source_target_pairs={{0,32},{32,0},{64,96},{96,64},{1,33},{33,1},{65,97},{97,65},{2,34}... | collective-permute-start | bytes 1179656 | tf_op jit(solution)/shard_map/ppermute | solution.py:515
  87.5 2.7 %collective-permute-start.11 = (bf16[128,1536]{1,0:T(8,128)(2,1)}, bf16[128,1536]{1,0:T(8,128)(2,1)}, u32[]{:S(2)}, u32[]{:S(2)}) collective-permute-start(bf16[128,1536]{1,0:T(8,128)(2,1)} %get-tuple-element.94), channel_id=1, source_target_pairs={{0,64},{32,96},{64,0},{96,32},{1,65},{33,97},{65,1},{97,33},{2,66}... | collective-permute-start | bytes 1179656 | tf_op jit(solution)/shard_map/ppermute | solution.py:515
  92.3 6.1 %point_shares.1 = (bf16[8,160,128]{2,1,0:T(8,128)(2,1)}, bf16[8,160,128]{2,1,0:T(8,128)(2,1)}, bf16[8,160,128]{2,1,0:T(8,128)(2,1)}, bf16[8,160,128]{2,1,0:T(8,128)(2,1)}) custom-call(s32[1]{0:T(128)} %bitcast.10.z_ref, s32[1]{0:T(128)} %bitcast.8.me_ref, bf16[512,1536]{1,0:T(8,128)(2,1)} %bitcast.41, bf16[512,1536]{1,0:T(8,128)(2,1)} %collective-permute-done.5.other_hbm, ...), custom_call_target="tpu_custom_call" | custom-call | flops 1207959552 | bytes 6000000 | tf_op jit(solution)/shard_map/point_shares/pallas_call | solution.py:354
  98.4 1.3 collective-permute-done.11.b2
  99.8 1.7 %collective-permute-start.13 = (bf16[8,160,128]{2,1,0:T(8,128)(2,1)}, bf16[8,160,128]{2,1,0:T(8,128)(2,1)}, u32[]{:S(2)}, u32[]{:S(2)}) collective-permute-start(bf16[8,160,128]{2,1,0:T(8,128)(2,1)} %get-tuple-element.106), channel_id=1, source_target_pairs={{0,4},{4,8},{8,12},{12,0},{1,5},{5,9},{9,13},{13,1},{2,6},{6,10},{... | collective-permute-start | bytes 983048 | tf_op jit(solution)/shard_map/ppermute | solution.py:570
  101.4 2.4 %collective-permute-start.14 = (bf16[8,160,128]{2,1,0:T(8,128)(2,1)}, bf16[8,160,128]{2,1,0:T(8,128)(2,1)}, u32[]{:S(2)}, u32[]{:S(2)}) collective-permute-start(bf16[8,160,128]{2,1,0:T(8,128)(2,1)} %get-tuple-element.107), channel_id=1, source_target_pairs={{0,8},{4,12},{8,0},{12,4},{1,9},{5,13},{9,1},{13,5},{2,10},{6,14},... | collective-permute-start | bytes 983048 | tf_op jit(solution)/shard_map/ppermute | solution.py:570
  103.8 1.2 collective-permute-start.15
  105.0 3.0 %collective-permute-done.12.b3 = bf16[128,1536]{1,0:T(8,128)(2,1)} collective-permute-done((bf16[128,1536]{1,0:T(8,128)(2,1)}, bf16[128,1536]{1,0:T(8,128)(2,1)}, u32[]{:S(2)}, u32[]{:S(2)}) %collective-permute-start.12) | collective-permute-done | bytes 393248 | tf_op jit(solution)/shard_map/ppermute | solution.py:515
  108.0 2.8 %stream_grad.1 = bf16[512,1536]{1,0:T(8,128)(2,1)} custom-call(s32[1]{0:T(128)} %bitcast.8.me_ref, bf16[128,1536]{1,0:T(8,128)(2,1)} %get-tuple-element.101.b0, bf16[128,1536]{1,0:T(8,128)(2,1)} %collective-permute-done.10.b1, bf16[128,1536]{1,0:T(8,128)(2,1)} %collective-permute-done.11.b2, bf16[128,1536]{1,0:T(8,128)(2,1)} %collective-permute-done.12.b3, ...), custom_call_target="tpu_custom_call" | custom-call | flops 1572864 | bytes 5000000 | tf_op jit(solution)/shard_map/stream_grad/pallas_call | solution.py:493
  110.8 4.9 %stream_out.1 = bf16[512,1536]{1,0:T(8,128)(2,1)} custom-call(s32[1]{0:T(128)} %bitcast.8.me_ref, bf16[128,768]{1,0:T(8,128)(2,1)} %get-tuple-element.95.m0, bf16[128,768]{1,0:T(8,128)(2,1)} %collective-permute-done.6.m1, bf16[128,768]{1,0:T(8,128)(2,1)} %collective-permute-done.7.m2, bf16[128,768]{1,0:T(8,128)(2,1)} %collective-permute-done.8.m3, ...), custom_call_target="tpu_custom_call" | custom-call | flops 1207959552 | bytes 6000000 | tf_op jit(solution)/shard_map/stream_out/pallas_call | solution.py:449
  117.7 1.4 plane_shares.1
  119.0 24.9 %all_to_all.15 = bf16[16,304,128]{2,1,0:T(8,128)(2,1)S(1)} all-to-all(bf16[16,304,128]{2,1,0:T(8,128)(2,1)S(1)} %bitcast.33), channel_id=1, replica_groups=mesh['xh'=2,'yh'=2,'yl'=2,'z'=4,'xl'=2,'core'=2] {'xh','yh','yl','xl'}, dimensions={0} | all-to-all | bytes 2490368 | tf_op jit(solution)/shard_map/all_to_all | solution.py:578
  144.1 9.2 %all-gather = f32[1184,128]{1,0:T(8,128)S(1)} all-gather(f32[296,128]{1,0:T(8,128)S(1)} %slice.37), channel_id=2, replica_groups=mesh['xh'=2,'yh'=2,'yl'=2,'z'=4,'xl'=2,'core'=2] {'xl','core'}, dimensions={0}, use_global_device_ids=true | all-gather | bytes 757760 | tf_op jit(solution)/shard_map/all_gather | solution.py:580
  (56 shorter events, 11.6 us)
Async XLA Ops:
  0.7 8.9 %copy-start.1 = (bf16[768,1536]{1,0:T(8,128)(2,1)S(1)}, bf16[768,1536]{1,0:T(8,128)(2,1)}, u32[]{:S(2)}) copy-start(bf16[768,1536]{1,0:T(8,128)(2,1)} %point_ref.1) | copy-start | bytes 7077892
  3.0 17.6 %collective-permute-start = (bf16[128,1536]{1,0:T(8,128)(2,1)S(1)}, bf16[128,1536]{1,0:T(8,128)(2,1)S(1)}, u32[]{:S(2)}, u32[]{:S(2)}) collective-permute-start(bf16[128,1536]{1,0:T(8,128)(2,1)S(1)} %get-tuple-element.117), channel_id=1, source_target_pairs={{0,32},{32,0},{64,96},{96,64},{1,33},{33,1},{65,97},{97,65},{2,34}... | collective-permute-start | bytes 1179656 | tf_op jit(solution)/shard_map/ppermute | solution.py:515
  6.8 13.9 %collective-permute-start.1 = (bf16[128,1536]{1,0:T(8,128)(2,1)S(1)}, bf16[128,1536]{1,0:T(8,128)(2,1)S(1)}, u32[]{:S(2)}, u32[]{:S(2)}) collective-permute-start(bf16[128,1536]{1,0:T(8,128)(2,1)S(1)} %get-tuple-element.116), channel_id=1, source_target_pairs={{0,64},{32,96},{64,0},{96,32},{1,65},{33,97},{65,1},{97,33},{2,66}... | collective-permute-start | bytes 1179656 | tf_op jit(solution)/shard_map/ppermute | solution.py:515
  9.5 16.6 %collective-permute-start.2 = (bf16[128,1536]{1,0:T(8,128)(2,1)S(1)}, bf16[128,1536]{1,0:T(8,128)(2,1)S(1)}, u32[]{:S(2)}, u32[]{:S(2)}) collective-permute-start(bf16[128,1536]{1,0:T(8,128)(2,1)S(1)} %get-tuple-element.115), channel_id=1, source_target_pairs={{0,96},{32,64},{64,32},{96,0},{1,97},{33,65},{65,33},{97,1},{2,98}... | collective-permute-start | bytes 1179656 | tf_op jit(solution)/shard_map/ppermute | solution.py:515
  13.2 6.8 %copy-start.7 = (f32[1536]{0:T(1024)S(1)}, f32[1536]{0:T(1024)}, u32[]{:S(2)}) copy-start(f32[1536]{0:T(1024)} %param.6) | copy-start | bytes 18436
  13.2 27.6 %all-to-all-start = ((bf16[4,128,768]{2,1,0:T(8,128)(2,1)}), bf16[4,128,768]{2,1,0:T(8,128)(2,1)S(1)}, u32[]{:S(2)}, u32[]{:S(2)}) async-start(bf16[4,128,768]{2,1,0:T(8,128)(2,1)} %bitcast.2), calls=%async_computation | async-start | bytes 1572864 | tf_op jit(solution)/shard_map/all_to_all | solution.py:536
  20.6 5.5 %copy-start.4 = (bf16[128,1536]{1,0:T(8,128)(2,1)}, bf16[128,1536]{1,0:T(8,128)(2,1)S(1)}, u32[]{:S(2)}) copy-start(bf16[128,1536]{1,0:T(8,128)(2,1)S(1)} %collective-permute-done.p1) | copy-start | bytes 1179652
  20.6 5.5 %copy-start.5 = (bf16[128,1536]{1,0:T(8,128)(2,1)}, bf16[128,1536]{1,0:T(8,128)(2,1)S(1)}, u32[]{:S(2)}) copy-start(bf16[128,1536]{1,0:T(8,128)(2,1)S(1)} %collective-permute-done.1.p2) | copy-start | bytes 1179652
  26.1 0.8 copy-start.6
  38.1 8.6 %collective-permute-start.3 = (bf16[512,1536]{1,0:T(8,128)(2,1)}, bf16[512,1536]{1,0:T(8,128)(2,1)S(1)}, u32[]{:S(2)}, u32[]{:S(2)}) collective-permute-start(bf16[512,1536]{1,0:T(8,128)(2,1)} %get-tuple-element.64.own_hbm), channel_id=1, source_target_pairs={{0,1},{1,0},{2,3},{3,2},{4,5},{5,4},{6,7},{7,6},{8,9},{9,8},{10,11... | collective-permute-start | bytes 4718600 | tf_op jit(solution)/shard_map/ppermute | solution.py:511
  40.8 0.9 copy-start.3
  44.8 1.9 %collective-permute-start.4 = (bf16[512,384]{1,0:T(8,128)(2,1)}, bf16[512,384]{1,0:T(8,128)(2,1)S(1)}, u32[]{:S(2)}, u32[]{:S(2)}) collective-permute-start(bf16[512,384]{1,0:T(8,128)(2,1)} %get-tuple-element.69), channel_id=1, source_target_pairs={{0,1},{1,0},{2,3},{3,2},{4,5},{5,4},{6,7},{7,6},{8,9},{9,8},{10,11... | collective-permute-start | bytes 1179656 | tf_op jit(solution)/shard_map/ppermute | solution.py:511
  46.7 0.8 copy-start.10
  46.7 1.3 copy-start.9
  56.8 58.9 %all-to-all-start.1 = ((bf16[4,8,432,128]{3,2,1,0:T(8,128)(2,1)}), bf16[4,8,432,128]{3,2,1,0:T(8,128)(2,1)S(1)}, u32[]{:S(2)}, u32[]{:S(2)}) async-start(bf16[4,8,432,128]{3,2,1,0:T(8,128)(2,1)} %kernel_shares.1), calls=%async_computation.1 | async-start | bytes 7077888 | tf_op jit(solution)/shard_map/all_to_all | solution.py:550
  61.9 30.4 %collective-permute-start.5 = (bf16[512,1536]{1,0:T(8,128)(2,1)}, bf16[512,1536]{1,0:T(8,128)(2,1)}, u32[]{:S(2)}, u32[]{:S(2)}) collective-permute-start(bf16[512,1536]{1,0:T(8,128)(2,1)} %bitcast.40), channel_id=1, source_target_pairs={{0,1},{1,0},{2,3},{3,2},{4,5},{5,4},{6,7},{7,6},{8,9},{9,8},{10,11... | collective-permute-start | bytes 4718600 | tf_op jit(solution)/shard_map/ppermute | solution.py:511
  62.4 17.5 %collective-permute-start.6 = (bf16[128,768]{1,0:T(8,128)(2,1)}, bf16[128,768]{1,0:T(8,128)(2,1)}, u32[]{:S(2)}, u32[]{:S(2)}) collective-permute-start(bf16[128,768]{1,0:T(8,128)(2,1)} %get-tuple-element.81), channel_id=1, source_target_pairs={{0,32},{32,0},{64,96},{96,64},{1,33},{33,1},{65,97},{97,65},{2,34}... | collective-permute-start | bytes 589832 | tf_op jit(solution)/shard_map/ppermute | solution.py:515
  66.1 13.8 %collective-permute-start.7 = (bf16[128,768]{1,0:T(8,128)(2,1)}, bf16[128,768]{1,0:T(8,128)(2,1)}, u32[]{:S(2)}, u32[]{:S(2)}) collective-permute-start(bf16[128,768]{1,0:T(8,128)(2,1)} %get-tuple-element.82), channel_id=1, source_target_pairs={{0,64},{32,96},{64,0},{96,32},{1,65},{33,97},{65,1},{97,33},{2,66}... | collective-permute-start | bytes 589832 | tf_op jit(solution)/shard_map/ppermute | solution.py:515
  68.8 11.0 %collective-permute-start.8 = (bf16[128,768]{1,0:T(8,128)(2,1)}, bf16[128,768]{1,0:T(8,128)(2,1)}, u32[]{:S(2)}, u32[]{:S(2)}) collective-permute-start(bf16[128,768]{1,0:T(8,128)(2,1)} %get-tuple-element.83), channel_id=1, source_target_pairs={{0,96},{32,64},{64,32},{96,0},{1,97},{33,65},{65,33},{97,1},{2,98}... | collective-permute-start | bytes 589832 | tf_op jit(solution)/shard_map/ppermute | solution.py:515
  68.8 11.1 %copy-start.2 = (bf16[128,768]{1,0:T(8,128)(2,1)S(1)}, bf16[128,768]{1,0:T(8,128)(2,1)}, u32[]{:S(2)}) copy-start(bf16[128,768]{1,0:T(8,128)(2,1)} %get-tuple-element.95.m0) | copy-start | bytes 589828
  79.9 10.4 %copy-start.8 = (f32[1,1536]{1,0:T(1,128)S(1)}, f32[1,1536]{1,0:T(1,128)}, u32[]{:S(2)}) copy-start(f32[1,1536]{1,0:T(1,128)} %get-tuple-element.88) | copy-start | bytes 18436
  83.7 8.7 %collective-permute-start.9 = (bf16[512,384]{1,0:T(8,128)(2,1)}, bf16[512,384]{1,0:T(8,128)(2,1)}, u32[]{:S(2)}, u32[]{:S(2)}) collective-permute-start(bf16[512,384]{1,0:T(8,128)(2,1)} %get-tuple-element.119), channel_id=1, source_target_pairs={{0,1},{1,0},{2,3},{3,2},{4,5},{5,4},{6,7},{7,6},{8,9},{9,8},{10,11... | collective-permute-start | bytes 1179656 | tf_op jit(solution)/shard_map/ppermute | solution.py:511
  84.5 14.0 %collective-permute-start.10 = (bf16[128,1536]{1,0:T(8,128)(2,1)}, bf16[128,1536]{1,0:T(8,128)(2,1)}, u32[]{:S(2)}, u32[]{:S(2)}) collective-permute-start(bf16[128,1536]{1,0:T(8,128)(2,1)} %get-tuple-element.93), channel_id=1, source_target_pairs={{0,32},{32,0},{64,96},{96,64},{1,33},{33,1},{65,97},{97,65},{2,34}... | collective-permute-start | bytes 1179656 | tf_op jit(solution)/shard_map/ppermute | solution.py:515
  87.5 12.2 %collective-permute-start.11 = (bf16[128,1536]{1,0:T(8,128)(2,1)}, bf16[128,1536]{1,0:T(8,128)(2,1)}, u32[]{:S(2)}, u32[]{:S(2)}) collective-permute-start(bf16[128,1536]{1,0:T(8,128)(2,1)} %get-tuple-element.94), channel_id=1, source_target_pairs={{0,64},{32,96},{64,0},{96,32},{1,65},{33,97},{65,1},{97,33},{2,66}... | collective-permute-start | bytes 1179656 | tf_op jit(solution)/shard_map/ppermute | solution.py:515
  90.3 17.8 %collective-permute-start.12 = (bf16[128,1536]{1,0:T(8,128)(2,1)}, bf16[128,1536]{1,0:T(8,128)(2,1)}, u32[]{:S(2)}, u32[]{:S(2)}) collective-permute-start(bf16[128,1536]{1,0:T(8,128)(2,1)} %get-tuple-element.104), channel_id=1, source_target_pairs={{0,96},{32,64},{64,32},{96,0},{1,97},{33,65},{65,33},{97,1},{2,98}... | collective-permute-start | bytes 1179656 | tf_op jit(solution)/shard_map/ppermute | solution.py:515
  99.8 16.8 %collective-permute-start.13 = (bf16[8,160,128]{2,1,0:T(8,128)(2,1)}, bf16[8,160,128]{2,1,0:T(8,128)(2,1)}, u32[]{:S(2)}, u32[]{:S(2)}) collective-permute-start(bf16[8,160,128]{2,1,0:T(8,128)(2,1)} %get-tuple-element.106), channel_id=1, source_target_pairs={{0,4},{4,8},{8,12},{12,0},{1,5},{5,9},{9,13},{13,1},{2,6},{6,10},{... | collective-permute-start | bytes 983048 | tf_op jit(solution)/shard_map/ppermute | solution.py:570
  101.4 15.7 %collective-permute-start.14 = (bf16[8,160,128]{2,1,0:T(8,128)(2,1)}, bf16[8,160,128]{2,1,0:T(8,128)(2,1)}, u32[]{:S(2)}, u32[]{:S(2)}) collective-permute-start(bf16[8,160,128]{2,1,0:T(8,128)(2,1)} %get-tuple-element.107), channel_id=1, source_target_pairs={{0,8},{4,12},{8,0},{12,4},{1,9},{5,13},{9,1},{13,5},{2,10},{6,14},... | collective-permute-start | bytes 983048 | tf_op jit(solution)/shard_map/ppermute | solution.py:570
  103.8 13.8 %collective-permute-start.15 = (bf16[8,160,128]{2,1,0:T(8,128)(2,1)}, bf16[8,160,128]{2,1,0:T(8,128)(2,1)}, u32[]{:S(2)}, u32[]{:S(2)}) collective-permute-start(bf16[8,160,128]{2,1,0:T(8,128)(2,1)} %get-tuple-element.108), channel_id=1, source_target_pairs={{0,12},{4,0},{8,4},{12,8},{1,13},{5,1},{9,5},{13,9},{2,14},{6,2},{... | collective-permute-start | bytes 983048 | tf_op jit(solution)/shard_map/ppermute | solution.py:570
  115.7 1.9 %copy-start = (bf16[8,160,128]{2,1,0:T(8,128)(2,1)S(1)}, bf16[8,160,128]{2,1,0:T(8,128)(2,1)}, u32[]{:S(2)}) copy-start(bf16[8,160,128]{2,1,0:T(8,128)(2,1)} %get-tuple-element.111.d0) | copy-start | bytes 983044

commit v6 on v5

--- a/solution.py
+++ b/solution.py
@@ -411,6 +411,53 @@
     )(taps, *points)
 
 
+def mid_half_kernel(core_ref, m0, m1, m2, m3, kept_ref, away_ref):
+    core = core_ref[0]
+    for k, source in enumerate((m0, m1, m2, m3)):
+        at = slice(k * Q, (k + 1) * Q)
+        low, high = source[:, :HALF], source[:, HALF:]
+        kept_ref[at, :] = jnp.where(core == 0, low, high)
+        away_ref[at, :] = jnp.where(core == 0, high, low)
+
+
+def mid_halves(core, mid):
+    shape = jax.ShapeDtypeStruct
+    return pl.pallas_call(
+        mid_half_kernel,
+        in_specs=[SMEM] + [VMEM] * 4,
+        out_specs=[VMEM] * 2,
+        out_shape=[shape((N, HALF), BF16)] * 2,
+        compiler_params=params(56),
+        cost_estimate=cost(N * H, 2_000_000),
+        name="mid_halves",
+    )(core, *mid)
+
+
+def unpack_kernel(whole_ref, kernel_ref, point_ref, gain_ref):
+    for core in range(2):
+        for b in range(3):
+            cols = slice(core * HALF + b * 128, core * HALF + b * 128 + 128)
+            first, second = slice(48 * b, 48 * b + 48), slice(144 + 48 * b, 192 + 48 * b)
+            kernel_ref[0, :, cols] = whole_ref[core, first]
+            kernel_ref[1, :, cols] = whole_ref[core, second]
+            kernel_ref[2, :, cols] = whole_ref[2 + core, first]
+            point_ref[:, cols] = whole_ref[2 + core, second]
+    gain_ref[...] = whole_ref[0, 288:296] + whole_ref[1, 288:296]
+
+
+def unpacked(whole):
+    shape = jax.ShapeDtypeStruct
+    return pl.pallas_call(
+        unpack_kernel,
+        in_specs=[VMEM],
+        out_specs=[VMEM] * 3,
+        out_shape=[shape((3, 48, H), F32), shape((48, H), F32), shape((8, 128), F32)],
+        compiler_params=params(32),
+        cost_estimate=cost(1_000_000, 1_200_000),
+        name="unpack",
+    )(whole)
+
+
 def home_rows(me_ref, k):
     return pl.ds(pl.multiple_of(lax.bitwise_xor(me_ref[0], k) * Q, Q), Q)
 
@@ -554,10 +601,8 @@
     )
     back = exchange([b0, b1, b2, b3])
     gain, *mid = lax.optimization_barrier((gain, *mid))
-    mid_home = jnp.concatenate(mid)
-    low, high = mid_home[:, :HALF], mid_home[:, HALF:]
-    mid_kept = jnp.where(core == 0, low, high)
-    mid_came = swap_core(jnp.where(core == 0, high, low))
+    mid_kept, mid_away = mid_halves(core_word, mid)
+    mid_came = swap_core(mid_away)
     gain = gain.astype(BF16).reshape(8, 4, 1, 48)
     gain = jnp.pad(gain, ((0, 0), (0, 0), (0, 15), (0, 80)))
     points = list(
@@ -578,11 +623,8 @@
     plane = lax.all_to_all(plane, PLANE, 0, 0, tiled=True)
     plane = jnp.sum(plane.astype(F32), axis=0)[:296]
     whole = lax.all_gather(plane, ("xl", "core"))
-    gain_grad = whole[0, 288, :48] + whole[1, 288, :48]
-    whole = whole[:, :288].reshape(2, 2, 2, 3, 48, 128).transpose(0, 2, 4, 1, 3, 5)
-    whole = whole.reshape(4, 48, H)
-    kernel_grad = jnp.stack([whole[0], whole[1], whole[2]])
-    return (stream_out[None], stream_grad[None], kernel_grad, whole[3].T, gain_grad)
+    kernel_grad, point_grad, gain_grad = unpacked(whole)
+    return (stream_out[None], stream_grad[None], kernel_grad, point_grad.T, gain_grad[0, :48])
 
 
 def solution(mesh):

time: 157 us -> 155 us (0.987)
  local copies, waits for them, and re-layouts: 12.3 us -> 8.66 us
  Pallas kernels: 50.1 us -> 53.1 us
    pallas_call x0 -> x2, Pallas kernels: none -> 3.03 us  [the longest x1 2.18 us: mid_halves(): pl.pallas_call(mid_half_kernel, in_specs=[SMEM] + [VMEM] * 4, out_specs=[...]
    unnamed x25 -> x24, local copies, waits for them, and re-layouts: 4.82 us -> 3.72 us
  transfers between devices with their start and end apart: 18 -> 18, of which waited for: 6 -> 6; matrix products, arithmetic and copies ran while one was open for 7% -> 5% of each run, Pallas kernels for 26% -> 27%
where the time goes in v6:
time: 155 us
  Pallas kernels  53.1 us (34%)
  starting transfers between devices  39.8 us (26%)
  blocking collectives  35 us (23%)
  waiting for transfers between devices  12.1 us (8%)
  local copies, waits for them, and re-layouts  8.66 us (6%)
  matrix products  3.73 us (2%)
    all_to_all x1, blocking collectives, shards(): plane = lax.all_to_all(plane, PLANE, 0, 0, tiled=True)  25.8 us
    ppermute x9, starting transfers between devices, partner(): return lax.ppermute(value, GROUP, [(i, i ^ k) for i in range(4)])  18.8 us
    pallas_call x1, Pallas kernels, forward(): pl.pallas_call(forward_kernel, in_specs=[SMEM] + [ANY] * 4 + [VMEM, ANY],...  11.3 us
    pallas_call x1, Pallas kernels, backward(): pl.pallas_call(backward_kernel, in_specs=[SMEM, VMEM] + [ANY] * 4 + [VMEM...  11 us
    all_gather x1, blocking collectives, shards(): whole = lax.all_gather(plane, ('xl', 'core'))  9.19 us
    ppermute x9, waiting for transfers between devices, partner(): return lax.ppermute(value, GROUP, [(i, i ^ k) for i in range(4)])  9.1 us
    pallas_call x1, Pallas kernels, kernel_shares(): pl.pallas_call(kernel_share_kernel, in_specs=[SMEM] + [ANY] * 4, out_spec...  8.85 us
    all_to_all x1, starting transfers between devices, shards(): mid_grad = lax.all_to_all(mid_grad, GROUP, 0, 0, tiled=True)  6.78 us
  transfers between devices with their start and end apart: 18, of which 6 were waited for; matrix products, arithmetic and copies ran while one was open for 5% of the time, Pallas kernels for 27%

profile of v6, /device:TPU:1, one launch (start us, length us, event | category | flops | bytes accessed | tf_op | source)
XLA Modules:
  0.0 154.7 jit_solution(10613242224184610795)
XLA Ops:
  0.7 2.4 %dynamic-slice_bitcast_fusion = (bf16[128,1536]{1,0:T(8,128)(2,1)S(1)}, bf16[128,1536]{1,0:T(8,128)(2,1)S(1)}, bf16[128,1536]{1,0:T(8,128)(2,1)S(1)}, bf16[128,1536]{1,0:T(8,128)(2,1)}) fusion(bf16[4,128,1536]{2,1,0:T(8,128)(2,1)} %bitcast.28, s32[]{:T(128)S(6)} %select_n.16, s32[]{:T(128)S(6)} %select_n.15, s32[]{:T(128)S(6)} %select_n.14, s32[]{:T(128)S(6)} %select_n.13), kind=kLoop, calls=%fused_computation.2 | loop fusion | bytes 3145744 | tf_op jit(solution)/shard_map/jit(dynamic_index_in_dim)/squeeze | solution.py:580
  3.0 3.7 %collective-permute-start = (bf16[128,1536]{1,0:T(8,128)(2,1)S(1)}, bf16[128,1536]{1,0:T(8,128)(2,1)S(1)}, u32[]{:S(2)}, u32[]{:S(2)}) collective-permute-start(bf16[128,1536]{1,0:T(8,128)(2,1)S(1)} %get-tuple-element.127), channel_id=1, source_target_pairs={{0,32},{32,0},{64,96},{96,64},{1,33},{33,1},{65,97},{97,65},{2,34}... | collective-permute-start | bytes 1179656 | tf_op jit(solution)/shard_map/ppermute | solution.py:562
  6.8 2.7 %collective-permute-start.1 = (bf16[128,1536]{1,0:T(8,128)(2,1)S(1)}, bf16[128,1536]{1,0:T(8,128)(2,1)S(1)}, u32[]{:S(2)}, u32[]{:S(2)}) collective-permute-start(bf16[128,1536]{1,0:T(8,128)(2,1)S(1)} %get-tuple-element.126), channel_id=1, source_target_pairs={{0,64},{32,96},{64,0},{96,32},{1,65},{33,97},{65,1},{97,33},{2,66}... | collective-permute-start | bytes 1179656 | tf_op jit(solution)/shard_map/ppermute | solution.py:562
  9.5 3.7 %convolution_convert_fusion = bf16[512,768]{1,0:T(8,128)(2,1)} fusion(bf16[768,1536]{1,0:T(8,128)(2,1)S(1)} %copy-done.1, bf16[1,512,1536]{2,1,0:T(8,128)(2,1)} %param.9), kind=kOutput, calls=%fused_computation.1 | convolution fusion | flops 1208352768 | bytes 4718592 | tf_op jit(solution)/shard_map/dot_general | solution.py:35
  13.3 6.8 %all-to-all-start = ((bf16[4,128,768]{2,1,0:T(8,128)(2,1)}), bf16[4,128,768]{2,1,0:T(8,128)(2,1)S(1)}, u32[]{:S(2)}, u32[]{:S(2)}) async-start(bf16[4,128,768]{2,1,0:T(8,128)(2,1)} %bitcast.2), calls=%async_computation | async-start | bytes 1572864 | tf_op jit(solution)/shard_map/all_to_all | solution.py:583
  20.7 5.5 %collective-permute-done.2.p3 = bf16[128,1536]{1,0:T(8,128)(2,1)S(1)} collective-permute-done((bf16[128,1536]{1,0:T(8,128)(2,1)S(1)}, bf16[128,1536]{1,0:T(8,128)(2,1)S(1)}, u32[]{:S(2)}, u32[]{:S(2)}) %collective-permute-start.2) | collective-permute-done | bytes 393248 | tf_op jit(solution)/shard_map/ppermute | solution.py:562
  26.9 11.3 %forward.1 = (bf16[512,1536]{1,0:T(8,128)(2,1)}, f32[512,1536]{1,0:T(8,128)}, f32[512,128]{1,0:T(8,128)}, bf16[128,768]{1,0:T(8,128)(2,1)}, bf16[128,768]{1,0:T(...) custom-call(s32[1]{0:T(128)} %bitcast.odd_ref, ...), custom_call_target="tpu_custom_call" | custom-call | flops 3623878656 | bytes 20000000 | tf_op jit(solution)/shard_map/forward/pallas_call | solution.py:119
  38.2 2.7 %collective-permute-start.3 = (bf16[512,1536]{1,0:T(8,128)(2,1)}, bf16[512,1536]{1,0:T(8,128)(2,1)S(1)}, u32[]{:S(2)}, u32[]{:S(2)}) collective-permute-start(bf16[512,1536]{1,0:T(8,128)(2,1)} %get-tuple-element.69.own_hbm), channel_id=1, source_target_pairs={{0,1},{1,0},{2,3},{3,2},{4,5},{5,4},{6,7},{7,6},{8,9},{9,8},{10,11... | collective-permute-start | bytes 4718600 | tf_op jit(solution)/shard_map/ppermute | solution.py:558
  40.9 0.9 copy-done.5
  41.8 3.1 %pre_grads.1 = (bf16[512,768]{1,0:T(8,128)(2,1)}, bf16[512,384]{1,0:T(8,128)(2,1)}, bf16[512,384]{1,0:T(8,128)(2,1)}) custom-call(s32[1]{0:T(128)} %bitcast.8.me_ref, s32[1]{0:T(128)} %bitcast.9.core_ref, bf16[4,128,768]{2,1,0:T(8,128)(2,1)} %copy-done.5, f32[512,768]{1,0:T(8,128)} %get-tuple-element.72.slope_ref), custom_call_target="tpu_custom_call" | custom-call | flops 30000001024 | bytes 5000000 | tf_op jit(solution)/shard_map/pre_grads/pallas_call | solution.py:156
  44.9 1.9 %collective-permute-done.4.came_ref = bf16[512,384]{1,0:T(8,128)(2,1)S(1)} collective-permute-done((bf16[512,384]{1,0:T(8,128)(2,1)}, bf16[512,384]{1,0:T(8,128)(2,1)S(1)}, u32[]{:S(2)}, u32[]{:S(2)}) %collective-permute-start.4) | collective-permute-done | bytes 393248 | tf_op jit(solution)/shard_map/ppermute | solution.py:558
  46.8 0.8 copy-done.11
  48.0 8.8 %kernel_shares.1 = bf16[4,8,432,128]{3,2,1,0:T(8,128)(2,1)} custom-call(s32[1]{0:T(128)} %bitcast.odd_ref, bf16[512,1536]{1,0:T(8,128)(2,1)} %get-tuple-element.69.own_hbm, bf16[512,1536]{1,0:T(8,128)(2,1)} %copy-done.10, bf16[512,384]{1,0:T(8,128)(2,1)} %get-tuple-element.73.kept_ref, bf16[512,384]{1,0:T(8,128)(2,1)} %copy-done.11), custom_call_target="tpu_custom_call" | custom-call | flops 3623878656 | bytes 10000000 | tf_op jit(solution)/shard_map/kernel_shares/pallas_call | solution.py:294
  56.9 5.1 %all-to-all-start.1 = ((bf16[4,8,432,128]{3,2,1,0:T(8,128)(2,1)}), bf16[4,8,432,128]{3,2,1,0:T(8,128)(2,1)S(1)}, u32[]{:S(2)}, u32[]{:S(2)}) async-start(bf16[4,8,432,128]{3,2,1,0:T(8,128)(2,1)} %kernel_shares.1), calls=%async_computation.1 | async-start | bytes 7077888 | tf_op jit(solution)/shard_map/all_to_all | solution.py:597
  62.4 3.7 %collective-permute-start.6 = (bf16[128,768]{1,0:T(8,128)(2,1)}, bf16[128,768]{1,0:T(8,128)(2,1)S(1)}, u32[]{:S(2)}, u32[]{:S(2)}) collective-permute-start(bf16[128,768]{1,0:T(8,128)(2,1)} %get-tuple-element.86), channel_id=1, source_target_pairs={{0,32},{32,0},{64,96},{96,64},{1,33},{33,1},{65,97},{97,65},{2,34}... | collective-permute-start | bytes 589832 | tf_op jit(solution)/shard_map/ppermute | solution.py:562
  66.1 2.7 %collective-permute-start.7 = (bf16[128,768]{1,0:T(8,128)(2,1)}, bf16[128,768]{1,0:T(8,128)(2,1)S(1)}, u32[]{:S(2)}, u32[]{:S(2)}) collective-permute-start(bf16[128,768]{1,0:T(8,128)(2,1)} %get-tuple-element.87), channel_id=1, source_target_pairs={{0,64},{32,96},{64,0},{96,32},{1,65},{33,97},{65,1},{97,33},{2,66}... | collective-permute-start | bytes 589832 | tf_op jit(solution)/shard_map/ppermute | solution.py:562
  68.9 11.0 %backward.1 = (bf16[128,1536]{1,0:T(8,128)(2,1)}, bf16[128,1536]{1,0:T(8,128)(2,1)}, bf16[128,1536]{1,0:T(8,128)(2,1)}, bf16[128,1536]{1,0:T(8,128)(2,1)}, f32[1,1536]{1,0:T(1,128)}) custom-call(s32[1]{0:T(128)} %bitcast.odd_ref, bf16[512,768]{1,0:T(8,128)(2,1)} %get-tuple-element.81.grad_ref, bf16[128,1536]{1,0:T(8,128)(2,1)} %get-tuple-element.65.p0, ...), custom_call_target="tpu_custom_call" | custom-call | flops 1000000 | bytes 100000 | tf_op jit(solution)/shard_map/backward/pallas_call | solution.py:219
  80.7 2.2 %mid_halves.1 = (bf16[512,384]{1,0:T(8,128)(2,1)}, bf16[512,384]{1,0:T(8,128)(2,1)}) custom-call(s32[1]{0:T(128)} %bitcast.9.core_ref, bf16[128,768]{1,0:T(8,128)(2,1)} %get-tuple-element.102.m0, bf16[128,768]{1,0:T(8,128)(2,1)} %copy-done.2, bf16[128,768]{1,0:T(8,128)(2,1)} %copy-done.3, bf16[128,768]{1,0:T(8,128)(2,1)} %copy-done.4), custom_call_target="tpu_custom_call" | custom-call | flops 393216 | bytes 2000000 | tf_op jit(solution)/shard_map/mid_halves/pallas_call | solution.py:425
  83.6 3.1 %collective-permute-start.10 = (bf16[128,1536]{1,0:T(8,128)(2,1)}, bf16[128,1536]{1,0:T(8,128)(2,1)}, u32[]{:S(2)}, u32[]{:S(2)}) collective-permute-start(bf16[128,1536]{1,0:T(8,128)(2,1)} %get-tuple-element.100), channel_id=1, source_target_pairs={{0,32},{32,0},{64,96},{96,64},{1,33},{33,1},{65,97},{97,65},{2,34}... | collective-permute-start | bytes 1179656 | tf_op jit(solution)/shard_map/ppermute | solution.py:562
  86.7 2.7 %collective-permute-start.11 = (bf16[128,1536]{1,0:T(8,128)(2,1)}, bf16[128,1536]{1,0:T(8,128)(2,1)}, u32[]{:S(2)}, u32[]{:S(2)}) collective-permute-start(bf16[128,1536]{1,0:T(8,128)(2,1)} %get-tuple-element.101), channel_id=1, source_target_pairs={{0,64},{32,96},{64,0},{96,32},{1,65},{33,97},{65,1},{97,33},{2,66}... | collective-permute-start | bytes 1179656 | tf_op jit(solution)/shard_map/ppermute | solution.py:562
  89.4 1.3 convert_reduce_fusion.1
  92.2 6.1 %point_shares.1 = (bf16[8,160,128]{2,1,0:T(8,128)(2,1)}, bf16[8,160,128]{2,1,0:T(8,128)(2,1)}, bf16[8,160,128]{2,1,0:T(8,128)(2,1)}, bf16[8,160,128]{2,1,0:T(8,128)(2,1)}) custom-call(s32[1]{0:T(128)} %bitcast.10.z_ref, s32[1]{0:T(128)} %bitcast.8.me_ref, bf16[512,1536]{1,0:T(8,128)(2,1)} %bitcast.31, bf16[512,1536]{1,0:T(8,128)(2,1)} %collective-permute-done.5.other_hbm, ...), custom_call_target="tpu_custom_call" | custom-call | flops 1207959552 | bytes 6000000 | tf_op jit(solution)/shard_map/point_shares/pallas_call | solution.py:354
  98.9 1.7 %collective-permute-start.13 = (bf16[8,160,128]{2,1,0:T(8,128)(2,1)}, bf16[8,160,128]{2,1,0:T(8,128)(2,1)}, u32[]{:S(2)}, u32[]{:S(2)}) collective-permute-start(bf16[8,160,128]{2,1,0:T(8,128)(2,1)} %get-tuple-element.113), channel_id=1, source_target_pairs={{0,4},{4,8},{8,12},{12,0},{1,5},{5,9},{9,13},{13,1},{2,6},{6,10},{... | collective-permute-start | bytes 983048 | tf_op jit(solution)/shard_map/ppermute | solution.py:615
  100.6 2.4 %collective-permute-start.14 = (bf16[8,160,128]{2,1,0:T(8,128)(2,1)}, bf16[8,160,128]{2,1,0:T(8,128)(2,1)}, u32[]{:S(2)}, u32[]{:S(2)}) collective-permute-start(bf16[8,160,128]{2,1,0:T(8,128)(2,1)} %get-tuple-element.114), channel_id=1, source_target_pairs={{0,8},{4,12},{8,0},{12,4},{1,9},{5,13},{9,1},{13,5},{2,10},{6,14},... | collective-permute-start | bytes 983048 | tf_op jit(solution)/shard_map/ppermute | solution.py:615
  103.0 1.2 collective-permute-start.15
  104.2 3.0 %collective-permute-done.12.b3 = bf16[128,1536]{1,0:T(8,128)(2,1)} collective-permute-done((bf16[128,1536]{1,0:T(8,128)(2,1)}, bf16[128,1536]{1,0:T(8,128)(2,1)}, u32[]{:S(2)}, u32[]{:S(2)}) %collective-permute-start.12) | collective-permute-done | bytes 393248 | tf_op jit(solution)/shard_map/ppermute | solution.py:562
  107.2 2.8 %stream_grad.1 = bf16[512,1536]{1,0:T(8,128)(2,1)} custom-call(s32[1]{0:T(128)} %bitcast.8.me_ref, bf16[128,1536]{1,0:T(8,128)(2,1)} %get-tuple-element.108.b0, bf16[128,1536]{1,0:T(8,128)(2,1)} %collective-permute-done.10.b1, bf16[128,1536]{1,0:T(8,128)(2,1)} %collective-permute-done.11.b2, bf16[128,1536]{1,0:T(8,128)(2,1)} %collective-permute-done.12.b3, ...), custom_call_target="tpu_custom_call" | custom-call | flops 1572864 | bytes 5000000 | tf_op jit(solution)/shard_map/stream_grad/pallas_call | solution.py:540
  109.9 4.9 %stream_out.1 = bf16[512,1536]{1,0:T(8,128)(2,1)} custom-call(s32[1]{0:T(128)} %bitcast.8.me_ref, bf16[128,768]{1,0:T(8,128)(2,1)} %get-tuple-element.102.m0, bf16[128,768]{1,0:T(8,128)(2,1)} %copy-done.2, bf16[128,768]{1,0:T(8,128)(2,1)} %copy-done.3, bf16[128,768]{1,0:T(8,128)(2,1)} %copy-done.4, bf16[768,1536]{1,0:T(8,128)(2,1)} %point_ref.1, ...), custom_call_target="tpu_custom_call" | custom-call | flops 1207959552 | bytes 6000000 | tf_op jit(solution)/shard_map/stream_out/pallas_call | solution.py:496
  116.8 1.4 plane_shares.1
  118.2 25.8 %all_to_all.15 = bf16[16,304,128]{2,1,0:T(8,128)(2,1)S(1)} all-to-all(bf16[16,304,128]{2,1,0:T(8,128)(2,1)S(1)} %bitcast.26), channel_id=1, replica_groups=mesh['xh'=2,'yh'=2,'yl'=2,'z'=4,'xl'=2,'core'=2] {'xh','yh','yl','xl'}, dimensions={0} | all-to-all | bytes 2490368 | tf_op jit(solution)/shard_map/all_to_all | solution.py:623
  144.2 9.2 %all-gather = f32[1184,128]{1,0:T(8,128)S(1)} all-gather(f32[296,128]{1,0:T(8,128)S(1)} %slice.8), channel_id=2, replica_groups=mesh['xh'=2,'yh'=2,'yl'=2,'z'=4,'xl'=2,'core'=2] {'xl','core'}, dimensions={0}, use_global_device_ids=true | all-gather | bytes 757760 | tf_op jit(solution)/shard_map/all_gather | solution.py:625
  153.4 0.8 unpack.1
  (50 shorter events, 8.5 us)
Async XLA Ops:
  0.7 8.9 %copy-start.1 = (bf16[768,1536]{1,0:T(8,128)(2,1)S(1)}, bf16[768,1536]{1,0:T(8,128)(2,1)}, u32[]{:S(2)}) copy-start(bf16[768,1536]{1,0:T(8,128)(2,1)} %point_ref.1) | copy-start | bytes 7077892
  3.0 17.6 %collective-permute-start = (bf16[128,1536]{1,0:T(8,128)(2,1)S(1)}, bf16[128,1536]{1,0:T(8,128)(2,1)S(1)}, u32[]{:S(2)}, u32[]{:S(2)}) collective-permute-start(bf16[128,1536]{1,0:T(8,128)(2,1)S(1)} %get-tuple-element.127), channel_id=1, source_target_pairs={{0,32},{32,0},{64,96},{96,64},{1,33},{33,1},{65,97},{97,65},{2,34}... | collective-permute-start | bytes 1179656 | tf_op jit(solution)/shard_map/ppermute | solution.py:562
  6.8 13.9 %collective-permute-start.1 = (bf16[128,1536]{1,0:T(8,128)(2,1)S(1)}, bf16[128,1536]{1,0:T(8,128)(2,1)S(1)}, u32[]{:S(2)}, u32[]{:S(2)}) collective-permute-start(bf16[128,1536]{1,0:T(8,128)(2,1)S(1)} %get-tuple-element.126), channel_id=1, source_target_pairs={{0,64},{32,96},{64,0},{96,32},{1,65},{33,97},{65,1},{97,33},{2,66}... | collective-permute-start | bytes 1179656 | tf_op jit(solution)/shard_map/ppermute | solution.py:562
  9.5 16.6 %collective-permute-start.2 = (bf16[128,1536]{1,0:T(8,128)(2,1)S(1)}, bf16[128,1536]{1,0:T(8,128)(2,1)S(1)}, u32[]{:S(2)}, u32[]{:S(2)}) collective-permute-start(bf16[128,1536]{1,0:T(8,128)(2,1)S(1)} %get-tuple-element.125), channel_id=1, source_target_pairs={{0,96},{32,64},{64,32},{96,0},{1,97},{33,65},{65,33},{97,1},{2,98}... | collective-permute-start | bytes 1179656 | tf_op jit(solution)/shard_map/ppermute | solution.py:562
  13.3 6.8 %copy-start.9 = (f32[1536]{0:T(1024)S(1)}, f32[1536]{0:T(1024)}, u32[]{:S(2)}) copy-start(f32[1536]{0:T(1024)} %param.6) | copy-start | bytes 18436
  13.3 27.6 %all-to-all-start = ((bf16[4,128,768]{2,1,0:T(8,128)(2,1)}), bf16[4,128,768]{2,1,0:T(8,128)(2,1)S(1)}, u32[]{:S(2)}, u32[]{:S(2)}) async-start(bf16[4,128,768]{2,1,0:T(8,128)(2,1)} %bitcast.2), calls=%async_computation | async-start | bytes 1572864 | tf_op jit(solution)/shard_map/all_to_all | solution.py:583
  20.6 5.5 %copy-start.6 = (bf16[128,1536]{1,0:T(8,128)(2,1)}, bf16[128,1536]{1,0:T(8,128)(2,1)S(1)}, u32[]{:S(2)}) copy-start(bf16[128,1536]{1,0:T(8,128)(2,1)S(1)} %collective-permute-done.p1) | copy-start | bytes 1179652
  20.6 5.5 %copy-start.7 = (bf16[128,1536]{1,0:T(8,128)(2,1)}, bf16[128,1536]{1,0:T(8,128)(2,1)S(1)}, u32[]{:S(2)}) copy-start(bf16[128,1536]{1,0:T(8,128)(2,1)S(1)} %collective-permute-done.1.p2) | copy-start | bytes 1179652
  26.1 0.8 copy-start.8
  38.2 8.6 %collective-permute-start.3 = (bf16[512,1536]{1,0:T(8,128)(2,1)}, bf16[512,1536]{1,0:T(8,128)(2,1)S(1)}, u32[]{:S(2)}, u32[]{:S(2)}) collective-permute-start(bf16[512,1536]{1,0:T(8,128)(2,1)} %get-tuple-element.69.own_hbm), channel_id=1, source_target_pairs={{0,1},{1,0},{2,3},{3,2},{4,5},{5,4},{6,7},{7,6},{8,9},{9,8},{10,11... | collective-permute-start | bytes 4718600 | tf_op jit(solution)/shard_map/ppermute | solution.py:558
  40.9 0.9 copy-start.5
  44.8 1.9 %collective-permute-start.4 = (bf16[512,384]{1,0:T(8,128)(2,1)}, bf16[512,384]{1,0:T(8,128)(2,1)S(1)}, u32[]{:S(2)}, u32[]{:S(2)}) collective-permute-start(bf16[512,384]{1,0:T(8,128)(2,1)} %get-tuple-element.74), channel_id=1, source_target_pairs={{0,1},{1,0},{2,3},{3,2},{4,5},{5,4},{6,7},{7,6},{8,9},{9,8},{10,11... | collective-permute-start | bytes 1179656 | tf_op jit(solution)/shard_map/ppermute | solution.py:558
  46.8 0.8 copy-start.11
  46.8 1.3 copy-start.10
  56.9 58.0 %all-to-all-start.1 = ((bf16[4,8,432,128]{3,2,1,0:T(8,128)(2,1)}), bf16[4,8,432,128]{3,2,1,0:T(8,128)(2,1)S(1)}, u32[]{:S(2)}, u32[]{:S(2)}) async-start(bf16[4,8,432,128]{3,2,1,0:T(8,128)(2,1)} %kernel_shares.1), calls=%async_computation.1 | async-start | bytes 7077888 | tf_op jit(solution)/shard_map/all_to_all | solution.py:597
  62.0 30.2 %collective-permute-start.5 = (bf16[512,1536]{1,0:T(8,128)(2,1)}, bf16[512,1536]{1,0:T(8,128)(2,1)}, u32[]{:S(2)}, u32[]{:S(2)}) collective-permute-start(bf16[512,1536]{1,0:T(8,128)(2,1)} %bitcast.30), channel_id=1, source_target_pairs={{0,1},{1,0},{2,3},{3,2},{4,5},{5,4},{6,7},{7,6},{8,9},{9,8},{10,11... | collective-permute-start | bytes 4718600 | tf_op jit(solution)/shard_map/ppermute | solution.py:558
  62.4 17.4 %collective-permute-start.6 = (bf16[128,768]{1,0:T(8,128)(2,1)}, bf16[128,768]{1,0:T(8,128)(2,1)S(1)}, u32[]{:S(2)}, u32[]{:S(2)}) collective-permute-start(bf16[128,768]{1,0:T(8,128)(2,1)} %get-tuple-element.86), channel_id=1, source_target_pairs={{0,32},{32,0},{64,96},{96,64},{1,33},{33,1},{65,97},{97,65},{2,34}... | collective-permute-start | bytes 589832 | tf_op jit(solution)/shard_map/ppermute | solution.py:562
  66.1 13.7 %collective-permute-start.7 = (bf16[128,768]{1,0:T(8,128)(2,1)}, bf16[128,768]{1,0:T(8,128)(2,1)S(1)}, u32[]{:S(2)}, u32[]{:S(2)}) collective-permute-start(bf16[128,768]{1,0:T(8,128)(2,1)} %get-tuple-element.87), channel_id=1, source_target_pairs={{0,64},{32,96},{64,0},{96,32},{1,65},{33,97},{65,1},{97,33},{2,66}... | collective-permute-start | bytes 589832 | tf_op jit(solution)/shard_map/ppermute | solution.py:562
  68.9 11.0 %collective-permute-start.8 = (bf16[128,768]{1,0:T(8,128)(2,1)}, bf16[128,768]{1,0:T(8,128)(2,1)S(1)}, u32[]{:S(2)}, u32[]{:S(2)}) collective-permute-start(bf16[128,768]{1,0:T(8,128)(2,1)} %get-tuple-element.88), channel_id=1, source_target_pairs={{0,96},{32,64},{64,32},{96,0},{1,97},{33,65},{65,33},{97,1},{2,98}... | collective-permute-start | bytes 589832 | tf_op jit(solution)/shard_map/ppermute | solution.py:562
  79.8 0.7 copy-start.2
  79.9 0.7 copy-start.3
  79.9 0.8 copy-start.4
  82.8 9.3 %collective-permute-start.9 = (bf16[512,384]{1,0:T(8,128)(2,1)}, bf16[512,384]{1,0:T(8,128)(2,1)}, u32[]{:S(2)}, u32[]{:S(2)}) collective-permute-start(bf16[512,384]{1,0:T(8,128)(2,1)} %get-tuple-element.94), channel_id=1, source_target_pairs={{0,1},{1,0},{2,3},{3,2},{4,5},{5,4},{6,7},{7,6},{8,9},{9,8},{10,11... | collective-permute-start | bytes 1179656 | tf_op jit(solution)/shard_map/ppermute | solution.py:558
  83.6 14.7 %collective-permute-start.10 = (bf16[128,1536]{1,0:T(8,128)(2,1)}, bf16[128,1536]{1,0:T(8,128)(2,1)}, u32[]{:S(2)}, u32[]{:S(2)}) collective-permute-start(bf16[128,1536]{1,0:T(8,128)(2,1)} %get-tuple-element.100), channel_id=1, source_target_pairs={{0,32},{32,0},{64,96},{96,64},{1,33},{33,1},{65,97},{97,65},{2,34}... | collective-permute-start | bytes 1179656 | tf_op jit(solution)/shard_map/ppermute | solution.py:562
  86.7 12.2 %collective-permute-start.11 = (bf16[128,1536]{1,0:T(8,128)(2,1)}, bf16[128,1536]{1,0:T(8,128)(2,1)}, u32[]{:S(2)}, u32[]{:S(2)}) collective-permute-start(bf16[128,1536]{1,0:T(8,128)(2,1)} %get-tuple-element.101), channel_id=1, source_target_pairs={{0,64},{32,96},{64,0},{96,32},{1,65},{33,97},{65,1},{97,33},{2,66}... | collective-permute-start | bytes 1179656 | tf_op jit(solution)/shard_map/ppermute | solution.py:562
  89.4 17.8 %collective-permute-start.12 = (bf16[128,1536]{1,0:T(8,128)(2,1)}, bf16[128,1536]{1,0:T(8,128)(2,1)}, u32[]{:S(2)}, u32[]{:S(2)}) collective-permute-start(bf16[128,1536]{1,0:T(8,128)(2,1)} %get-tuple-element.111), channel_id=1, source_target_pairs={{0,96},{32,64},{64,32},{96,0},{1,97},{33,65},{65,33},{97,1},{2,98}... | collective-permute-start | bytes 1179656 | tf_op jit(solution)/shard_map/ppermute | solution.py:562
  98.9 16.8 %collective-permute-start.13 = (bf16[8,160,128]{2,1,0:T(8,128)(2,1)}, bf16[8,160,128]{2,1,0:T(8,128)(2,1)}, u32[]{:S(2)}, u32[]{:S(2)}) collective-permute-start(bf16[8,160,128]{2,1,0:T(8,128)(2,1)} %get-tuple-element.113), channel_id=1, source_target_pairs={{0,4},{4,8},{8,12},{12,0},{1,5},{5,9},{9,13},{13,1},{2,6},{6,10},{... | collective-permute-start | bytes 983048 | tf_op jit(solution)/shard_map/ppermute | solution.py:615
  100.6 15.7 %collective-permute-start.14 = (bf16[8,160,128]{2,1,0:T(8,128)(2,1)}, bf16[8,160,128]{2,1,0:T(8,128)(2,1)}, u32[]{:S(2)}, u32[]{:S(2)}) collective-permute-start(bf16[8,160,128]{2,1,0:T(8,128)(2,1)} %get-tuple-element.114), channel_id=1, source_target_pairs={{0,8},{4,12},{8,0},{12,4},{1,9},{5,13},{9,1},{13,5},{2,10},{6,14},... | collective-permute-start | bytes 983048 | tf_op jit(solution)/shard_map/ppermute | solution.py:615
  103.0 13.8 %collective-permute-start.15 = (bf16[8,160,128]{2,1,0:T(8,128)(2,1)}, bf16[8,160,128]{2,1,0:T(8,128)(2,1)}, u32[]{:S(2)}, u32[]{:S(2)}) collective-permute-start(bf16[8,160,128]{2,1,0:T(8,128)(2,1)} %get-tuple-element.115), channel_id=1, source_target_pairs={{0,12},{4,0},{8,4},{12,8},{1,13},{5,1},{9,5},{13,9},{2,14},{6,2},{... | collective-permute-start | bytes 983048 | tf_op jit(solution)/shard_map/ppermute | solution.py:615
  114.9 1.9 %copy-start = (bf16[8,160,128]{2,1,0:T(8,128)(2,1)S(1)}, bf16[8,160,128]{2,1,0:T(8,128)(2,1)}, u32[]{:S(2)}) copy-start(bf16[8,160,128]{2,1,0:T(8,128)(2,1)} %get-tuple-element.118.d0) | copy-start | bytes 983044

commit v7 on v6

--- a/solution.py
+++ b/solution.py
@@ -608,8 +608,8 @@
     points = list(
         point_shares(z_word, me_word, cotan, cotan_other, mid_kept, mid_came, gain)
     )
-    points[0], points[1], points[2], points[3], back[1], back[2], *mid = lax.optimization_barrier(
-        (*points, back[1], back[2], *mid)
+    points[0], points[1], points[2], points[3], back[1], *mid = lax.optimization_barrier(
+        (*points, back[1], *mid)
     )
     points = [points[0]] + [
         lax.ppermute(points[d], "z", [(i, (i + d) % 4) for i in range(4)]) for d in (1, 2, 3)

time: 155 us -> 155 us (level)
  transfers between devices with their start and end apart: 18 -> 18, of which waited for: 6 -> 4; matrix products, arithmetic and copies ran while one was open for 5% -> 5% of each run, Pallas kernels for 27% -> 27%
where the time goes in v7:
time: 155 us
  Pallas kernels  53.1 us (34%)
  starting transfers between devices  39.8 us (26%)
  blocking collectives  33.9 us (22%)
  waiting for transfers between devices  13.1 us (8%)
  local copies, waits for them, and re-layouts  8.66 us (6%)
  matrix products  3.73 us (2%)
    all_to_all x1, blocking collectives, shards(): plane = lax.all_to_all(plane, PLANE, 0, 0, tiled=True)  24.7 us
    ppermute x9, starting transfers between devices, partner(): return lax.ppermute(value, GROUP, [(i, i ^ k) for i in range(4)])  18.8 us
    pallas_call x1, Pallas kernels, forward(): pl.pallas_call(forward_kernel, in_specs=[SMEM] + [ANY] * 4 + [VMEM, ANY],...  11.3 us
    pallas_call x1, Pallas kernels, backward(): pl.pallas_call(backward_kernel, in_specs=[SMEM, VMEM] + [ANY] * 4 + [VMEM...  10.9 us
    all_gather x1, blocking collectives, shards(): whole = lax.all_gather(plane, ('xl', 'core'))  9.19 us
    ppermute x9, waiting for transfers between devices, partner(): return lax.ppermute(value, GROUP, [(i, i ^ k) for i in range(4)])  9.04 us
    pallas_call x1, Pallas kernels, kernel_shares(): pl.pallas_call(kernel_share_kernel, in_specs=[SMEM] + [ANY] * 4, out_spec...  8.85 us
    all_to_all x1, starting transfers between devices, shards(): mid_grad = lax.all_to_all(mid_grad, GROUP, 0, 0, tiled=True)  6.78 us
  transfers between devices with their start and end apart: 18, of which 4 were waited for; matrix products, arithmetic and copies ran while one was open for 5% of the time, Pallas kernels for 27%

profile of v7, /device:TPU:1, one launch (start us, length us, event | category | flops | bytes accessed | tf_op | source)
XLA Modules:
  0.0 154.7 jit_solution(3776039613920313077)
XLA Ops:
  0.7 2.4 %dynamic-slice_bitcast_fusion = (bf16[128,1536]{1,0:T(8,128)(2,1)S(1)}, bf16[128,1536]{1,0:T(8,128)(2,1)S(1)}, bf16[128,1536]{1,0:T(8,128)(2,1)S(1)}, bf16[128,1536]{1,0:T(8,128)(2,1)}) fusion(bf16[4,128,1536]{2,1,0:T(8,128)(2,1)} %bitcast.28, s32[]{:T(128)S(6)} %select_n.16, s32[]{:T(128)S(6)} %select_n.15, s32[]{:T(128)S(6)} %select_n.14, s32[]{:T(128)S(6)} %select_n.13), kind=kLoop, calls=%fused_computation.2 | loop fusion | bytes 3145744 | tf_op jit(solution)/shard_map/jit(dynamic_index_in_dim)/squeeze | solution.py:580
  3.0 3.7 %collective-permute-start = (bf16[128,1536]{1,0:T(8,128)(2,1)S(1)}, bf16[128,1536]{1,0:T(8,128)(2,1)S(1)}, u32[]{:S(2)}, u32[]{:S(2)}) collective-permute-start(bf16[128,1536]{1,0:T(8,128)(2,1)S(1)} %get-tuple-element.125), channel_id=1, source_target_pairs={{0,32},{32,0},{64,96},{96,64},{1,33},{33,1},{65,97},{97,65},{2,34}... | collective-permute-start | bytes 1179656 | tf_op jit(solution)/shard_map/ppermute | solution.py:562
  6.8 2.7 %collective-permute-start.1 = (bf16[128,1536]{1,0:T(8,128)(2,1)S(1)}, bf16[128,1536]{1,0:T(8,128)(2,1)S(1)}, u32[]{:S(2)}, u32[]{:S(2)}) collective-permute-start(bf16[128,1536]{1,0:T(8,128)(2,1)S(1)} %get-tuple-element.124), channel_id=1, source_target_pairs={{0,64},{32,96},{64,0},{96,32},{1,65},{33,97},{65,1},{97,33},{2,66}... | collective-permute-start | bytes 1179656 | tf_op jit(solution)/shard_map/ppermute | solution.py:562
  9.5 3.7 %convolution_convert_fusion = bf16[512,768]{1,0:T(8,128)(2,1)} fusion(bf16[768,1536]{1,0:T(8,128)(2,1)S(1)} %copy-done.1, bf16[1,512,1536]{2,1,0:T(8,128)(2,1)} %param.9), kind=kOutput, calls=%fused_computation.1 | convolution fusion | flops 1208352768 | bytes 4718592 | tf_op jit(solution)/shard_map/dot_general | solution.py:35
  13.3 6.8 %all-to-all-start = ((bf16[4,128,768]{2,1,0:T(8,128)(2,1)}), bf16[4,128,768]{2,1,0:T(8,128)(2,1)S(1)}, u32[]{:S(2)}, u32[]{:S(2)}) async-start(bf16[4,128,768]{2,1,0:T(8,128)(2,1)} %bitcast.2), calls=%async_computation | async-start | bytes 1572864 | tf_op jit(solution)/shard_map/all_to_all | solution.py:583
  20.7 5.5 %collective-permute-done.2.p3 = bf16[128,1536]{1,0:T(8,128)(2,1)S(1)} collective-permute-done((bf16[128,1536]{1,0:T(8,128)(2,1)S(1)}, bf16[128,1536]{1,0:T(8,128)(2,1)S(1)}, u32[]{:S(2)}, u32[]{:S(2)}) %collective-permute-start.2) | collective-permute-done | bytes 393248 | tf_op jit(solution)/shard_map/ppermute | solution.py:562
  26.9 11.3 %forward.1 = (bf16[512,1536]{1,0:T(8,128)(2,1)}, f32[512,1536]{1,0:T(8,128)}, f32[512,128]{1,0:T(8,128)}, bf16[128,768]{1,0:T(8,128)(2,1)}, bf16[128,768]{1,0:T(...) custom-call(s32[1]{0:T(128)} %bitcast.odd_ref, ...), custom_call_target="tpu_custom_call" | custom-call | flops 3623878656 | bytes 20000000 | tf_op jit(solution)/shard_map/forward/pallas_call | solution.py:119
  38.2 2.7 %collective-permute-start.3 = (bf16[512,1536]{1,0:T(8,128)(2,1)}, bf16[512,1536]{1,0:T(8,128)(2,1)S(1)}, u32[]{:S(2)}, u32[]{:S(2)}) collective-permute-start(bf16[512,1536]{1,0:T(8,128)(2,1)} %get-tuple-element.68.own_hbm), channel_id=1, source_target_pairs={{0,1},{1,0},{2,3},{3,2},{4,5},{5,4},{6,7},{7,6},{8,9},{9,8},{10,11... | collective-permute-start | bytes 4718600 | tf_op jit(solution)/shard_map/ppermute | solution.py:558
  40.9 0.9 copy-done.5
  41.8 3.1 %pre_grads.1 = (bf16[512,768]{1,0:T(8,128)(2,1)}, bf16[512,384]{1,0:T(8,128)(2,1)}, bf16[512,384]{1,0:T(8,128)(2,1)}) custom-call(s32[1]{0:T(128)} %bitcast.8.me_ref, s32[1]{0:T(128)} %bitcast.9.core_ref, bf16[4,128,768]{2,1,0:T(8,128)(2,1)} %copy-done.5, f32[512,768]{1,0:T(8,128)} %get-tuple-element.71.slope_ref), custom_call_target="tpu_custom_call" | custom-call | flops 30000001024 | bytes 5000000 | tf_op jit(solution)/shard_map/pre_grads/pallas_call | solution.py:156
  44.9 1.9 %collective-permute-done.4.came_ref = bf16[512,384]{1,0:T(8,128)(2,1)S(1)} collective-permute-done((bf16[512,384]{1,0:T(8,128)(2,1)}, bf16[512,384]{1,0:T(8,128)(2,1)S(1)}, u32[]{:S(2)}, u32[]{:S(2)}) %collective-permute-start.4) | collective-permute-done | bytes 393248 | tf_op jit(solution)/shard_map/ppermute | solution.py:558
  48.0 8.8 %kernel_shares.1 = bf16[4,8,432,128]{3,2,1,0:T(8,128)(2,1)} custom-call(s32[1]{0:T(128)} %bitcast.odd_ref, bf16[512,1536]{1,0:T(8,128)(2,1)} %get-tuple-element.68.own_hbm, bf16[512,1536]{1,0:T(8,128)(2,1)} %copy-done.10, bf16[512,384]{1,0:T(8,128)(2,1)} %get-tuple-element.72.kept_ref, bf16[512,384]{1,0:T(8,128)(2,1)} %copy-done.11), custom_call_target="tpu_custom_call" | custom-call | flops 3623878656 | bytes 10000000 | tf_op jit(solution)/shard_map/kernel_shares/pallas_call | solution.py:294
  56.9 5.1 %all-to-all-start.1 = ((bf16[4,8,432,128]{3,2,1,0:T(8,128)(2,1)}), bf16[4,8,432,128]{3,2,1,0:T(8,128)(2,1)S(1)}, u32[]{:S(2)}, u32[]{:S(2)}) async-start(bf16[4,8,432,128]{3,2,1,0:T(8,128)(2,1)} %kernel_shares.1), calls=%async_computation.1 | async-start | bytes 7077888 | tf_op jit(solution)/shard_map/all_to_all | solution.py:597
  62.4 3.7 %collective-permute-start.6 = (bf16[128,768]{1,0:T(8,128)(2,1)}, bf16[128,768]{1,0:T(8,128)(2,1)S(1)}, u32[]{:S(2)}, u32[]{:S(2)}) collective-permute-start(bf16[128,768]{1,0:T(8,128)(2,1)} %get-tuple-element.85), channel_id=1, source_target_pairs={{0,32},{32,0},{64,96},{96,64},{1,33},{33,1},{65,97},{97,65},{2,34}... | collective-permute-start | bytes 589832 | tf_op jit(solution)/shard_map/ppermute | solution.py:562
  66.1 2.7 %collective-permute-start.7 = (bf16[128,768]{1,0:T(8,128)(2,1)}, bf16[128,768]{1,0:T(8,128)(2,1)S(1)}, u32[]{:S(2)}, u32[]{:S(2)}) collective-permute-start(bf16[128,768]{1,0:T(8,128)(2,1)} %get-tuple-element.86), channel_id=1, source_target_pairs={{0,64},{32,96},{64,0},{96,32},{1,65},{33,97},{65,1},{97,33},{2,66}... | collective-permute-start | bytes 589832 | tf_op jit(solution)/shard_map/ppermute | solution.py:562
  68.9 10.9 %backward.1 = (bf16[128,1536]{1,0:T(8,128)(2,1)}, bf16[128,1536]{1,0:T(8,128)(2,1)}, bf16[128,1536]{1,0:T(8,128)(2,1)}, bf16[128,1536]{1,0:T(8,128)(2,1)}, f32[1,1536]{1,0:T(1,128)}) custom-call(s32[1]{0:T(128)} %bitcast.odd_ref, bf16[512,768]{1,0:T(8,128)(2,1)} %get-tuple-element.80.grad_ref, bf16[128,1536]{1,0:T(8,128)(2,1)} %get-tuple-element.64.p0, ...), custom_call_target="tpu_custom_call" | custom-call | flops 1000000 | bytes 100000 | tf_op jit(solution)/shard_map/backward/pallas_call | solution.py:219
  80.7 2.2 %mid_halves.1 = (bf16[512,384]{1,0:T(8,128)(2,1)}, bf16[512,384]{1,0:T(8,128)(2,1)}) custom-call(s32[1]{0:T(128)} %bitcast.9.core_ref, bf16[128,768]{1,0:T(8,128)(2,1)} %get-tuple-element.100.m0, bf16[128,768]{1,0:T(8,128)(2,1)} %copy-done.2, bf16[128,768]{1,0:T(8,128)(2,1)} %copy-done.3, bf16[128,768]{1,0:T(8,128)(2,1)} %copy-done.4), custom_call_target="tpu_custom_call" | custom-call | flops 393216 | bytes 2000000 | tf_op jit(solution)/shard_map/mid_halves/pallas_call | solution.py:425
  83.6 3.1 %collective-permute-start.10 = (bf16[128,1536]{1,0:T(8,128)(2,1)}, bf16[128,1536]{1,0:T(8,128)(2,1)}, u32[]{:S(2)}, u32[]{:S(2)}) collective-permute-start(bf16[128,1536]{1,0:T(8,128)(2,1)} %get-tuple-element.99), channel_id=1, source_target_pairs={{0,32},{32,0},{64,96},{96,64},{1,33},{33,1},{65,97},{97,65},{2,34}... | collective-permute-start | bytes 1179656 | tf_op jit(solution)/shard_map/ppermute | solution.py:562
  86.7 2.7 %collective-permute-start.11 = (bf16[128,1536]{1,0:T(8,128)(2,1)}, bf16[128,1536]{1,0:T(8,128)(2,1)}, u32[]{:S(2)}, u32[]{:S(2)}) collective-permute-start(bf16[128,1536]{1,0:T(8,128)(2,1)} %get-tuple-element.108), channel_id=1, source_target_pairs={{0,64},{32,96},{64,0},{96,32},{1,65},{33,97},{65,1},{97,33},{2,66}... | collective-permute-start | bytes 1179656 | tf_op jit(solution)/shard_map/ppermute | solution.py:562
  89.4 1.3 convert_reduce_fusion.1
  92.2 6.1 %point_shares.1 = (bf16[8,160,128]{2,1,0:T(8,128)(2,1)}, bf16[8,160,128]{2,1,0:T(8,128)(2,1)}, bf16[8,160,128]{2,1,0:T(8,128)(2,1)}, bf16[8,160,128]{2,1,0:T(8,128)(2,1)}) custom-call(s32[1]{0:T(128)} %bitcast.10.z_ref, s32[1]{0:T(128)} %bitcast.8.me_ref, bf16[512,1536]{1,0:T(8,128)(2,1)} %bitcast.31, bf16[512,1536]{1,0:T(8,128)(2,1)} %collective-permute-done.5.other_hbm, ...), custom_call_target="tpu_custom_call" | custom-call | flops 1207959552 | bytes 6000000 | tf_op jit(solution)/shard_map/point_shares/pallas_call | solution.py:354
  98.3 1.7 %collective-permute-start.13 = (bf16[8,160,128]{2,1,0:T(8,128)(2,1)}, bf16[8,160,128]{2,1,0:T(8,128)(2,1)}, u32[]{:S(2)}, u32[]{:S(2)}) collective-permute-start(bf16[8,160,128]{2,1,0:T(8,128)(2,1)} %get-tuple-element.111), channel_id=1, source_target_pairs={{0,4},{4,8},{8,12},{12,0},{1,5},{5,9},{9,13},{13,1},{2,6},{6,10},{... | collective-permute-start | bytes 983048 | tf_op jit(solution)/shard_map/ppermute | solution.py:615
  100.0 2.4 %collective-permute-start.14 = (bf16[8,160,128]{2,1,0:T(8,128)(2,1)}, bf16[8,160,128]{2,1,0:T(8,128)(2,1)}, u32[]{:S(2)}, u32[]{:S(2)}) collective-permute-start(bf16[8,160,128]{2,1,0:T(8,128)(2,1)} %get-tuple-element.112), channel_id=1, source_target_pairs={{0,8},{4,12},{8,0},{12,4},{1,9},{5,13},{9,1},{13,5},{2,10},{6,14},... | collective-permute-start | bytes 983048 | tf_op jit(solution)/shard_map/ppermute | solution.py:615
  102.4 1.2 collective-permute-start.15
  103.6 3.6 %collective-permute-done.12.b3 = bf16[128,1536]{1,0:T(8,128)(2,1)} collective-permute-done((bf16[128,1536]{1,0:T(8,128)(2,1)}, bf16[128,1536]{1,0:T(8,128)(2,1)}, u32[]{:S(2)}, u32[]{:S(2)}) %collective-permute-start.12) | collective-permute-done | bytes 393248 | tf_op jit(solution)/shard_map/ppermute | solution.py:562
  107.2 2.8 %stream_grad.1 = bf16[512,1536]{1,0:T(8,128)(2,1)} custom-call(s32[1]{0:T(128)} %bitcast.8.me_ref, bf16[128,1536]{1,0:T(8,128)(2,1)} %get-tuple-element.106.b0, bf16[128,1536]{1,0:T(8,128)(2,1)} %collective-permute-done.10.b1, bf16[128,1536]{1,0:T(8,128)(2,1)} %collective-permute-done.11.b2, bf16[128,1536]{1,0:T(8,128)(2,1)} %collective-permute-done.12.b3, ...), custom_call_target="tpu_custom_call" | custom-call | flops 1572864 | bytes 5000000 | tf_op jit(solution)/shard_map/stream_grad/pallas_call | solution.py:540
  109.9 4.9 %stream_out.1 = bf16[512,1536]{1,0:T(8,128)(2,1)} custom-call(s32[1]{0:T(128)} %bitcast.8.me_ref, bf16[128,768]{1,0:T(8,128)(2,1)} %get-tuple-element.100.m0, bf16[128,768]{1,0:T(8,128)(2,1)} %copy-done.2, bf16[128,768]{1,0:T(8,128)(2,1)} %copy-done.3, bf16[128,768]{1,0:T(8,128)(2,1)} %copy-done.4, bf16[768,1536]{1,0:T(8,128)(2,1)} %point_ref.1, ...), custom_call_target="tpu_custom_call" | custom-call | flops 1207959552 | bytes 6000000 | tf_op jit(solution)/shard_map/stream_out/pallas_call | solution.py:496
  115.7 2.2 %collective-permute-done.14.d2 = bf16[8,160,128]{2,1,0:T(8,128)(2,1)} collective-permute-done((bf16[8,160,128]{2,1,0:T(8,128)(2,1)}, bf16[8,160,128]{2,1,0:T(8,128)(2,1)}, u32[]{:S(2)}, u32[]{:S(2)}) %collective-permute-start.14) | collective-permute-done | bytes 327712 | tf_op jit(solution)/shard_map/ppermute | solution.py:615
  117.9 1.4 plane_shares.1
  119.3 24.7 %all_to_all.15 = bf16[16,304,128]{2,1,0:T(8,128)(2,1)S(1)} all-to-all(bf16[16,304,128]{2,1,0:T(8,128)(2,1)S(1)} %bitcast.26), channel_id=1, replica_groups=mesh['xh'=2,'yh'=2,'yl'=2,'z'=4,'xl'=2,'core'=2] {'xh','yh','yl','xl'}, dimensions={0} | all-to-all | bytes 2490368 | tf_op jit(solution)/shard_map/all_to_all | solution.py:623
  144.2 9.2 %all-gather = f32[1184,128]{1,0:T(8,128)S(1)} all-gather(f32[296,128]{1,0:T(8,128)S(1)} %slice.8), channel_id=2, replica_groups=mesh['xh'=2,'yh'=2,'yl'=2,'z'=4,'xl'=2,'core'=2] {'xl','core'}, dimensions={0}, use_global_device_ids=true | all-gather | bytes 757760 | tf_op jit(solution)/shard_map/all_gather | solution.py:625
  153.4 0.8 unpack.1
  (50 shorter events, 7.6 us)
Async XLA Ops:
  0.7 8.9 %copy-start.1 = (bf16[768,1536]{1,0:T(8,128)(2,1)S(1)}, bf16[768,1536]{1,0:T(8,128)(2,1)}, u32[]{:S(2)}) copy-start(bf16[768,1536]{1,0:T(8,128)(2,1)} %point_ref.1) | copy-start | bytes 7077892
  3.0 17.6 %collective-permute-start = (bf16[128,1536]{1,0:T(8,128)(2,1)S(1)}, bf16[128,1536]{1,0:T(8,128)(2,1)S(1)}, u32[]{:S(2)}, u32[]{:S(2)}) collective-permute-start(bf16[128,1536]{1,0:T(8,128)(2,1)S(1)} %get-tuple-element.125), channel_id=1, source_target_pairs={{0,32},{32,0},{64,96},{96,64},{1,33},{33,1},{65,97},{97,65},{2,34}... | collective-permute-start | bytes 1179656 | tf_op jit(solution)/shard_map/ppermute | solution.py:562
  6.8 13.9 %collective-permute-start.1 = (bf16[128,1536]{1,0:T(8,128)(2,1)S(1)}, bf16[128,1536]{1,0:T(8,128)(2,1)S(1)}, u32[]{:S(2)}, u32[]{:S(2)}) collective-permute-start(bf16[128,1536]{1,0:T(8,128)(2,1)S(1)} %get-tuple-element.124), channel_id=1, source_target_pairs={{0,64},{32,96},{64,0},{96,32},{1,65},{33,97},{65,1},{97,33},{2,66}... | collective-permute-start | bytes 1179656 | tf_op jit(solution)/shard_map/ppermute | solution.py:562
  9.5 16.6 %collective-permute-start.2 = (bf16[128,1536]{1,0:T(8,128)(2,1)S(1)}, bf16[128,1536]{1,0:T(8,128)(2,1)S(1)}, u32[]{:S(2)}, u32[]{:S(2)}) collective-permute-start(bf16[128,1536]{1,0:T(8,128)(2,1)S(1)} %get-tuple-element.123), channel_id=1, source_target_pairs={{0,96},{32,64},{64,32},{96,0},{1,97},{33,65},{65,33},{97,1},{2,98}... | collective-permute-start | bytes 1179656 | tf_op jit(solution)/shard_map/ppermute | solution.py:562
  13.3 6.8 %copy-start.9 = (f32[1536]{0:T(1024)S(1)}, f32[1536]{0:T(1024)}, u32[]{:S(2)}) copy-start(f32[1536]{0:T(1024)} %param.6) | copy-start | bytes 18436
  13.3 27.6 %all-to-all-start = ((bf16[4,128,768]{2,1,0:T(8,128)(2,1)}), bf16[4,128,768]{2,1,0:T(8,128)(2,1)S(1)}, u32[]{:S(2)}, u32[]{:S(2)}) async-start(bf16[4,128,768]{2,1,0:T(8,128)(2,1)} %bitcast.2), calls=%async_computation | async-start | bytes 1572864 | tf_op jit(solution)/shard_map/all_to_all | solution.py:583
  20.6 5.5 %copy-start.6 = (bf16[128,1536]{1,0:T(8,128)(2,1)}, bf16[128,1536]{1,0:T(8,128)(2,1)S(1)}, u32[]{:S(2)}) copy-start(bf16[128,1536]{1,0:T(8,128)(2,1)S(1)} %collective-permute-done.p1) | copy-start | bytes 1179652
  20.6 5.5 %copy-start.7 = (bf16[128,1536]{1,0:T(8,128)(2,1)}, bf16[128,1536]{1,0:T(8,128)(2,1)S(1)}, u32[]{:S(2)}) copy-start(bf16[128,1536]{1,0:T(8,128)(2,1)S(1)} %collective-permute-done.1.p2) | copy-start | bytes 1179652
  26.1 0.8 copy-start.8
  38.2 8.6 %collective-permute-start.3 = (bf16[512,1536]{1,0:T(8,128)(2,1)}, bf16[512,1536]{1,0:T(8,128)(2,1)S(1)}, u32[]{:S(2)}, u32[]{:S(2)}) collective-permute-start(bf16[512,1536]{1,0:T(8,128)(2,1)} %get-tuple-element.68.own_hbm), channel_id=1, source_target_pairs={{0,1},{1,0},{2,3},{3,2},{4,5},{5,4},{6,7},{7,6},{8,9},{9,8},{10,11... | collective-permute-start | bytes 4718600 | tf_op jit(solution)/shard_map/ppermute | solution.py:558
  40.9 0.9 copy-start.5
  44.8 1.9 %collective-permute-start.4 = (bf16[512,384]{1,0:T(8,128)(2,1)}, bf16[512,384]{1,0:T(8,128)(2,1)S(1)}, u32[]{:S(2)}, u32[]{:S(2)}) collective-permute-start(bf16[512,384]{1,0:T(8,128)(2,1)} %get-tuple-element.73), channel_id=1, source_target_pairs={{0,1},{1,0},{2,3},{3,2},{4,5},{5,4},{6,7},{7,6},{8,9},{9,8},{10,11... | collective-permute-start | bytes 1179656 | tf_op jit(solution)/shard_map/ppermute | solution.py:558
  46.8 0.8 copy-start.11
  46.8 1.3 copy-start.10
  56.9 58.0 %all-to-all-start.1 = ((bf16[4,8,432,128]{3,2,1,0:T(8,128)(2,1)}), bf16[4,8,432,128]{3,2,1,0:T(8,128)(2,1)S(1)}, u32[]{:S(2)}, u32[]{:S(2)}) async-start(bf16[4,8,432,128]{3,2,1,0:T(8,128)(2,1)} %kernel_shares.1), calls=%async_computation.1 | async-start | bytes 7077888 | tf_op jit(solution)/shard_map/all_to_all | solution.py:597
  62.0 30.2 %collective-permute-start.5 = (bf16[512,1536]{1,0:T(8,128)(2,1)}, bf16[512,1536]{1,0:T(8,128)(2,1)}, u32[]{:S(2)}, u32[]{:S(2)}) collective-permute-start(bf16[512,1536]{1,0:T(8,128)(2,1)} %bitcast.30), channel_id=1, source_target_pairs={{0,1},{1,0},{2,3},{3,2},{4,5},{5,4},{6,7},{7,6},{8,9},{9,8},{10,11... | collective-permute-start | bytes 4718600 | tf_op jit(solution)/shard_map/ppermute | solution.py:558
  62.4 17.4 %collective-permute-start.6 = (bf16[128,768]{1,0:T(8,128)(2,1)}, bf16[128,768]{1,0:T(8,128)(2,1)S(1)}, u32[]{:S(2)}, u32[]{:S(2)}) collective-permute-start(bf16[128,768]{1,0:T(8,128)(2,1)} %get-tuple-element.85), channel_id=1, source_target_pairs={{0,32},{32,0},{64,96},{96,64},{1,33},{33,1},{65,97},{97,65},{2,34}... | collective-permute-start | bytes 589832 | tf_op jit(solution)/shard_map/ppermute | solution.py:562
  66.1 13.7 %collective-permute-start.7 = (bf16[128,768]{1,0:T(8,128)(2,1)}, bf16[128,768]{1,0:T(8,128)(2,1)S(1)}, u32[]{:S(2)}, u32[]{:S(2)}) collective-permute-start(bf16[128,768]{1,0:T(8,128)(2,1)} %get-tuple-element.86), channel_id=1, source_target_pairs={{0,64},{32,96},{64,0},{96,32},{1,65},{33,97},{65,1},{97,33},{2,66}... | collective-permute-start | bytes 589832 | tf_op jit(solution)/shard_map/ppermute | solution.py:562
  68.9 11.0 %collective-permute-start.8 = (bf16[128,768]{1,0:T(8,128)(2,1)}, bf16[128,768]{1,0:T(8,128)(2,1)S(1)}, u32[]{:S(2)}, u32[]{:S(2)}) collective-permute-start(bf16[128,768]{1,0:T(8,128)(2,1)} %get-tuple-element.87), channel_id=1, source_target_pairs={{0,96},{32,64},{64,32},{96,0},{1,97},{33,65},{65,33},{97,1},{2,98}... | collective-permute-start | bytes 589832 | tf_op jit(solution)/shard_map/ppermute | solution.py:562
  79.8 0.7 copy-start.2
  79.9 0.7 copy-start.3
  79.9 0.8 copy-start.4
  82.8 9.3 %collective-permute-start.9 = (bf16[512,384]{1,0:T(8,128)(2,1)}, bf16[512,384]{1,0:T(8,128)(2,1)}, u32[]{:S(2)}, u32[]{:S(2)}) collective-permute-start(bf16[512,384]{1,0:T(8,128)(2,1)} %get-tuple-element.93), channel_id=1, source_target_pairs={{0,1},{1,0},{2,3},{3,2},{4,5},{5,4},{6,7},{7,6},{8,9},{9,8},{10,11... | collective-permute-start | bytes 1179656 | tf_op jit(solution)/shard_map/ppermute | solution.py:558
  83.6 14.7 %collective-permute-start.10 = (bf16[128,1536]{1,0:T(8,128)(2,1)}, bf16[128,1536]{1,0:T(8,128)(2,1)}, u32[]{:S(2)}, u32[]{:S(2)}) collective-permute-start(bf16[128,1536]{1,0:T(8,128)(2,1)} %get-tuple-element.99), channel_id=1, source_target_pairs={{0,32},{32,0},{64,96},{96,64},{1,33},{33,1},{65,97},{97,65},{2,34}... | collective-permute-start | bytes 1179656 | tf_op jit(solution)/shard_map/ppermute | solution.py:562
  86.7 17.0 %collective-permute-start.11 = (bf16[128,1536]{1,0:T(8,128)(2,1)}, bf16[128,1536]{1,0:T(8,128)(2,1)}, u32[]{:S(2)}, u32[]{:S(2)}) collective-permute-start(bf16[128,1536]{1,0:T(8,128)(2,1)} %get-tuple-element.108), channel_id=1, source_target_pairs={{0,64},{32,96},{64,0},{96,32},{1,65},{33,97},{65,1},{97,33},{2,66}... | collective-permute-start | bytes 1179656 | tf_op jit(solution)/shard_map/ppermute | solution.py:562
  89.4 17.8 %collective-permute-start.12 = (bf16[128,1536]{1,0:T(8,128)(2,1)}, bf16[128,1536]{1,0:T(8,128)(2,1)}, u32[]{:S(2)}, u32[]{:S(2)}) collective-permute-start(bf16[128,1536]{1,0:T(8,128)(2,1)} %get-tuple-element.109), channel_id=1, source_target_pairs={{0,96},{32,64},{64,32},{96,0},{1,97},{33,65},{65,33},{97,1},{2,98}... | collective-permute-start | bytes 1179656 | tf_op jit(solution)/shard_map/ppermute | solution.py:562
  98.3 17.4 %collective-permute-start.13 = (bf16[8,160,128]{2,1,0:T(8,128)(2,1)}, bf16[8,160,128]{2,1,0:T(8,128)(2,1)}, u32[]{:S(2)}, u32[]{:S(2)}) collective-permute-start(bf16[8,160,128]{2,1,0:T(8,128)(2,1)} %get-tuple-element.111), channel_id=1, source_target_pairs={{0,4},{4,8},{8,12},{12,0},{1,5},{5,9},{9,13},{13,1},{2,6},{6,10},{... | collective-permute-start | bytes 983048 | tf_op jit(solution)/shard_map/ppermute | solution.py:615
  100.0 17.8 %collective-permute-start.14 = (bf16[8,160,128]{2,1,0:T(8,128)(2,1)}, bf16[8,160,128]{2,1,0:T(8,128)(2,1)}, u32[]{:S(2)}, u32[]{:S(2)}) collective-permute-start(bf16[8,160,128]{2,1,0:T(8,128)(2,1)} %get-tuple-element.112), channel_id=1, source_target_pairs={{0,8},{4,12},{8,0},{12,4},{1,9},{5,13},{9,1},{13,5},{2,10},{6,14},... | collective-permute-start | bytes 983048 | tf_op jit(solution)/shard_map/ppermute | solution.py:615
  102.4 15.4 %collective-permute-start.15 = (bf16[8,160,128]{2,1,0:T(8,128)(2,1)}, bf16[8,160,128]{2,1,0:T(8,128)(2,1)}, u32[]{:S(2)}, u32[]{:S(2)}) collective-permute-start(bf16[8,160,128]{2,1,0:T(8,128)(2,1)} %get-tuple-element.113), channel_id=1, source_target_pairs={{0,12},{4,0},{8,4},{12,8},{1,13},{5,1},{9,5},{13,9},{2,14},{6,2},{... | collective-permute-start | bytes 983048 | tf_op jit(solution)/shard_map/ppermute | solution.py:615
  114.9 3.0 %copy-start = (bf16[8,160,128]{2,1,0:T(8,128)(2,1)S(1)}, bf16[8,160,128]{2,1,0:T(8,128)(2,1)}, u32[]{:S(2)}) copy-start(bf16[8,160,128]{2,1,0:T(8,128)(2,1)} %get-tuple-element.116.d0) | copy-start | bytes 983044
